TPU v7x, 512 devices: a whole 4x4x16 slice. The times are simulated.
512 devices in a mesh: ctx: 64 (over z, y_lo, core), tp: 8 (over x, y_hi).
Axes of the slice: x: 4, y: 4 (y_hi: 2, y_lo: 2; y = y_hi * 2 + y_lo), z: 16, core: 2. Of those that a mesh axis runs over, the one named last changes fastest.
Arguments:
- byte_ids: int32 [32768], P('ctx'), may hold values from 0 to 255
- patch_lens: int32 [8192], P('ctx'), may hold values from 1 to 11, as said below
- byte_table: bfloat16 [256, 1024], replicated, may hold values from -6 to 6
- wq_cross: bfloat16 [1024, 2048], P(None, 'tp'), may hold values from -128 to 128
- wk_cross: bfloat16 [1024, 2048], P(None, 'tp'), may hold values from -1 to 1
- wv_cross: bfloat16 [1024, 2048], P(None, 'tp'), may hold values from -0.1875 to 0.1875
- norm_gain: float32 [2048], replicated, may hold values from 0.1 to 1.9
- wq_latent: bfloat16 [2048, 2048], P('ctx', 'tp'), may hold values from -8 to 8
- wk_latent: bfloat16 [2048, 2048], P('ctx', 'tp'), may hold values from -1 to 1
- wv_latent: bfloat16 [2048, 2048], P('ctx', 'tp'), may hold values from -0.125 to 0.125
Outputs:
- patch_latent: bfloat16 [8192, 2048], P('ctx', 'tp')
- latent_mixed: bfloat16 [8192, 2048], P('ctx', 'tp')
Inputs may be any that keep to these rules, and one draw needn't show every extreme that they name: `patch_lens`: all patches together hold 32768 bytes; the patches of ctx index d begin at byte d * 512 + e_d with 0 <= e_d <= 256, e_0 = 0, and e_d = 256 for some d.
All inputs are finite; a program needn't handle non-finite values.
Results may differ from a plain program's by a relative error of at most 0.012.
The roundings to bfloat16 on the way count: a program that leaves them out, or rounds other values in their place, can miss the bound.
Values may be sent and summed in bfloat16 or wider, within the bound.
No kernel may reach another device: no remote copies, remote signals or barrier semaphores. Data moves between devices by JAX's collectives and lax.ppermute only.
A program may use at most 64 MiB of HBM per device.

v0:
```python
import math

import jax
import jax.numpy as jnp
from jax import lax
from jax.sharding import PartitionSpec as P

HD = 128


def carried_in(value, axis, join, neutral):
    count, mine = (lax.axis_size(axis), lax.axis_index(axis))
    pieces = lax.all_gather(value, axis)
    so_far = jnp.full_like(value, 0) + jnp.asarray(neutral, value.dtype)

    def step(position, so_far):
        longer = join(so_far, pieces[position])
        return jnp.where(position < mine, longer, so_far)

    return lax.fori_loop(0, count - 1, step, so_far)


def from_behind(value, axis, steps):
    count = lax.axis_size(axis)
    initial, last = (max(0, -steps), min(count, count - steps))
    return lax.ppermute(value, axis, [(source, source + steps) for source in range(initial, last)])


def add_ints(earlier, later):
    return earlier + later


def project_bytes(ids_here, byte_table, wq_cross, wk_cross, wv_cross):
    vocab_size = byte_table.shape[0]
    onehot = (ids_here[:, None] == jnp.arange(vocab_size, dtype=jnp.int32)[None, :]).astype(
        jnp.bfloat16
    )
    hidden = jnp.dot(onehot, byte_table, preferred_element_type=jnp.float32).astype(jnp.bfloat16)
    return tuple(
        (
            jnp.dot(hidden, weight, preferred_element_type=jnp.float32).astype(jnp.bfloat16)
            for weight in (wq_cross, wk_cross, wv_cross)
        )
    )


def on_device(
    byte_ids,
    patch_lens,
    byte_table,
    wq_cross,
    wk_cross,
    wv_cross,
    norm_gain,
    wq_latent,
    wk_latent,
    wv_latent,
):
    bytes_here = byte_ids.shape[0]
    patches_here = patch_lens.shape[0]
    half_window = bytes_here // 2
    local_cols = wq_cross.shape[1]
    local_heads = local_cols // HD
    scale = 1.0 / math.sqrt(HD)
    device_pos = lax.axis_index("ctx")
    lens_total = jnp.sum(patch_lens)
    lens_before = carried_in(lens_total, "ctx", add_ints, jnp.int32(0))
    patch_start = lens_before + jnp.cumsum(patch_lens) - patch_lens - device_pos * bytes_here
    local_proj = project_bytes(byte_ids, byte_table, wq_cross, wk_cross, wv_cross)
    next_proj = from_behind(
        (local_proj[0][:half_window], local_proj[1][:half_window], local_proj[2][:half_window]),
        "ctx",
        -1,
    )
    window_q = jnp.concatenate([local_proj[0], next_proj[0]], axis=0)
    window_k = jnp.concatenate([local_proj[1], next_proj[1]], axis=0)
    window_v = jnp.concatenate([local_proj[2], next_proj[2]], axis=0)
    window_len = window_q.shape[0]
    slots = jnp.arange(window_len, dtype=jnp.int32)
    member = (slots[None, :] >= patch_start[:, None]) & (
        slots[None, :] < patch_start[:, None] + patch_lens[:, None]
    )
    pooled = jnp.dot(member.astype(jnp.bfloat16), window_q, preferred_element_type=jnp.float32)
    patch_q = (pooled / patch_lens.astype(jnp.float32)[:, None]).astype(jnp.bfloat16)
    cross_scores = (
        jnp.einsum(
            "phd,whd->hpw",
            patch_q.reshape(patches_here, local_heads, HD),
            window_k.reshape(window_len, local_heads, HD),
            preferred_element_type=jnp.float32,
        )
        * scale
    )
    cross_scores = jnp.where(member[None], cross_scores, jnp.float32(-1e30))
    cross_top = jnp.max(cross_scores, axis=-1, keepdims=True)
    cross_expo = jnp.exp(cross_scores - cross_top) * member[None].astype(jnp.float32)
    cross_weights = (cross_expo / jnp.sum(cross_expo, axis=-1, keepdims=True)).astype(jnp.bfloat16)
    cross_out = jnp.einsum(
        "hpw,whd->phd",
        cross_weights,
        window_v.reshape(window_len, local_heads, HD),
        preferred_element_type=jnp.float32,
    )
    patch_latent = cross_out.reshape(patches_here, local_cols).astype(jnp.bfloat16)
    all_heads = lax.all_gather(patch_latent, "tp", axis=1, tiled=True)
    latent32 = all_heads.astype(jnp.float32)
    inverse = lax.rsqrt(jnp.mean(latent32 * latent32, axis=-1, keepdims=True) + 1e-05)
    normed = (latent32 * inverse * norm_gain[None, :]).astype(jnp.bfloat16)

    def add_rows(piece):
        return jnp.dot(normed, piece, preferred_element_type=jnp.float32)

    query_sum = add_rows(lax.all_gather(wq_latent, "ctx", axis=0, tiled=True))
    key_sum = add_rows(lax.all_gather(wk_latent, "ctx", axis=0, tiled=True))
    value_sum = add_rows(lax.all_gather(wv_latent, "ctx", axis=0, tiled=True))
    lat_q = query_sum.astype(jnp.bfloat16).reshape(patches_here, local_heads, HD)
    lat_k = key_sum.astype(jnp.bfloat16)
    lat_v = value_sum.astype(jnp.bfloat16)
    query_index = device_pos * patches_here + jnp.arange(patches_here, dtype=jnp.int32)
    running_max = jnp.full((local_heads, patches_here), -1e30, jnp.float32)
    key_piece = lax.all_gather(lat_k, "ctx", axis=0, tiled=True)
    value_piece = lax.all_gather(lat_v, "ctx", axis=0, tiled=True)
    count = key_piece.shape[0]
    key_index = jnp.arange(count, dtype=jnp.int32)
    allowed = key_index[None, :] <= query_index[:, None]
    scores = (
        jnp.einsum(
            "phd,nhd->hpn",
            lat_q,
            key_piece.reshape(count, local_heads, HD),
            preferred_element_type=jnp.float32,
        )
        * scale
    )
    scores = jnp.where(allowed[None], scores, jnp.float32(-1e30))
    new_max = jnp.maximum(running_max, jnp.max(scores, axis=-1))
    expo = jnp.exp(scores - new_max[..., None]) * allowed[None].astype(jnp.float32)
    new_sum = jnp.sum(expo, axis=-1)
    weights = expo.astype(jnp.bfloat16)
    new_acc = jnp.einsum(
        "hpn,nhd->hpd",
        weights,
        value_piece.reshape(count, local_heads, HD),
        preferred_element_type=jnp.float32,
    )
    mixed = new_acc / new_sum[..., None]
    latent_mixed = (
        jnp.transpose(mixed, (1, 0, 2)).reshape(patches_here, local_cols).astype(jnp.bfloat16)
    )
    return (patch_latent, latent_mixed)


def solution(mesh):
    return jax.shard_map(
        on_device,
        mesh=mesh,
        in_specs=(
            P("ctx"),
            P("ctx"),
            P(),
            P(None, "tp"),
            P(None, "tp"),
            P(None, "tp"),
            P(),
            P("ctx", "tp"),
            P("ctx", "tp"),
            P("ctx", "tp"),
        ),
        out_specs=(P("ctx", "tp"), P("ctx", "tp")),
        check_vma=False,
    )
```

profile of v0, /device:TPU:1, one launch (start us, length us, event | category | flops | bytes accessed | tf_op | source)
XLA Modules:
  0.0 642.2 jit_solution(10197914719936423205)
XLA Ops:
  9.9 1.5 convolution_convert_fusion.2
  11.4 8.8 %collective-permute-start.1 = (bf16[256,256]{1,0:T(8,128)(2,1)S(1)}, bf16[256,256]{1,0:T(8,128)(2,1)S(1)}, u32[]{:S(2)}, u32[]{:S(2)}) collective-permute-start(bf16[256,256]{1,0:T(8,128)(2,1)S(1)} %slice.13), channel_id=1, source_target_pairs={{8,0},{16,8},{24,16},{32,24},{40,32},{48,40},{56,48},{64,56},{72,6... | collective-permute-start | bytes 393224 | tf_op jit(solution)/shard_map/ppermute | solution.py:26
  20.2 1.5 convolution_convert_fusion.1
  21.7 1.9 collective-permute-start.2
  24.1 1.9 collective-permute-start
  26.8 1.3 dynamic-slice
  28.1 1.4 dynamic-update-slice
  29.5 21.9 %all-reduce = s32[64]{0:T(128)S(1)} all-reduce(s32[64]{0:T(128)S(1)} %dynamic-update-slice), channel_id=1, replica_groups=mesh['ctx'=64,'tp'=8] {'ctx'}, use_global_device_ids=true, to_apply=%add | all-reduce | flops 64 | bytes 512
  51.4 80.1 %while.13 = (s32[]{:T(128)}, s32[]{:T(128)}, s32[]{:T(128)}, s32[64]{0:T(128)S(1)}, s32[]{:T(128)}) while((s32[]{:T(128)}, s32[]{:T(128)}, s32[]{:T(128)}, s32[64]{0:T(128)S(1)}, s32[]{:T(128)}) %tuple.39), condition=%wide.region_2.3_spmd, body=%wide.region_1.2_spmd.sunk | while | flops 5 | bytes 107 | solution.py:20
  134.3 2.0 convolution_convert_fusion.7
  136.3 29.5 %all_gather.26 = bf16[128,2048]{0,1:T(8,128)(2,1)S(1)} all-gather(bf16[128,256]{0,1:T(8,128)(2,1)S(1)} %bitcast.74), channel_id=1, replica_groups=mesh['ctx'=64,'tp'=8] {'tp'}, dimensions={1}, use_global_device_ids=true | all-gather | bytes 589824 | tf_op jit(solution)/shard_map/all_gather | solution.py:105
  166.1 2.5 convolution_convert_fusion.5
  168.7 87.0 %all-gather.12.cloned.1.call-done = bf16[2048,256]{1,0:T(8,128)(2,1)} async-done(((bf16[32,256]{1,0:T(8,128)(2,1)}), bf16[2048,256]{1,0:T(8,128)(2,1)}) %all-gather.12.cloned.1.call-update) | async-done | bytes 1048592 | tf_op jit(solution)/shard_map/all_gather | solution.py:115
  255.7 2.5 convolution_convert_fusion.4
  258.2 2.8 fusion.36
  261.8 113.1 %all-gather.6.cloned.1.call-done = bf16[2048,256]{1,0:T(8,128)(2,1)} async-done(((bf16[32,256]{1,0:T(8,128)(2,1)}), bf16[2048,256]{1,0:T(8,128)(2,1)}) %all-gather.6.cloned.1.call-update) | async-done | bytes 1048592 | tf_op jit(solution)/shard_map/all_gather | solution.py:113
  374.8 1.9 fusion.18
  376.7 121.0 %all-gather.10.cloned.1.call-done = bf16[8192,256]{1,0:T(8,128)(2,1)} async-done(((bf16[128,256]{1,0:T(8,128)(2,1)}), bf16[8192,256]{1,0:T(8,128)(2,1)}) %all-gather.10.cloned.1.call-update) | async-done | bytes 4194320 | tf_op jit(solution)/shard_map/all_gather | solution.py:121
  497.8 4.1 fusion.61
  501.9 3.2 copy-done.2
  505.1 1.7 fusion.2
  506.8 114.1 %all-gather.14.cloned.1.call-done = bf16[8192,256]{1,0:T(8,128)(2,1)} async-done(((bf16[128,256]{1,0:T(8,128)(2,1)}), bf16[8192,256]{1,0:T(8,128)(2,1)}) %all-gather.14.cloned.1.call-update) | async-done | bytes 4194320 | tf_op jit(solution)/shard_map/all_gather | solution.py:122
  620.9 6.4 copy.31
  627.3 7.7 %fusion.23 = bf16[128,2,128]{0,2,1:T(8,128)(2,1)S(1)} fusion(bf16[8192,2,128]{0,2,1:T(8,128)(2,1)} %bitcast.71, f32[2,128,8192]{2,1,0:T(8,128)} %copy-done.2, f32[128,8192]{1,0:T(8,128)} %get-tuple-element.98, f32[2,128]{1,0:T(2,128)S(1)} %broadcast_maximum_fusion, f32[128,2]{0,1:T(2,128)S(1)} %bitcast.76), kind=kOutput, calls=%fused_computation.33 | convolution fusion | flops 543227904 | bytes 16844800 | tf_op jit(solution)/shard_map/hpn,nhd->hpd/dot_general | solution.py:140
  (111 shorter events, 47.1 us)
Async XLA Ops:
  7.2 1.6 copy-start
  7.2 16.5 %copy-start.5 = (bf16[1024,256]{1,0:T(8,128)(2,1)S(1)}, bf16[1024,256]{1,0:T(8,128)(2,1)}, u32[]{:S(2)}) copy-start(bf16[1024,256]{1,0:T(8,128)(2,1)} %param.17) | copy-start | bytes 1572868
  7.2 18.9 %copy-start.4 = (s32[128]{0:T(128)S(1)}, s32[128]{0:T(128)}, u32[]{:S(2)}) copy-start(s32[128]{0:T(128)} %param.13) | copy-start | bytes 1540
  7.2 158.9 %all-gather.8.cloned.1.call-start = ((), (), s32[]{:S(2)}) async-start(), calls=%async_computation.1 | async-start | bytes 1064960 | tf_op jit(solution)/shard_map/all_gather | solution.py:114
  7.9 247.8 %all-gather.12.cloned.1.call-start = ((), (), s32[]{:S(2)}) async-start(), calls=%async_computation.3 | async-start | bytes 1064960 | tf_op jit(solution)/shard_map/all_gather | solution.py:115
  8.7 366.2 %all-gather.6.cloned.1.call-start = ((), (), s32[]{:S(2)}) async-start(), calls=%async_computation | async-start | bytes 1064960 | tf_op jit(solution)/shard_map/all_gather | solution.py:113
  11.4 120.9 %collective-permute-start.1 = (bf16[256,256]{1,0:T(8,128)(2,1)S(1)}, bf16[256,256]{1,0:T(8,128)(2,1)S(1)}, u32[]{:S(2)}, u32[]{:S(2)}) collective-permute-start(bf16[256,256]{1,0:T(8,128)(2,1)S(1)} %slice.13), channel_id=1, source_target_pairs={{8,0},{16,8},{24,16},{32,24},{40,32},{48,40},{56,48},{64,56},{72,6... | collective-permute-start | bytes 393224 | tf_op jit(solution)/shard_map/ppermute | solution.py:26
  21.7 110.9 %collective-permute-start.2 = (bf16[256,256]{1,0:T(8,128)(2,1)S(1)}, bf16[256,256]{1,0:T(8,128)(2,1)S(1)}, u32[]{:S(2)}, u32[]{:S(2)}) collective-permute-start(bf16[256,256]{1,0:T(8,128)(2,1)S(1)} %slice.14), channel_id=1, source_target_pairs={{8,0},{16,8},{24,16},{32,24},{40,32},{48,40},{56,48},{64,56},{72,6... | collective-permute-start | bytes 393224 | tf_op jit(solution)/shard_map/ppermute | solution.py:26
  24.1 107.9 %collective-permute-start = (bf16[256,256]{1,0:T(8,128)(2,1)S(1)}, bf16[256,256]{1,0:T(8,128)(2,1)S(1)}, u32[]{:S(2)}, u32[]{:S(2)}) collective-permute-start(bf16[256,256]{1,0:T(8,128)(2,1)S(1)} %slice.12), channel_id=1, source_target_pairs={{8,0},{16,8},{24,16},{32,24},{40,32},{48,40},{56,48},{64,56},{72,6... | collective-permute-start | bytes 393224 | tf_op jit(solution)/shard_map/ppermute | solution.py:26
  26.1 471.7 %all-gather.10.cloned.1.call-start = ((), (), s32[]{:S(2)}) async-start(), calls=%async_computation.2 | async-start | bytes 4259840 | tf_op jit(solution)/shard_map/all_gather | solution.py:121
  132.6 33.6 %copy-start.3 = (f32[2048]{0:T(1024)S(1)}, f32[2048]{0:T(1024)}, u32[]{:S(2)}) copy-start(f32[2048]{0:T(1024)} %param.18) | copy-start | bytes 24580
  168.6 452.3 %all-gather.14.cloned.1.call-start = ((), (), s32[]{:S(2)}) async-start(), calls=%async_computation.4 | async-start | bytes 4259840 | tf_op jit(solution)/shard_map/all_gather | solution.py:122
  497.8 7.4 %copy-start.1 = (f32[128,8192]{1,0:T(8,128)S(1)}, f32[128,8192]{1,0:T(8,128)}, u32[]{:S(2)}) copy-start(f32[128,8192]{1,0:T(8,128)} %get-tuple-element.98) | copy-start | bytes 12582916
  501.9 3.2 copy-start.2
Sparse Core Ops, SparseCore 0:
  10.2 126.4 all-gather.7
  138.8 116.8 all-gather.11
  257.8 116.9 all-gather.5
  376.9 120.8 all-gather.9
  500.3 120.5 all-gather.13
where the time goes:
time: 644 us; the launch traced here: 642 us
  waiting for transfers between devices  437 us (68%)
  local copies, waits for them, and re-layouts  52.7 us (8%)
  blocking collectives  51.4 us (8%)
  loops' own time  41.5 us (6%)
  matrix products  27.2 us (4%)
  between operations  14.1 us (2%)
  starting transfers between devices  12.8 us (2%)
    all_gather x1, waiting for transfers between devices, on_device(): key_piece = lax.all_gather(lat_k, 'ctx', axis=0, tiled=True)  121 us
    all_gather x1, waiting for transfers between devices, on_device(): value_piece = lax.all_gather(lat_v, 'ctx', axis=0, tiled=True)  114 us
    all_gather x1, waiting for transfers between devices, on_device(): query_sum = add_rows(lax.all_gather(wq_latent, 'ctx', axis=0, tiled=True))  113 us
    all_gather x1, waiting for transfers between devices, on_device(): value_sum = add_rows(lax.all_gather(wv_latent, 'ctx', axis=0, tiled=True))  87 us
    another operation x1, loops' own time, carried_in(): return lax.fori_loop(0, count - 1, step, so_far)  41.5 us
    dynamic_slice x63, local copies, waits for them, and re-layouts, step(): longer = join(so_far, pieces[position])  38.6 us
    all_gather x1, blocking collectives, on_device(): all_heads = lax.all_gather(patch_latent, 'tp', axis=1, tiled=True)  29.5 us
    unnamed x1, blocking collectives  21.9 us
  transfers between devices with their start and end apart: 8, of which 4 were waited for; matrix products, arithmetic and copies ran while one was open for 11% of the time, Pallas kernels for 0%

commit v1 on v0

v1 whole, which is shorter than its diff:
```python
import math

import jax
import jax.numpy as jnp
from jax import lax
from jax.experimental import pallas as pl
from jax.experimental.pallas import tpu as pltpu
from jax.sharding import Mesh
from jax.sharding import PartitionSpec as P

HD = 128
SCALE = 1.0 / math.sqrt(HD)
NEG = -1e30
N_CTX = 64
N_TP = 8
BYTES_DEV = 512
P_DEV = 128
W_ROWS = 32
ROWS = 3 * W_ROWS
MSG = ROWS + 16
VMEM = 56 * 1024 * 1024

CTX = ("z", "yl", "c")
TP = ("x", "yh")
PLANE = ("yl", "x", "yh")
TURN = ("z", "x", "yh")


def turns():
    same, other = [], []
    for z in range(16):
        for t in range(N_TP):
            same.append((z * N_TP + t, (2 * t + z % 2) * N_TP + z // 2))
            other.append((z * N_TP + t, (2 * t + 1 - z % 2) * N_TP + z // 2))
    return same, other


def back(pairs):
    return [(target, source) for source, target in pairs]


def to_all(value, axes, count):
    return lax.all_to_all(jnp.broadcast_to(value[None], (count, *value.shape)), axes, 0, 0)


def nt_dot(a, b):
    return lax.dot_general(a, b, (((1,), (1,)), ((), ())), preferred_element_type=jnp.float32)


def lens_before(d, c, own_ref, other_ref):
    total = jnp.zeros((), jnp.float32)
    for ref, core in ((own_ref, c), (other_ref, 1 - c)):
        tiles = ref[:, :, ROWS:MSG, :].astype(jnp.float32)
        unit, b, row = (lax.broadcasted_iota(jnp.int32, tiles.shape, i) for i in range(3))
        place = 8 * (unit % 8) + 4 * b + 2 * (unit // 8) + core
        total = total + jnp.sum(jnp.where((row == 4) & (place < d), tiles, 0.0))
    return total


def byte_counts(d, c, own_ref, other_ref):
    follow = jnp.where(d < N_CTX - 1, d + 1, d - 1)

    def tile(ref, place):
        unit = ((place // 2) % 2) * 8 + place // 8
        return ref[unit, (place // 4) % 2, ROWS:MSG, :].astype(jnp.float32)

    here, beyond = tile(own_ref, d), tile(other_ref, follow)
    begin = lens_before(d, c, own_ref, other_ref) - (d * BYTES_DEV).astype(jnp.float32)
    lens_row = here[4:5, :]
    row = lax.broadcasted_iota(jnp.int32, (P_DEV, P_DEV), 0)
    col = lax.broadcasted_iota(jnp.int32, (P_DEV, P_DEV), 1)
    lens = jnp.sum(jnp.where(col == row, lens_row, 0.0), axis=1, keepdims=True)
    start = begin + jnp.sum(jnp.where(col < row, lens_row, 0.0), axis=1, keepdims=True)
    end = start + lens
    value = (lax.broadcasted_iota(jnp.int32, (256, P_DEV), 0) + 128 * c) % 256
    value = value.astype(jnp.float32)
    slot = col.astype(jnp.float32)
    counts = jnp.zeros((P_DEV, 256), jnp.float32)
    for chunk in range(6):
        ids = here[chunk : chunk + 1, :] if chunk < 4 else beyond[chunk - 4 : chunk - 3, :]
        at = slot + 128.0 * chunk
        member = ((at >= start) & (at < end)).astype(jnp.bfloat16)
        onehot = (value == ids).astype(jnp.bfloat16)
        counts = counts + nt_dot(member, onehot)
    return counts, lens


def two_heads(counts, lens, table):
    pooled = jnp.dot(counts.astype(jnp.bfloat16), table[:, :256], preferred_element_type=jnp.float32)
    query = (pooled / lens).astype(jnp.bfloat16)
    outs = []
    for a in range(2):
        lanes = slice(a * HD, (a + 1) * HD)
        scores = nt_dot(query[:, lanes], table[:, 256 + a * HD : 256 + (a + 1) * HD]) * SCALE
        scores = jnp.where(counts > 0.0, scores, NEG)
        expo = jnp.exp(scores - jnp.max(scores, axis=-1, keepdims=True))
        norm = jnp.sum(expo * counts, axis=-1, keepdims=True)
        weights = (expo * (1.0 / norm)).astype(jnp.bfloat16).astype(jnp.float32) * counts
        high = weights.astype(jnp.bfloat16)
        low = (weights - high.astype(jnp.float32)).astype(jnp.bfloat16)
        vals = table[:, 512 + a * HD : 512 + (a + 1) * HD]
        out = jnp.dot(high, vals, preferred_element_type=jnp.float32)
        out = out + jnp.dot(low, vals, preferred_element_type=jnp.float32)
        outs.append(out.astype(jnp.bfloat16))
    return jnp.concatenate(outs, axis=1)


def encode_kernel(
    place_ref, tab_own, tab_other, msg_own, msg_other, gain_ref, q_ref, kv_ref, latent, weight
):
    c, yl, t = place_ref[0], place_ref[1], place_ref[2]
    parts = [byte_counts(8 * t + 4 * b + 2 * yl + c, c, msg_own, msg_other) for b in range(2)]
    counts = jnp.concatenate([part[0] for part in parts], axis=0)
    lens = jnp.concatenate([part[1] for part in parts], axis=0)

    def heads(tt, squares):
        table = jnp.concatenate([tab_own[tt], tab_other[tt]], axis=0)
        out = two_heads(counts, lens, table)
        latent[tt] = out
        wide = out.astype(jnp.float32)
        for ref, core in ((msg_own, c), (msg_other, 1 - c)):
            for b in range(2):
                for side in range(2):
                    first = pl.multiple_of(W_ROWS * (4 * b + 2 * side + core), W_ROWS)
                    for n in range(3):
                        weight[tt, pl.ds(first, W_ROWS), n * HD : (n + 1) * HD] = ref[
                            8 * side + tt, b, n * W_ROWS : (n + 1) * W_ROWS, :
                        ]
        return squares + jnp.sum(wide * wide, axis=-1, keepdims=True)

    squares = lax.fori_loop(0, N_TP, heads, jnp.zeros((2 * P_DEV, 1), jnp.float32))
    inverse = lax.rsqrt(squares / 2048.0 + 1e-05)
    total = jnp.zeros((2 * P_DEV, 3 * HD), jnp.float32)
    for tt in range(N_TP):
        normed = latent[tt].astype(jnp.float32) * inverse * gain_ref[tt : tt + 1, :]
        total = total + jnp.dot(
            normed.astype(jnp.bfloat16), weight[tt], preferred_element_type=jnp.float32
        )
    total = total.astype(jnp.bfloat16)
    q_ref[...] = total[:, :HD]
    kv_ref[...] = total[:, HD:]


def latent_kernel(place_ref, tab_own, tab_other, msg_own, msg_other, out_ref):
    c, t, d = place_ref[0], place_ref[2], place_ref[3]
    counts, lens = byte_counts(d, c, msg_own, msg_other)
    table = jnp.concatenate([tab_own[t], tab_other[t]], axis=0)
    out_ref[...] = two_heads(counts, lens, table)


def attend_kernel(place_ref, q_ref, kv_own, kv_other, out_ref, scores):
    c, yl, t = place_ref[0], place_ref[1], place_ref[2]
    query = q_ref[...]
    size = 2 * P_DEV
    row = lax.broadcasted_iota(jnp.int32, (size, size), 0)
    col = lax.broadcasted_iota(jnp.int32, (size, size), 1)
    row_at = 1024 * t + 512 * (row // P_DEV) + 256 * yl + P_DEV * c + row % P_DEV
    col_at = 512 * (col // P_DEV) + col % P_DEV

    def first(tt, top):
        for i, (ref, core) in enumerate(((kv_own, c), (kv_other, 1 - c))):
            for side in range(2):
                s = nt_dot(query, ref[8 * side + tt, :, :HD]) * SCALE
                s = jnp.where(col_at + (1024 * tt + 256 * side + P_DEV * core) <= row_at, s, NEG)
                scores[tt, 2 * i + side] = s
                top = jnp.maximum(top, jnp.maximum(s[:, :HD], s[:, HD:]))
        return top

    top = lax.fori_loop(0, t + 1, first, jnp.full((size, HD), NEG, jnp.float32))
    top = jnp.max(top, axis=-1, keepdims=True)

    def second(tt, carry):
        norm, acc = carry
        for i, ref in enumerate((kv_own, kv_other)):
            for side in range(2):
                e = jnp.exp(scores[tt, 2 * i + side] - top)
                norm = norm + (e[:, :HD] + e[:, HD:])
                acc = acc + jnp.dot(
                    e.astype(jnp.bfloat16),
                    ref[8 * side + tt, :, HD:],
                    preferred_element_type=jnp.float32,
                )
        return norm, acc

    zero = jnp.zeros((size, HD), jnp.float32)
    norm, acc = lax.fori_loop(0, t + 1, second, (zero, zero))
    out = acc / jnp.sum(norm, axis=-1, keepdims=True)
    out_ref[...] = out.astype(jnp.bfloat16)


def call(body, outs, scratch, flops, *args):
    vmem = pl.BlockSpec(memory_space=pltpu.VMEM)
    smem = pl.BlockSpec(memory_space=pltpu.SMEM)
    return pl.pallas_call(
        body,
        out_shape=[jax.ShapeDtypeStruct(shape, jnp.bfloat16) for shape in outs],
        in_specs=[smem] + [vmem] * (len(args) - 1),
        out_specs=[vmem] * len(outs),
        scratch_shapes=scratch,
        compiler_params=pltpu.CompilerParams(vmem_limit_bytes=VMEM),
        cost_estimate=pl.CostEstimate(flops=flops, bytes_accessed=4 << 20, transcendentals=1 << 20),
    )(*args)


def on_device(
    byte_ids,
    patch_lens,
    byte_table,
    wq_cross,
    wk_cross,
    wv_cross,
    norm_gain,
    wq_latent,
    wk_latent,
    wv_latent,
):
    z, yl, c = (lax.axis_index(name) for name in CTX)
    t = lax.axis_index("x") * 2 + lax.axis_index("yh")
    place = jnp.stack([c, yl, t, 4 * z + 2 * yl + c]).astype(jnp.int32)
    swap = [(0, 1), (1, 0)]
    same, other = turns()

    ints = jnp.concatenate([byte_ids, patch_lens]).astype(jnp.bfloat16).reshape(5, HD)
    ints = jnp.pad(ints, ((0, 11), (0, 0)))
    latent = (wq_latent, wk_latent, wv_latent)
    messages = [
        jnp.concatenate([w[:, a * HD : (a + 1) * HD] for w in latent] + [ints], axis=0) for a in range(2)
    ]
    odd = z % 2 == 1
    got_same = lax.ppermute(jnp.where(odd, messages[1], messages[0]), TURN, same)
    got_other = lax.ppermute(jnp.where(odd, messages[0], messages[1]), TURN, other)
    message = jnp.stack(
        [jnp.where(odd, got_other, got_same), jnp.where(odd, got_same, got_other)]
    )

    rows = lax.dynamic_slice_in_dim(byte_table, 128 * c, 128, axis=0)
    tables = jnp.concatenate(
        [
            jnp.dot(rows, w, preferred_element_type=jnp.float32).astype(jnp.bfloat16)
            for w in (wq_cross, wk_cross, wv_cross)
        ],
        axis=1,
    )
    tab_own = to_all(tables, TP, N_TP)
    tab_other = lax.ppermute(tab_own, "c", swap)
    msg_own = to_all(message, PLANE, 16)
    msg_other = lax.ppermute(msg_own, "c", swap)

    q, kv = call(
        encode_kernel,
        [(2 * P_DEV, HD), (2 * P_DEV, 2 * HD)],
        [pltpu.VMEM((N_TP, 256, 256), jnp.bfloat16), pltpu.VMEM((N_TP, 256, 3 * HD), jnp.bfloat16)],
        1 << 30,
        place,
        tab_own,
        tab_other,
        msg_own,
        msg_other,
        norm_gain.reshape(N_TP, 256),
    )
    kv_own = to_all(kv, PLANE, 16)
    kv_other = lax.ppermute(kv_own, "c", swap)
    (mixed,) = call(
        attend_kernel,
        [(2 * P_DEV, HD)],
        [pltpu.VMEM((N_TP, 4, 2 * P_DEV, 2 * P_DEV), jnp.float32)],
        1 << 30,
        place,
        q,
        kv_own,
        kv_other,
    )
    sent_same = jnp.where(odd, mixed[P_DEV:], mixed[:P_DEV])
    sent_other = jnp.where(odd, mixed[:P_DEV], mixed[P_DEV:])
    head_same = lax.ppermute(sent_same, TURN, back(same))
    head_other = lax.ppermute(sent_other, TURN, back(other))
    (patch_latent,) = call(
        latent_kernel, [(P_DEV, 256)], [], 1 << 26, place, tab_own, tab_other, msg_own, msg_other
    )
    latent_mixed = jnp.concatenate(
        [jnp.where(odd, head_other, head_same), jnp.where(odd, head_same, head_other)], axis=1
    )
    return (patch_latent, latent_mixed)


def solution(mesh):
    fine = Mesh(mesh.devices.reshape(16, 2, 2, 4, 2), ("z", "yl", "c", "x", "yh"))
    return jax.shard_map(
        on_device,
        mesh=fine,
        in_specs=(
            P(CTX),
            P(CTX),
            P(),
            P(None, TP),
            P(None, TP),
            P(None, TP),
            P(),
            P(CTX, TP),
            P(CTX, TP),
            P(CTX, TP),
        ),
        out_specs=(P(CTX, TP), P(CTX, TP)),
        check_vma=False,
    )
```

time: 644 us -> 160 us (0.25)
  the two profiles are of different devices: /device:TPU:1 before, /device:TPU:68 now
where the time goes in v1:
time: 160 us; the launch traced here: 159 us
  starting transfers between devices  52.4 us (33%)
  waiting for transfers between devices  36.7 us (23%)
  blocking collectives  31.9 us (20%)
  Pallas kernels  24.8 us (16%)
  local copies, waits for them, and re-layouts  6.56 us (4%)
  matrix products  3.83 us (2%)
  other arithmetic  2.1 us (1%)
    all_to_all x1, blocking collectives, to_all(): lax.all_to_all(jnp.broadcast_to(value[None], (count, *value.shape)), axes...  31.9 us
    pallas_call x3, Pallas kernels, call(): pl.pallas_call(body, out_shape=[jax.ShapeDtypeStruct(shape, jnp.bfloat16)...  24.8 us
    ppermute x1, starting transfers between devices, on_device(): lax.ppermute(jnp.where(odd, messages[0], messages[1]), TURN, other)  15.9 us
    ppermute x1, waiting for transfers between devices, on_device(): lax.ppermute(jnp.where(odd, messages[1], messages[0]), TURN, same)  13.9 us
    all_to_all x2, starting transfers between devices, to_all(): lax.all_to_all(jnp.broadcast_to(value[None], (count, *value.shape)), axes...  12.4 us
    all_to_all x2, waiting for transfers between devices, to_all(): lax.all_to_all(jnp.broadcast_to(value[None], (count, *value.shape)), axes...  11 us
    ppermute x1, starting transfers between devices, on_device(): head_same = lax.ppermute(sent_same, TURN, back(same))  8.24 us
    ppermute x1, starting transfers between devices, on_device(): head_other = lax.ppermute(sent_other, TURN, back(other))  8.01 us
  transfers between devices with their start and end apart: 9, of which 6 were waited for; matrix products, arithmetic and copies ran while one was open for 1% of the time, Pallas kernels for 3%

profile of v1, /device:TPU:68, one launch (start us, length us, event | category | flops | bytes accessed | tf_op | source)
XLA Modules:
  0.0 159.2 jit_solution(2501838240219432489)
XLA Ops:
  1.7 1.3 convolution_convert_fusion.2
  3.0 1.3 convolution_convert_fusion.1
  4.2 1.3 convolution_convert_fusion
  5.6 1.3 broadcast_in_dim.6
  6.9 7.4 %all-to-all-start = ((bf16[8,128,768]{2,1,0:T(8,128)(2,1)}), bf16[8,128,768]{2,1,0:T(8,128)(2,1)S(1)}, u32[]{:S(2)}, u32[]{:S(2)}) async-start(bf16[8,128,768]{2,1,0:T(8,128)(2,1)} %broadcast_in_dim.6), calls=%async_computation | async-start | bytes 3145728 | tf_op jit(solution)/shard_map/all_to_all | solution.py:43
  14.5 15.9 %collective-permute-start.1 = (bf16[112,128]{1,0:T(8,128)(2,1)S(1)}, bf16[112,128]{1,0:T(8,128)(2,1)S(1)}, u32[]{:S(2)}, u32[]{:S(2)}) collective-permute-start(bf16[112,128]{1,0:T(8,128)(2,1)S(1)} %get-tuple-element.12), channel_id=1, source_target_pairs={{0,32},{1,96},{2,160},{3,224},{4,288},{5,352},{6,416},{7,480},{32,... | collective-permute-start | bytes 86024 | tf_op jit(solution)/shard_map/ppermute | solution.py:231
  30.3 2.1 %collective-permute-start.2 = (bf16[112,128]{1,0:T(8,128)(2,1)S(1)}, bf16[112,128]{1,0:T(8,128)(2,1)S(1)}, u32[]{:S(2)}, u32[]{:S(2)}) collective-permute-start(bf16[112,128]{1,0:T(8,128)(2,1)S(1)} %get-tuple-element.13), channel_id=1, source_target_pairs={{0,0},{1,64},{2,128},{3,192},{4,256},{5,320},{6,384},{7,448},{32,3... | collective-permute-start | bytes 86024 | tf_op jit(solution)/shard_map/ppermute | solution.py:230
  32.5 1.6 %collective-permute-done.1 = bf16[112,128]{1,0:T(8,128)(2,1)S(1)} collective-permute-done((bf16[112,128]{1,0:T(8,128)(2,1)S(1)}, bf16[112,128]{1,0:T(8,128)(2,1)S(1)}, u32[]{:S(2)}, u32[]{:S(2)}) %collective-permute-start.1) | collective-permute-done | bytes 28704 | tf_op jit(solution)/shard_map/ppermute | solution.py:231
  34.1 13.9 %collective-permute-done.2 = bf16[112,128]{1,0:T(8,128)(2,1)S(1)} collective-permute-done((bf16[112,128]{1,0:T(8,128)(2,1)S(1)}, bf16[112,128]{1,0:T(8,128)(2,1)S(1)}, u32[]{:S(2)}, u32[]{:S(2)}) %collective-permute-start.2) | collective-permute-done | bytes 28704 | tf_op jit(solution)/shard_map/ppermute | solution.py:230
  49.2 4.9 %all-to-all-start.1 = ((bf16[16,2,112,128]{3,2,1,0:T(8,128)(2,1)}), bf16[16,2,112,128]{3,2,1,0:T(8,128)(2,1)S(1)}, u32[]{:S(2)}, u32[]{:S(2)}) async-start(bf16[16,2,112,128]{3,2,1,0:T(8,128)(2,1)} %broadcast_in_dim.7), calls=%async_computation.1 | async-start | bytes 1835008 | tf_op jit(solution)/shard_map/all_to_all | solution.py:43
  54.2 1.9 %collective-permute-start = (bf16[8,128,768]{2,1,0:T(8,128)(2,1)S(1)}, bf16[8,128,768]{2,1,0:T(8,128)(2,1)}, u32[]{:S(2)}, u32[]{:S(2)}) collective-permute-start(bf16[8,128,768]{2,1,0:T(8,128)(2,1)S(1)} %all-to-all-done.tab_own), channel_id=1, source_target_pairs={{0,8},{8,0},{1,9},{9,1},{2,10},{10,2},{3,11},{11,3},{4,12},{12,4},... | collective-permute-start | bytes 4718600 | tf_op jit(solution)/shard_map/ppermute | solution.py:245
  56.1 11.0 %all-to-all-done.1.msg_own = bf16[16,2,112,128]{3,2,1,0:T(8,128)(2,1)S(1)} async-done(((bf16[16,2,112,128]{3,2,1,0:T(8,128)(2,1)}), bf16[16,2,112,128]{3,2,1,0:T(8,128)(2,1)S(1)}, u32[]{:S(2)}, u32[]{:S(2)}) %all-to-all-start.1) | async-done | bytes 917536 | tf_op jit(solution)/shard_map/all_to_all | solution.py:43
  67.0 1.9 %collective-permute-start.3 = (bf16[16,2,112,128]{3,2,1,0:T(8,128)(2,1)S(1)}, bf16[16,2,112,128]{3,2,1,0:T(8,128)(2,1)}, u32[]{:S(2)}, u32[]{:S(2)}) collective-permute-start(bf16[16,2,112,128]{3,2,1,0:T(8,128)(2,1)S(1)} %all-to-all-done.1.msg_own), channel_id=1, source_target_pairs={{0,8},{8,0},{1,9},{9,1},{2,10},{10,2},{3,11},{11,3},{4,12},{12,4},... | collective-permute-start | bytes 2752520 | tf_op jit(solution)/shard_map/ppermute | solution.py:247
  70.2 1.3 collective-permute-done.3.msg_other
  71.5 13.9 %shard_map.114 = (bf16[256,128]{1,0:T(8,128)(2,1)}, bf16[256,256]{1,0:T(8,128)(2,1)}) custom-call(s32[4]{0:T(128)} %pad_add_fusion.place_ref, bf16[8,128,768]{2,1,0:T(8,128)(2,1)} %copy-done.1, bf16[8,128,768]{2,1,0:T(8,128)(2,1)} %collective-permute-done.tab_other, bf16[16,2,112,128]{3,2,1,0:T(8,128)(2,1)} %copy-done.3, ...), custom_call_target="tpu_custom_call" | custom-call | flops 1073741824 | bytes 4194304 | tf_op jit(solution)/shard_map/pallas_call | solution.py:194
  86.5 31.9 %all_to_all.15.kv_own = bf16[16,256,256]{2,1,0:T(8,128)(2,1)S(1)} all-to-all(bf16[16,256,256]{2,1,0:T(8,128)(2,1)S(1)} %broadcast_in_dim.8), channel_id=1, replica_groups=mesh['z'=16,'yl'=2,'c'=2,'x'=4,'yh'=2] {'yl','x','yh'}, dimensions={0} | all-to-all | bytes 4194304 | tf_op jit(solution)/shard_map/all_to_all | solution.py:43
  118.4 1.9 %collective-permute-start.4 = (bf16[16,256,256]{2,1,0:T(8,128)(2,1)S(1)}, bf16[16,256,256]{2,1,0:T(8,128)(2,1)S(1)}, u32[]{:S(2)}, u32[]{:S(2)}) collective-permute-start(bf16[16,256,256]{2,1,0:T(8,128)(2,1)S(1)} %all_to_all.15.kv_own), channel_id=1, source_target_pairs={{0,8},{8,0},{1,9},{9,1},{2,10},{10,2},{3,11},{11,3},{4,12},{12,4},... | collective-permute-start | bytes 6291464 | tf_op jit(solution)/shard_map/ppermute | solution.py:262
  120.3 4.1 %collective-permute-done.4.kv_other = bf16[16,256,256]{2,1,0:T(8,128)(2,1)S(1)} collective-permute-done((bf16[16,256,256]{2,1,0:T(8,128)(2,1)S(1)}, bf16[16,256,256]{2,1,0:T(8,128)(2,1)S(1)}, u32[]{:S(2)}, u32[]{:S(2)}) %collective-permute-start.4) | collective-permute-done | bytes 2097184 | tf_op jit(solution)/shard_map/ppermute | solution.py:262
  124.5 1.3 copy-done.4
  125.8 6.4 %shard_map.115 = bf16[256,128]{1,0:T(8,128)(2,1)} custom-call(s32[4]{0:T(128)} %pad_add_fusion.place_ref, bf16[256,128]{1,0:T(8,128)(2,1)} %get-tuple-element.4.q_ref, bf16[16,256,256]{2,1,0:T(8,128)(2,1)} %copy-done.2, bf16[16,256,256]{2,1,0:T(8,128)(2,1)} %copy-done.4), custom_call_target="tpu_custom_call" | custom-call | flops 1073741824 | bytes 4194304 | tf_op jit(solution)/shard_map/pallas_call | solution.py:194
  133.0 8.0 %collective-permute-start.5 = (bf16[128,128]{1,0:T(8,128)(2,1)S(1)}, bf16[128,128]{1,0:T(8,128)(2,1)S(1)}, u32[]{:S(2)}, u32[]{:S(2)}) collective-permute-start(bf16[128,128]{1,0:T(8,128)(2,1)S(1)} %get-tuple-element.8), channel_id=1, source_target_pairs={{32,0},{96,1},{160,2},{224,3},{288,4},{352,5},{416,6},{480,7},{0,3... | collective-permute-start | bytes 98312 | tf_op jit(solution)/shard_map/ppermute | solution.py:276
  141.0 8.2 %collective-permute-start.6 = (bf16[128,128]{1,0:T(8,128)(2,1)S(1)}, bf16[128,128]{1,0:T(8,128)(2,1)S(1)}, u32[]{:S(2)}, u32[]{:S(2)}) collective-permute-start(bf16[128,128]{1,0:T(8,128)(2,1)S(1)} %get-tuple-element.9), channel_id=1, source_target_pairs={{0,0},{64,1},{128,2},{192,3},{256,4},{320,5},{384,6},{448,7},{32,3... | collective-permute-start | bytes 98312 | tf_op jit(solution)/shard_map/ppermute | solution.py:275
  149.2 4.5 %shard_map.113 = bf16[128,256]{1,0:T(8,128)(2,1)} custom-call(s32[4]{0:T(128)} %pad_add_fusion.place_ref, bf16[8,128,768]{2,1,0:T(8,128)(2,1)} %copy-done.1, bf16[8,128,768]{2,1,0:T(8,128)(2,1)} %collective-permute-done.tab_other, bf16[16,2,112,128]{3,2,1,0:T(8,128)(2,1)} %copy-done.3, bf16[16,2,112,128]{3,2,1,0:T(8,128)(2,1)} %collective-permute-done.3.msg_other), custom_call_target="tpu_custom_call" | custom-call | flops 67108864 | bytes 4194304 | tf_op jit(solution)/shard_map/pallas_call | solution.py:194
  153.7 4.8 %collective-permute-done.6 = bf16[128,128]{1,0:T(8,128)(2,1)S(1)} collective-permute-done((bf16[128,128]{1,0:T(8,128)(2,1)S(1)}, bf16[128,128]{1,0:T(8,128)(2,1)S(1)}, u32[]{:S(2)}, u32[]{:S(2)}) %collective-permute-start.6) | collective-permute-done | bytes 32800 | tf_op jit(solution)/shard_map/ppermute | solution.py:275
  (40 shorter events, 6.1 us)
Async XLA Ops:
  0.6 1.0 copy-start
  5.6 8.8 %copy-start.10 = (s32[128]{0:T(128)S(1)}, s32[128]{0:T(128)}, u32[]{:S(2)}) copy-start(s32[128]{0:T(128)} %param.11) | copy-start | bytes 1540
  5.6 8.8 %copy-start.9 = (s32[512]{0:T(512)S(1)}, s32[512]{0:T(512)}, u32[]{:S(2)}) copy-start(s32[512]{0:T(512)} %param.10) | copy-start | bytes 6148
  5.6 8.8 %copy-start.5 = (bf16[32,256]{1,0:T(8,128)(2,1)S(1)}, bf16[32,256]{1,0:T(8,128)(2,1)}, u32[]{:S(2)}) copy-start(bf16[32,256]{1,0:T(8,128)(2,1)} %param.19) | copy-start | bytes 49156
  5.6 8.8 %copy-start.6 = (bf16[32,256]{1,0:T(8,128)(2,1)S(1)}, bf16[32,256]{1,0:T(8,128)(2,1)}, u32[]{:S(2)}) copy-start(bf16[32,256]{1,0:T(8,128)(2,1)} %param.17) | copy-start | bytes 49156
  5.6 8.8 %copy-start.7 = (bf16[32,256]{1,0:T(8,128)(2,1)S(1)}, bf16[32,256]{1,0:T(8,128)(2,1)}, u32[]{:S(2)}) copy-start(bf16[32,256]{1,0:T(8,128)(2,1)} %param.18) | copy-start | bytes 49156
  6.9 41.1 %all-to-all-start = ((bf16[8,128,768]{2,1,0:T(8,128)(2,1)}), bf16[8,128,768]{2,1,0:T(8,128)(2,1)S(1)}, u32[]{:S(2)}, u32[]{:S(2)}) async-start(bf16[8,128,768]{2,1,0:T(8,128)(2,1)} %broadcast_in_dim.6), calls=%async_computation | async-start | bytes 3145728 | tf_op jit(solution)/shard_map/all_to_all | solution.py:43
  14.3 54.6 %copy-start.8 = (f32[2048]{0:T(1024)S(1)}, f32[2048]{0:T(1024)}, u32[]{:S(2)}) copy-start(f32[2048]{0:T(1024)} %param.16) | copy-start | bytes 24580
  14.5 19.6 %collective-permute-start.1 = (bf16[112,128]{1,0:T(8,128)(2,1)S(1)}, bf16[112,128]{1,0:T(8,128)(2,1)S(1)}, u32[]{:S(2)}, u32[]{:S(2)}) collective-permute-start(bf16[112,128]{1,0:T(8,128)(2,1)S(1)} %get-tuple-element.12), channel_id=1, source_target_pairs={{0,32},{1,96},{2,160},{3,224},{4,288},{5,352},{6,416},{7,480},{32,... | collective-permute-start | bytes 86024 | tf_op jit(solution)/shard_map/ppermute | solution.py:231
  30.3 17.6 %collective-permute-start.2 = (bf16[112,128]{1,0:T(8,128)(2,1)S(1)}, bf16[112,128]{1,0:T(8,128)(2,1)S(1)}, u32[]{:S(2)}, u32[]{:S(2)}) collective-permute-start(bf16[112,128]{1,0:T(8,128)(2,1)S(1)} %get-tuple-element.13), channel_id=1, source_target_pairs={{0,0},{1,64},{2,128},{3,192},{4,256},{5,320},{6,384},{7,448},{32,3... | collective-permute-start | bytes 86024 | tf_op jit(solution)/shard_map/ppermute | solution.py:230
  48.0 23.5 %copy-start.1 = (bf16[8,128,768]{2,1,0:T(8,128)(2,1)}, bf16[8,128,768]{2,1,0:T(8,128)(2,1)S(1)}, u32[]{:S(2)}) copy-start(bf16[8,128,768]{2,1,0:T(8,128)(2,1)S(1)} %all-to-all-done.tab_own) | copy-start | bytes 4718596
  49.2 17.8 %all-to-all-start.1 = ((bf16[16,2,112,128]{3,2,1,0:T(8,128)(2,1)}), bf16[16,2,112,128]{3,2,1,0:T(8,128)(2,1)S(1)}, u32[]{:S(2)}, u32[]{:S(2)}) async-start(bf16[16,2,112,128]{3,2,1,0:T(8,128)(2,1)} %broadcast_in_dim.7), calls=%async_computation.1 | async-start | bytes 1835008 | tf_op jit(solution)/shard_map/all_to_all | solution.py:43
  54.2 17.4 %collective-permute-start = (bf16[8,128,768]{2,1,0:T(8,128)(2,1)S(1)}, bf16[8,128,768]{2,1,0:T(8,128)(2,1)}, u32[]{:S(2)}, u32[]{:S(2)}) collective-permute-start(bf16[8,128,768]{2,1,0:T(8,128)(2,1)S(1)} %all-to-all-done.tab_own), channel_id=1, source_target_pairs={{0,8},{8,0},{1,9},{9,1},{2,10},{10,2},{3,11},{11,3},{4,12},{12,4},... | collective-permute-start | bytes 4718600 | tf_op jit(solution)/shard_map/ppermute | solution.py:245
  67.0 4.5 %copy-start.3 = (bf16[16,2,112,128]{3,2,1,0:T(8,128)(2,1)}, bf16[16,2,112,128]{3,2,1,0:T(8,128)(2,1)S(1)}, u32[]{:S(2)}) copy-start(bf16[16,2,112,128]{3,2,1,0:T(8,128)(2,1)S(1)} %all-to-all-done.1.msg_own) | copy-start | bytes 2752516
  67.0 4.5 %collective-permute-start.3 = (bf16[16,2,112,128]{3,2,1,0:T(8,128)(2,1)S(1)}, bf16[16,2,112,128]{3,2,1,0:T(8,128)(2,1)}, u32[]{:S(2)}, u32[]{:S(2)}) collective-permute-start(bf16[16,2,112,128]{3,2,1,0:T(8,128)(2,1)S(1)} %all-to-all-done.1.msg_own), channel_id=1, source_target_pairs={{0,8},{8,0},{1,9},{9,1},{2,10},{10,2},{3,11},{11,3},{4,12},{12,4},... | collective-permute-start | bytes 2752520 | tf_op jit(solution)/shard_map/ppermute | solution.py:247
  118.4 6.0 %copy-start.2 = (bf16[16,256,256]{2,1,0:T(8,128)(2,1)}, bf16[16,256,256]{2,1,0:T(8,128)(2,1)S(1)}, u32[]{:S(2)}) copy-start(bf16[16,256,256]{2,1,0:T(8,128)(2,1)S(1)} %all_to_all.15.kv_own) | copy-start | bytes 6291460
  118.4 6.0 %collective-permute-start.4 = (bf16[16,256,256]{2,1,0:T(8,128)(2,1)S(1)}, bf16[16,256,256]{2,1,0:T(8,128)(2,1)S(1)}, u32[]{:S(2)}, u32[]{:S(2)}) collective-permute-start(bf16[16,256,256]{2,1,0:T(8,128)(2,1)S(1)} %all_to_all.15.kv_own), channel_id=1, source_target_pairs={{0,8},{8,0},{1,9},{9,1},{2,10},{10,2},{3,11},{11,3},{4,12},{12,4},... | collective-permute-start | bytes 6291464 | tf_op jit(solution)/shard_map/ppermute | solution.py:262
  124.4 1.3 copy-start.4
  133.0 20.8 %collective-permute-start.5 = (bf16[128,128]{1,0:T(8,128)(2,1)S(1)}, bf16[128,128]{1,0:T(8,128)(2,1)S(1)}, u32[]{:S(2)}, u32[]{:S(2)}) collective-permute-start(bf16[128,128]{1,0:T(8,128)(2,1)S(1)} %get-tuple-element.8), channel_id=1, source_target_pairs={{32,0},{96,1},{160,2},{224,3},{288,4},{352,5},{416,6},{480,7},{0,3... | collective-permute-start | bytes 98312 | tf_op jit(solution)/shard_map/ppermute | solution.py:276
  141.0 17.5 %collective-permute-start.6 = (bf16[128,128]{1,0:T(8,128)(2,1)S(1)}, bf16[128,128]{1,0:T(8,128)(2,1)S(1)}, u32[]{:S(2)}, u32[]{:S(2)}) collective-permute-start(bf16[128,128]{1,0:T(8,128)(2,1)S(1)} %get-tuple-element.9), channel_id=1, source_target_pairs={{0,0},{64,1},{128,2},{192,3},{256,4},{320,5},{384,6},{448,7},{32,3... | collective-permute-start | bytes 98312 | tf_op jit(solution)/shard_map/ppermute | solution.py:275

commit v2 on v1

v2 whole, which is shorter than its diff:
```python
import math

import jax
import jax.numpy as jnp
from jax import lax
from jax.experimental import pallas as pl
from jax.experimental.pallas import tpu as pltpu
from jax.sharding import Mesh
from jax.sharding import PartitionSpec as P

HD = 128
SCALE = 1.0 / math.sqrt(HD)
NEG = -1e30
N_CTX = 64
N_TP = 8
BYTES_DEV = 512
P_DEV = 128
W_ROWS = 32
VALUES = 64
TABLE = 6 * VALUES
ROWS = TABLE + 2 * 3 * W_ROWS
MSG = ROWS + 2 * 16
VMEM = 56 * 1024 * 1024

CTX = ("z", "yl", "c")
TP = ("x", "yh")
PLANE = ("x", "yh", "yl")
TURN = ("z", "x", "yh")


def turns():
    same, other = [], []
    for z in range(16):
        for t in range(N_TP):
            far, low = z // 8, min(z, 15 - z)
            same.append((z * N_TP + t, (2 * t + far) * N_TP + low))
            other.append((z * N_TP + t, (2 * t + 1 - far) * N_TP + low))
    return same, other


def back(pairs):
    return [(target, source) for source, target in pairs]


def to_all(value, axes, count):
    return lax.all_to_all(jnp.broadcast_to(value[None], (count, *value.shape)), axes, 0, 0)


def nt_dot(a, b):
    return lax.dot_general(a, b, (((1,), (1,)), ((), ())), preferred_element_type=jnp.float32)


def lens_before(d, c, own_ref, other_ref):
    total = jnp.zeros((), jnp.float32)
    for ref, core in ((own_ref, c), (other_ref, 1 - c)):
        for b in range(2):
            tiles = ref[:, ROWS + 16 * b : ROWS + 16 * (b + 1), :].astype(jnp.float32)
            unit, row = (lax.broadcasted_iota(jnp.int32, tiles.shape, i) for i in range(2))
            z = unit // 2 if b == 0 else 15 - unit // 2
            place = 4 * z + 2 * (unit % 2) + core
            total = total + jnp.sum(jnp.where((row == 4) & (place < d), tiles, 0.0))
    return total


def byte_counts(d, c, own_ref, other_ref):
    follow = jnp.where(d < N_CTX - 1, d + 1, d - 1)

    def tile(ref, place):
        z = place // 4
        unit = 2 * jnp.minimum(z, 15 - z) + (place // 2) % 2
        first = pl.multiple_of(ROWS + 16 * (z // 8), 16)
        return ref[unit, pl.ds(first, 16), :].astype(jnp.float32)

    here, beyond = tile(own_ref, d), tile(other_ref, follow)
    begin = lens_before(d, c, own_ref, other_ref) - (d * BYTES_DEV).astype(jnp.float32)
    lens_row = here[4:5, :]
    row = lax.broadcasted_iota(jnp.int32, (P_DEV, P_DEV), 0)
    col = lax.broadcasted_iota(jnp.int32, (P_DEV, P_DEV), 1)
    lens = jnp.sum(jnp.where(col == row, lens_row, 0.0), axis=1, keepdims=True)
    start = begin + jnp.sum(jnp.where(col < row, lens_row, 0.0), axis=1, keepdims=True)
    end = start + lens
    value = (lax.broadcasted_iota(jnp.int32, (256, P_DEV), 0) + 128 * c) % 256
    value = value.astype(jnp.float32)
    slot = col.astype(jnp.float32)
    counts = jnp.zeros((P_DEV, 256), jnp.float32)
    for chunk in range(6):
        ids = here[chunk : chunk + 1, :] if chunk < 4 else beyond[chunk - 4 : chunk - 3, :]
        at = slot + 128.0 * chunk
        member = ((at >= start) & (at < end)).astype(jnp.bfloat16)
        onehot = (value == ids).astype(jnp.bfloat16)
        counts = counts + nt_dot(member, onehot)
    return counts, lens


def table_of(tt, own_ref, other_ref):
    def piece(i):
        rows = slice(i * VALUES, (i + 1) * VALUES)
        parts = [ref[2 * tt + side, rows, :] for ref in (own_ref, other_ref) for side in range(2)]
        return jnp.concatenate(parts, axis=0)

    return [piece(i) for i in range(6)]


def two_heads(counts, lens, table):
    times = counts.astype(jnp.bfloat16)
    share = 1.0 / lens
    hide = jnp.where(counts > 0.0, 0.0, NEG)
    outs = []
    for a in range(2):
        queries, keys, values = table[a], table[2 + a], table[4 + a]
        pooled = jnp.dot(times, queries, preferred_element_type=jnp.float32)
        scores = nt_dot((pooled * share).astype(jnp.bfloat16), keys) * SCALE + hide
        expo = jnp.exp(scores - jnp.max(scores, axis=-1, keepdims=True))
        norm = jnp.sum(expo * counts, axis=-1, keepdims=True)
        weights = (expo * (1.0 / norm)).astype(jnp.bfloat16).astype(jnp.float32) * counts
        out = jnp.dot(weights.astype(jnp.bfloat16), values, preferred_element_type=jnp.float32)
        outs.append(out.astype(jnp.bfloat16))
    return jnp.concatenate(outs, axis=1)


def encode_kernel(place_ref, own_ref, other_ref, gain_ref, q_ref, kv_ref, latent, weight):
    c, yl, t = place_ref[0], place_ref[1], place_ref[2]
    parts = [
        byte_counts(4 * z + 2 * yl + c, c, own_ref, other_ref) for z in (t, 2 * N_TP - 1 - t)
    ]
    counts = jnp.concatenate([part[0] for part in parts], axis=0)
    lens = jnp.concatenate([part[1] for part in parts], axis=0)

    def heads(tt, squares):
        out = two_heads(counts, lens, table_of(tt, own_ref, other_ref))
        latent[tt] = out
        wide = out.astype(jnp.float32)
        for ref, core in ((own_ref, c), (other_ref, 1 - c)):
            for b in range(2):
                z = tt if b == 0 else 15 - tt
                for side in range(2):
                    first = pl.multiple_of(W_ROWS * (4 * (z % 2) + 2 * side + core), W_ROWS)
                    for n in range(3):
                        start = TABLE + (3 * b + n) * W_ROWS
                        weight[z // 2, pl.ds(first, W_ROWS), n * HD : (n + 1) * HD] = ref[
                            2 * tt + side, start : start + W_ROWS, :
                        ]
        return squares + jnp.sum(wide * wide, axis=-1, keepdims=True)

    squares = lax.fori_loop(0, N_TP, heads, jnp.zeros((2 * P_DEV, 1), jnp.float32))
    inverse = lax.rsqrt(squares / 2048.0 + 1e-05)
    total = jnp.zeros((2 * P_DEV, 3 * HD), jnp.float32)
    for tt in range(N_TP):
        normed = latent[tt].astype(jnp.float32) * inverse * gain_ref[tt : tt + 1, :]
        total = total + jnp.dot(
            normed.astype(jnp.bfloat16), weight[tt], preferred_element_type=jnp.float32
        )
    total = total.astype(jnp.bfloat16)
    q_ref[...] = total[:, :HD]
    kv_ref[...] = total[:, HD:]


def latent_kernel(place_ref, own_ref, other_ref, out_ref):
    c, t, d = place_ref[0], place_ref[2], place_ref[3]
    counts, lens = byte_counts(d, c, own_ref, other_ref)
    out_ref[...] = two_heads(counts, lens, table_of(t, own_ref, other_ref))


def table_kernel(place_ref, table_ref, wq_ref, wk_ref, wv_ref, out_ref):
    first = 2 * VALUES * place_ref[0] + VALUES * place_ref[1]
    rows = table_ref[pl.ds(pl.multiple_of(first, VALUES), VALUES), :]
    for i, ref in enumerate((wq_ref, wk_ref, wv_ref)):
        part = jnp.dot(rows, ref[...], preferred_element_type=jnp.float32).astype(jnp.bfloat16)
        for a in range(2):
            start = (2 * i + a) * VALUES
            out_ref[start : start + VALUES, :] = part[:, a * HD : (a + 1) * HD]


def attend_kernel(place_ref, q_ref, kv_own, kv_other, out_ref, scores):
    c, yl, t = place_ref[0], place_ref[1], place_ref[2]
    query = q_ref[...]
    size = 2 * P_DEV
    row = lax.broadcasted_iota(jnp.int32, (size, size), 0)
    col = lax.broadcasted_iota(jnp.int32, (size, size), 1)
    last = 2 * N_TP - 1

    def places(index, tt):
        z = jnp.where(index < P_DEV, tt, last - tt)
        return 512 * z + index % P_DEV

    row_at = places(row, t) + 256 * yl + P_DEV * c

    def first(tt, top):
        for i, (ref, core) in enumerate(((kv_own, c), (kv_other, 1 - c))):
            for side in range(2):
                s = nt_dot(query, ref[2 * tt + side, :, :HD]) * SCALE
                s = jnp.where(places(col, tt) + (256 * side + P_DEV * core) <= row_at, s, NEG)
                scores[tt, 2 * i + side] = s
                top = jnp.maximum(top, jnp.maximum(s[:, :HD], s[:, HD:]))
        return top

    top = lax.fori_loop(0, N_TP, first, jnp.full((size, HD), NEG, jnp.float32))
    top = jnp.max(top, axis=-1, keepdims=True)

    def second(tt, carry):
        norm, acc = carry
        for i, ref in enumerate((kv_own, kv_other)):
            for side in range(2):
                e = jnp.exp(scores[tt, 2 * i + side] - top)
                norm = norm + (e[:, :HD] + e[:, HD:])
                acc = acc + jnp.dot(
                    e.astype(jnp.bfloat16),
                    ref[2 * tt + side, :, HD:],
                    preferred_element_type=jnp.float32,
                )
        return norm, acc

    zero = jnp.zeros((size, HD), jnp.float32)
    norm, acc = lax.fori_loop(0, N_TP, second, (zero, zero))
    out = acc / jnp.sum(norm, axis=-1, keepdims=True)
    out_ref[...] = out.astype(jnp.bfloat16)


def call(body, outs, scratch, flops, *args):
    vmem = pl.BlockSpec(memory_space=pltpu.VMEM)
    smem = pl.BlockSpec(memory_space=pltpu.SMEM)
    return pl.pallas_call(
        body,
        out_shape=[jax.ShapeDtypeStruct(shape, jnp.bfloat16) for shape in outs],
        in_specs=[smem] + [vmem] * (len(args) - 1),
        out_specs=[vmem] * len(outs),
        scratch_shapes=scratch,
        compiler_params=pltpu.CompilerParams(vmem_limit_bytes=VMEM),
        cost_estimate=pl.CostEstimate(flops=flops, bytes_accessed=4 << 20, transcendentals=1 << 20),
    )(*args)


def run_table(*args):
    return call(table_kernel, [(TABLE, HD)], [], 1 << 28, *args)[0]


def run_encode(*args):
    return call(
        encode_kernel,
        [(2 * P_DEV, HD), (2 * P_DEV, 2 * HD)],
        [pltpu.VMEM((N_TP, 256, 256), jnp.bfloat16), pltpu.VMEM((N_TP, 256, 3 * HD), jnp.bfloat16)],
        1 << 30,
        *args,
    )


def run_latent(*args):
    return call(latent_kernel, [(P_DEV, 256)], [], 1 << 26, *args)[0]


def run_attend(*args):
    scratch = [pltpu.VMEM((N_TP, 4, 2 * P_DEV, 2 * P_DEV), jnp.float32)]
    return call(attend_kernel, [(2 * P_DEV, HD)], scratch, 1 << 30, *args)[0]


def on_device(
    byte_ids,
    patch_lens,
    byte_table,
    wq_cross,
    wk_cross,
    wv_cross,
    norm_gain,
    wq_latent,
    wk_latent,
    wv_latent,
):
    z, yl, c = (lax.axis_index(name) for name in CTX)
    t = lax.axis_index("x") * 2 + lax.axis_index("yh")
    place = jnp.stack([c, yl, t, 4 * z + 2 * yl + c]).astype(jnp.int32)
    swap = [(0, 1), (1, 0)]
    same, other = turns()

    ints = jnp.concatenate([byte_ids, patch_lens]).astype(jnp.bfloat16).reshape(5, HD)
    ints = jnp.pad(ints, ((0, 11), (0, 0)))
    latent = (wq_latent, wk_latent, wv_latent)
    messages = [
        jnp.concatenate([w[:, a * HD : (a + 1) * HD] for w in latent] + [ints], axis=0) for a in range(2)
    ]
    far, odd = z >= 8, z % 2 == 1
    got_same = lax.ppermute(jnp.where(far, messages[1], messages[0]), TURN, same)
    got_other = lax.ppermute(jnp.where(far, messages[0], messages[1]), TURN, other)

    table = run_table(place, byte_table, wq_cross, wk_cross, wv_cross)
    table, got_same, got_other = lax.optimization_barrier((table, got_same, got_other))
    near = jnp.where(odd, got_other, got_same)
    away = jnp.where(odd, got_same, got_other)
    cut = 3 * W_ROWS
    message = jnp.concatenate([table, near[:cut], away[:cut], near[cut:], away[cut:]], axis=0)
    own = to_all(message, PLANE, 16)
    other_core = lax.ppermute(own, "c", swap)

    gain = norm_gain.reshape(N_TP, 256)
    q, kv = run_encode(place, own, other_core, gain)
    kv_own = to_all(kv, PLANE, 16)
    kv_other = lax.ppermute(kv_own, "c", swap)
    mixed = run_attend(place, q, kv_own, kv_other)
    sent_same = jnp.where(odd, mixed[P_DEV:], mixed[:P_DEV])
    sent_other = jnp.where(odd, mixed[:P_DEV], mixed[P_DEV:])
    head_same = lax.ppermute(sent_same, TURN, back(same))
    head_other = lax.ppermute(sent_other, TURN, back(other))
    patch_latent = run_latent(place, own, other_core)
    latent_mixed = jnp.concatenate(
        [jnp.where(far, head_other, head_same), jnp.where(far, head_same, head_other)], axis=1
    )
    return (patch_latent, latent_mixed)


def solution(mesh):
    fine = Mesh(mesh.devices.reshape(16, 2, 2, 4, 2), ("z", "yl", "c", "x", "yh"))
    return jax.shard_map(
        on_device,
        mesh=fine,
        in_specs=(
            P(CTX),
            P(CTX),
            P(),
            P(None, TP),
            P(None, TP),
            P(None, TP),
            P(),
            P(CTX, TP),
            P(CTX, TP),
            P(CTX, TP),
        ),
        out_specs=(P(CTX, TP), P(CTX, TP)),
        check_vma=False,
    )
```

time: 160 us -> 166 us (1.038)
  the two profiles are of different devices: /device:TPU:68 before, /device:TPU:102 now
where the time goes in v2:
time: 166 us; the launch traced here: 165 us
  blocking collectives  68.1 us (41%)
  starting transfers between devices  40.4 us (24%)
  Pallas kernels  29.2 us (18%)
  waiting for transfers between devices  17.6 us (11%)
  local copies, waits for them, and re-layouts  5.82 us (4%)
  other arithmetic  3.47 us (2%)
    all_to_all x2, blocking collectives, to_all(): lax.all_to_all(jnp.broadcast_to(value[None], (count, *value.shape)), axes...  68.1 us
    pallas_call x4, Pallas kernels, call(): pl.pallas_call(body, out_shape=[jax.ShapeDtypeStruct(shape, jnp.bfloat16)...  29.2 us
    ppermute x1, starting transfers between devices, on_device(): head_same = lax.ppermute(sent_same, TURN, back(same))  15.3 us
    ppermute x1, starting transfers between devices, on_device(): lax.ppermute(jnp.where(far, messages[0], messages[1]), TURN, other)  14.4 us
    ppermute x1, waiting for transfers between devices, on_device(): lax.ppermute(jnp.where(far, messages[1], messages[0]), TURN, same)  9.26 us
    ppermute x1, starting transfers between devices, on_device(): lax.ppermute(jnp.where(far, messages[1], messages[0]), TURN, same)  4.99 us
    ppermute x1, waiting for transfers between devices, on_device(): other_core = lax.ppermute(own, 'c', swap)  4.21 us
    ppermute x1, waiting for transfers between devices, on_device(): kv_other = lax.ppermute(kv_own, 'c', swap)  4.13 us
  transfers between devices with their start and end apart: 6, of which 3 were waited for; matrix products, arithmetic and copies ran while one was open for 1% of the time, Pallas kernels for 4%

profile of v2, /device:TPU:102, one launch (start us, length us, event | category | flops | bytes accessed | tf_op | source)
XLA Modules:
  0.0 165.4 jit_solution(5910759893176779964)
XLA Ops:
  0.6 0.7 convert.7
  1.3 0.7 convert.6
  2.0 0.7 fusion.5
  2.7 0.8 fusion.3
  3.5 14.4 %collective-permute-start.1 = (bf16[112,128]{1,0:T(8,128)(2,1)S(1)}, bf16[112,128]{1,0:T(8,128)(2,1)S(1)}, u32[]{:S(2)}, u32[]{:S(2)}) collective-permute-start(bf16[112,128]{1,0:T(8,128)(2,1)S(1)} %get-tuple-element.18), channel_id=1, source_target_pairs={{0,32},{1,96},{2,160},{3,224},{4,288},{5,352},{6,416},{7,480},{32,... | collective-permute-start | bytes 86024 | tf_op jit(solution)/shard_map/ppermute | solution.py:282
  17.9 5.0 %collective-permute-start = (bf16[112,128]{1,0:T(8,128)(2,1)S(1)}, bf16[112,128]{1,0:T(8,128)(2,1)S(1)}, u32[]{:S(2)}, u32[]{:S(2)}) collective-permute-start(bf16[112,128]{1,0:T(8,128)(2,1)S(1)} %get-tuple-element.19), channel_id=1, source_target_pairs={{0,0},{1,64},{2,128},{3,192},{4,256},{5,320},{6,384},{7,448},{32,1... | collective-permute-start | bytes 86024 | tf_op jit(solution)/shard_map/ppermute | solution.py:281
  22.9 0.7 pad_add_fusion.place_ref
  23.6 2.6 %shard_map.113 = bf16[384,128]{1,0:T(8,128)(2,1)} custom-call(s32[4]{0:T(128)} %pad_add_fusion.place_ref, bf16[256,1024]{1,0:T(8,128)(2,1)} %table_ref.1, bf16[1024,256]{1,0:T(8,128)(2,1)} %wq_ref.1, bf16[1024,256]{1,0:T(8,128)(2,1)} %wk_ref.1, bf16[1024,256]{1,0:T(8,128)(2,1)} %wv_ref.1), custom_call_target="tpu_custom_call" | custom-call | flops 268435456 | bytes 4194304 | tf_op jit(solution)/shard_map/pallas_call | solution.py:222
  26.1 9.3 %collective-permute-done = bf16[112,128]{1,0:T(8,128)(2,1)S(1)} collective-permute-done((bf16[112,128]{1,0:T(8,128)(2,1)S(1)}, bf16[112,128]{1,0:T(8,128)(2,1)S(1)}, u32[]{:S(2)}, u32[]{:S(2)}) %collective-permute-start) | collective-permute-done | bytes 28704 | tf_op jit(solution)/shard_map/ppermute | solution.py:281
  35.4 0.9 constant_dynamic-update-slice_fusion.2
  36.7 36.1 %all_to_all.10.own_ref = bf16[16,608,128]{2,1,0:T(8,128)(2,1)S(1)} all-to-all(bf16[16,608,128]{2,1,0:T(8,128)(2,1)S(1)} %broadcast_in_dim.4), channel_id=1, replica_groups=mesh['z'=16,'yl'=2,'c'=2,'x'=4,'yh'=2] {'x','yh','yl'}, dimensions={0} | all-to-all | bytes 4980736 | tf_op jit(solution)/shard_map/all_to_all | solution.py:46
  72.7 1.9 %collective-permute-start.2 = (bf16[16,608,128]{2,1,0:T(8,128)(2,1)S(1)}, bf16[16,608,128]{2,1,0:T(8,128)(2,1)}, u32[]{:S(2)}, u32[]{:S(2)}) collective-permute-start(bf16[16,608,128]{2,1,0:T(8,128)(2,1)S(1)} %all_to_all.10.own_ref), channel_id=1, source_target_pairs={{0,8},{8,0},{1,9},{9,1},{2,10},{10,2},{3,11},{11,3},{4,12},{12,4},... | collective-permute-start | bytes 7471112 | tf_op jit(solution)/shard_map/ppermute | solution.py:291
  75.3 4.2 %collective-permute-done.2.other_ref = bf16[16,608,128]{2,1,0:T(8,128)(2,1)} collective-permute-done((bf16[16,608,128]{2,1,0:T(8,128)(2,1)S(1)}, bf16[16,608,128]{2,1,0:T(8,128)(2,1)}, u32[]{:S(2)}, u32[]{:S(2)}) %collective-permute-start.2) | collective-permute-done | bytes 2490400 | tf_op jit(solution)/shard_map/ppermute | solution.py:291
  79.5 13.8 %shard_map.115 = (bf16[256,128]{1,0:T(8,128)(2,1)}, bf16[256,256]{1,0:T(8,128)(2,1)}) custom-call(s32[4]{0:T(128)} %pad_add_fusion.place_ref, bf16[16,608,128]{2,1,0:T(8,128)(2,1)} %copy-done, bf16[16,608,128]{2,1,0:T(8,128)(2,1)} %collective-permute-done.2.other_ref, f32[8,256]{1,0:T(8,128)} %reshape.12.gain_ref), custom_call_target="tpu_custom_call" | custom-call | flops 1073741824 | bytes 4194304 | tf_op jit(solution)/shard_map/pallas_call | solution.py:222
  93.3 1.1 broadcast_in_dim.5
  94.4 32.0 %all_to_all.11.kv_own = bf16[16,256,256]{2,1,0:T(8,128)(2,1)S(1)} all-to-all(bf16[16,256,256]{2,1,0:T(8,128)(2,1)S(1)} %broadcast_in_dim.5), channel_id=1, replica_groups=mesh['z'=16,'yl'=2,'c'=2,'x'=4,'yh'=2] {'x','yh','yl'}, dimensions={0} | all-to-all | bytes 4194304 | tf_op jit(solution)/shard_map/all_to_all | solution.py:46
  126.4 1.9 %collective-permute-start.3 = (bf16[16,256,256]{2,1,0:T(8,128)(2,1)S(1)}, bf16[16,256,256]{2,1,0:T(8,128)(2,1)S(1)}, u32[]{:S(2)}, u32[]{:S(2)}) collective-permute-start(bf16[16,256,256]{2,1,0:T(8,128)(2,1)S(1)} %all_to_all.11.kv_own), channel_id=1, source_target_pairs={{0,8},{8,0},{1,9},{9,1},{2,10},{10,2},{3,11},{11,3},{4,12},{12,4},... | collective-permute-start | bytes 6291464 | tf_op jit(solution)/shard_map/ppermute | solution.py:296
  128.3 4.1 %collective-permute-done.3.kv_other = bf16[16,256,256]{2,1,0:T(8,128)(2,1)S(1)} collective-permute-done((bf16[16,256,256]{2,1,0:T(8,128)(2,1)S(1)}, bf16[16,256,256]{2,1,0:T(8,128)(2,1)S(1)}, u32[]{:S(2)}, u32[]{:S(2)}) %collective-permute-start.3) | collective-permute-done | bytes 2097184 | tf_op jit(solution)/shard_map/ppermute | solution.py:296
  132.4 1.4 copy-done.2
  133.8 8.3 %shard_map.116 = bf16[256,128]{1,0:T(8,128)(2,1)} custom-call(s32[4]{0:T(128)} %pad_add_fusion.place_ref, bf16[256,128]{1,0:T(8,128)(2,1)} %get-tuple-element.10.q_ref, bf16[16,256,256]{2,1,0:T(8,128)(2,1)} %copy-done.1, bf16[16,256,256]{2,1,0:T(8,128)(2,1)} %copy-done.2), custom_call_target="tpu_custom_call" | custom-call | flops 1073741824 | bytes 4194304 | tf_op jit(solution)/shard_map/pallas_call | solution.py:222
  142.1 0.8 broadcast_select_fusion.1
  142.9 1.9 %collective-permute-start.4 = (bf16[128,128]{1,0:T(8,128)(2,1)S(1)}, bf16[128,128]{1,0:T(8,128)(2,1)S(1)}, u32[]{:S(2)}, u32[]{:S(2)}) collective-permute-start(bf16[128,128]{1,0:T(8,128)(2,1)S(1)} %get-tuple-element.14), channel_id=1, source_target_pairs={{32,0},{96,1},{160,2},{224,3},{288,4},{352,5},{416,6},{480,7},{33,... | collective-permute-start | bytes 98312 | tf_op jit(solution)/shard_map/ppermute | solution.py:301
  144.8 15.3 %collective-permute-start.5 = (bf16[128,128]{1,0:T(8,128)(2,1)S(1)}, bf16[128,128]{1,0:T(8,128)(2,1)S(1)}, u32[]{:S(2)}, u32[]{:S(2)}) collective-permute-start(bf16[128,128]{1,0:T(8,128)(2,1)S(1)} %get-tuple-element.15), channel_id=1, source_target_pairs={{0,0},{64,1},{128,2},{192,3},{256,4},{320,5},{384,6},{448,7},{1,32... | collective-permute-start | bytes 98312 | tf_op jit(solution)/shard_map/ppermute | solution.py:300
  160.1 4.6 %shard_map.114 = bf16[128,256]{1,0:T(8,128)(2,1)} custom-call(s32[4]{0:T(128)} %pad_add_fusion.place_ref, bf16[16,608,128]{2,1,0:T(8,128)(2,1)} %copy-done, bf16[16,608,128]{2,1,0:T(8,128)(2,1)} %collective-permute-done.2.other_ref), custom_call_target="tpu_custom_call" | custom-call | flops 67108864 | bytes 4194304 | tf_op jit(solution)/shard_map/pallas_call | solution.py:222
  (21 shorter events, 1.7 us)
Async XLA Ops:
  3.5 22.6 %collective-permute-start.1 = (bf16[112,128]{1,0:T(8,128)(2,1)S(1)}, bf16[112,128]{1,0:T(8,128)(2,1)S(1)}, u32[]{:S(2)}, u32[]{:S(2)}) collective-permute-start(bf16[112,128]{1,0:T(8,128)(2,1)S(1)} %get-tuple-element.18), channel_id=1, source_target_pairs={{0,32},{1,96},{2,160},{3,224},{4,288},{5,352},{6,416},{7,480},{32,... | collective-permute-start | bytes 86024 | tf_op jit(solution)/shard_map/ppermute | solution.py:282
  17.9 17.5 %collective-permute-start = (bf16[112,128]{1,0:T(8,128)(2,1)S(1)}, bf16[112,128]{1,0:T(8,128)(2,1)S(1)}, u32[]{:S(2)}, u32[]{:S(2)}) collective-permute-start(bf16[112,128]{1,0:T(8,128)(2,1)S(1)} %get-tuple-element.19), channel_id=1, source_target_pairs={{0,0},{1,64},{2,128},{3,192},{4,256},{5,320},{6,384},{7,448},{32,1... | collective-permute-start | bytes 86024 | tf_op jit(solution)/shard_map/ppermute | solution.py:281
  36.7 38.0 %copy-start.3 = (f32[2048]{0:T(1024)S(1)}, f32[2048]{0:T(1024)}, u32[]{:S(2)}) copy-start(f32[2048]{0:T(1024)} %param.16) | copy-start | bytes 24580
  72.7 6.7 %copy-start = (bf16[16,608,128]{2,1,0:T(8,128)(2,1)}, bf16[16,608,128]{2,1,0:T(8,128)(2,1)S(1)}, u32[]{:S(2)}) copy-start(bf16[16,608,128]{2,1,0:T(8,128)(2,1)S(1)} %all_to_all.10.own_ref) | copy-start | bytes 7471108
  72.7 6.7 %collective-permute-start.2 = (bf16[16,608,128]{2,1,0:T(8,128)(2,1)S(1)}, bf16[16,608,128]{2,1,0:T(8,128)(2,1)}, u32[]{:S(2)}, u32[]{:S(2)}) collective-permute-start(bf16[16,608,128]{2,1,0:T(8,128)(2,1)S(1)} %all_to_all.10.own_ref), channel_id=1, source_target_pairs={{0,8},{8,0},{1,9},{9,1},{2,10},{10,2},{3,11},{11,3},{4,12},{12,4},... | collective-permute-start | bytes 7471112 | tf_op jit(solution)/shard_map/ppermute | solution.py:291
  126.4 6.0 %copy-start.1 = (bf16[16,256,256]{2,1,0:T(8,128)(2,1)}, bf16[16,256,256]{2,1,0:T(8,128)(2,1)S(1)}, u32[]{:S(2)}) copy-start(bf16[16,256,256]{2,1,0:T(8,128)(2,1)S(1)} %all_to_all.11.kv_own) | copy-start | bytes 6291460
  126.4 6.0 %collective-permute-start.3 = (bf16[16,256,256]{2,1,0:T(8,128)(2,1)S(1)}, bf16[16,256,256]{2,1,0:T(8,128)(2,1)S(1)}, u32[]{:S(2)}, u32[]{:S(2)}) collective-permute-start(bf16[16,256,256]{2,1,0:T(8,128)(2,1)S(1)} %all_to_all.11.kv_own), channel_id=1, source_target_pairs={{0,8},{8,0},{1,9},{9,1},{2,10},{10,2},{3,11},{11,3},{4,12},{12,4},... | collective-permute-start | bytes 6291464 | tf_op jit(solution)/shard_map/ppermute | solution.py:296
  132.4 1.4 copy-start.2
  142.9 21.8 %collective-permute-start.4 = (bf16[128,128]{1,0:T(8,128)(2,1)S(1)}, bf16[128,128]{1,0:T(8,128)(2,1)S(1)}, u32[]{:S(2)}, u32[]{:S(2)}) collective-permute-start(bf16[128,128]{1,0:T(8,128)(2,1)S(1)} %get-tuple-element.14), channel_id=1, source_target_pairs={{32,0},{96,1},{160,2},{224,3},{288,4},{352,5},{416,6},{480,7},{33,... | collective-permute-start | bytes 98312 | tf_op jit(solution)/shard_map/ppermute | solution.py:301
  144.8 19.9 %collective-permute-start.5 = (bf16[128,128]{1,0:T(8,128)(2,1)S(1)}, bf16[128,128]{1,0:T(8,128)(2,1)S(1)}, u32[]{:S(2)}, u32[]{:S(2)}) collective-permute-start(bf16[128,128]{1,0:T(8,128)(2,1)S(1)} %get-tuple-element.15), channel_id=1, source_target_pairs={{0,0},{64,1},{128,2},{192,3},{256,4},{320,5},{384,6},{448,7},{1,32... | collective-permute-start | bytes 98312 | tf_op jit(solution)/shard_map/ppermute | solution.py:300

commit v3 on v2

v3 whole, which is shorter than its diff:
```python
import math

import jax
import jax.numpy as jnp
from jax import lax
from jax.experimental import pallas as pl
from jax.experimental.pallas import tpu as pltpu
from jax.sharding import Mesh
from jax.sharding import PartitionSpec as P

HD = 128
SCALE = 1.0 / math.sqrt(HD)
NEG = -1e30
N_CTX = 64
N_TP = 8
BYTES_DEV = 512
P_DEV = 128
W_ROWS = 32
VALUES = 128
ROWS = 2 * 3 * W_ROWS
MSG = ROWS + 2 * 16
PART = 2 * P_DEV + 8
VMEM = 56 * 1024 * 1024

CTX = ("z", "yl", "c")
TP = ("x", "yh")
PLANE = ("x", "yh", "yl")
TURN = ("z", "x", "yh")


def turns():
    same, other = [], []
    for z in range(16):
        for t in range(N_TP):
            far, low = z // 8, min(z, 15 - z)
            same.append((z * N_TP + t, (2 * t + far) * N_TP + low))
            other.append((z * N_TP + t, (2 * t + 1 - far) * N_TP + low))
    return same, other


def back(pairs):
    return [(target, source) for source, target in pairs]


def to_all(value, axes, count):
    return lax.all_to_all(jnp.broadcast_to(value[None], (count, *value.shape)), axes, 0, 0)


def nt_dot(a, b):
    return lax.dot_general(a, b, (((1,), (1,)), ((), ())), preferred_element_type=jnp.float32)


def lens_before(d, c, own_ref, other_ref):
    total = jnp.zeros((), jnp.float32)
    for ref, core in ((own_ref, c), (other_ref, 1 - c)):
        for b in range(2):
            tiles = ref[:, ROWS + 16 * b : ROWS + 16 * (b + 1), :].astype(jnp.float32)
            unit, row = (lax.broadcasted_iota(jnp.int32, tiles.shape, i) for i in range(2))
            z = unit // 2 if b == 0 else 15 - unit // 2
            place = 4 * z + 2 * (unit % 2) + core
            total = total + jnp.sum(jnp.where((row == 4) & (place < d), tiles, 0.0))
    return total


def byte_counts(d, c, own_ref, other_ref):
    follow = jnp.where(d < N_CTX - 1, d + 1, d - 1)

    def tile(ref, place):
        z = place // 4
        unit = 2 * jnp.minimum(z, 15 - z) + (place // 2) % 2
        first = pl.multiple_of(ROWS + 16 * (z // 8), 16)
        return ref[unit, pl.ds(first, 16), :].astype(jnp.float32)

    here, beyond = tile(own_ref, d), tile(other_ref, follow)
    begin = lens_before(d, c, own_ref, other_ref) - (d * BYTES_DEV).astype(jnp.float32)
    lens_row = here[4:5, :]
    row = lax.broadcasted_iota(jnp.int32, (P_DEV, P_DEV), 0)
    col = lax.broadcasted_iota(jnp.int32, (P_DEV, P_DEV), 1)
    lens = jnp.sum(jnp.where(col == row, lens_row, 0.0), axis=1, keepdims=True)
    start = begin + jnp.sum(jnp.where(col < row, lens_row, 0.0), axis=1, keepdims=True)
    end = start + lens
    value = (lax.broadcasted_iota(jnp.int32, (256, P_DEV), 0) + 128 * c) % 256
    value = value.astype(jnp.float32)
    slot = col.astype(jnp.float32)
    counts = jnp.zeros((P_DEV, 256), jnp.float32)
    for chunk in range(6):
        ids = here[chunk : chunk + 1, :] if chunk < 4 else beyond[chunk - 4 : chunk - 3, :]
        at = slot + 128.0 * chunk
        member = ((at >= start) & (at < end)).astype(jnp.bfloat16)
        onehot = (value == ids).astype(jnp.bfloat16)
        counts = counts + nt_dot(member, onehot)
    return counts, lens


def two_heads(counts, lens, table):
    times = counts.astype(jnp.bfloat16)
    share = 1.0 / lens
    hide = jnp.where(counts > 0.0, 0.0, NEG)
    pooled = jnp.dot(times, table[:, :256], preferred_element_type=jnp.float32)
    query = (pooled * share).astype(jnp.bfloat16)
    outs = []
    for a in range(2):
        keys, values = (table[:, (i + a) * HD : (i + a + 1) * HD] for i in (2, 4))
        scores = nt_dot(query[:, a * HD : (a + 1) * HD], keys) * SCALE + hide
        expo = jnp.exp(scores - jnp.max(scores, axis=-1, keepdims=True))
        norm = jnp.sum(expo * counts, axis=-1, keepdims=True)
        weights = (expo * (1.0 / norm)).astype(jnp.bfloat16).astype(jnp.float32) * counts
        out = jnp.dot(weights.astype(jnp.bfloat16), values, preferred_element_type=jnp.float32)
        outs.append(out.astype(jnp.bfloat16))
    return jnp.concatenate(outs, axis=1)


def coordinates():
    z, yl, c = (lax.axis_index(name) for name in CTX)
    return z, yl, c, 2 * lax.axis_index("x") + lax.axis_index("yh")


def table_of(tt, own_ref, other_ref):
    return jnp.concatenate([own_ref[tt], other_ref[tt]], axis=0)


def start_kernel(
    ids_ref, lens_ref, table_ref, wq, wk, wv, lq, lk, lv, tables_ref, same_ref, other_ref
):
    z, _, c, _ = coordinates()
    rows = table_ref[pl.ds(pl.multiple_of(VALUES * c, VALUES), VALUES), :]
    for i, ref in enumerate((wq, wk, wv)):
        part = jnp.dot(rows, ref[...], preferred_element_type=jnp.float32).astype(jnp.bfloat16)
        for tt in range(N_TP):
            tables_ref[tt, :, 2 * i * HD : 2 * (i + 1) * HD] = part
    ints = jnp.concatenate(
        [ids_ref[...], lens_ref[...], jnp.zeros((11, HD), jnp.int32)], axis=0
    ).astype(jnp.float32)
    far = z // 8
    for out, a in ((same_ref, far), (other_ref, 1 - far)):
        for i, ref in enumerate((lq, lk, lv)):
            out[i * W_ROWS : (i + 1) * W_ROWS, :] = ref[:, pl.ds(pl.multiple_of(a * HD, HD), HD)]
        out[3 * W_ROWS :, :] = ints.astype(jnp.bfloat16)


def encode_kernel(
    tab_own, tab_other, own_ref, other_ref, gain_ref, q_ref, kv_ref, latent, weight
):
    _, yl, c, t = coordinates()
    parts = [
        byte_counts(4 * z + 2 * yl + c, c, own_ref, other_ref) for z in (t, 2 * N_TP - 1 - t)
    ]
    counts = jnp.concatenate([part[0] for part in parts], axis=0)
    lens = jnp.concatenate([part[1] for part in parts], axis=0)

    def heads(tt, squares):
        out = two_heads(counts, lens, table_of(tt, tab_own, tab_other))
        latent[tt] = out
        wide = out.astype(jnp.float32)
        for ref, core in ((own_ref, c), (other_ref, 1 - c)):
            for b in range(2):
                z = tt if b == 0 else 15 - tt
                for side in range(2):
                    first = pl.multiple_of(W_ROWS * (4 * (z % 2) + 2 * side + core), W_ROWS)
                    for n in range(3):
                        start = (3 * b + n) * W_ROWS
                        weight[z // 2, pl.ds(first, W_ROWS), n * HD : (n + 1) * HD] = ref[
                            2 * tt + side, start : start + W_ROWS, :
                        ]
        return squares + jnp.sum(wide * wide, axis=-1, keepdims=True)

    squares = lax.fori_loop(0, N_TP, heads, jnp.zeros((2 * P_DEV, 1), jnp.float32), unroll=4)
    inverse = lax.rsqrt(squares / 2048.0 + 1e-05)
    total = jnp.zeros((2 * P_DEV, 3 * HD), jnp.float32)
    for tt in range(N_TP):
        gain = gain_ref[:, tt * 256 : (tt + 1) * 256]
        normed = latent[tt].astype(jnp.float32) * inverse * gain
        total = total + jnp.dot(
            normed.astype(jnp.bfloat16), weight[tt], preferred_element_type=jnp.float32
        )
    total = total.astype(jnp.bfloat16)
    q_ref[...] = total[:, :HD]
    for tt in range(N_TP):
        kv_ref[tt] = total[:, HD:]


def latent_kernel(tab_own, tab_other, own_ref, other_ref, out_ref):
    z, yl, c, t = coordinates()
    counts, lens = byte_counts(4 * z + 2 * yl + c, c, own_ref, other_ref)
    out_ref[...] = two_heads(counts, lens, table_of(t, tab_own, tab_other))


def diagonal():
    shape = (P_DEV, P_DEV)
    return lax.broadcasted_iota(jnp.int32, shape, 0) == lax.broadcasted_iota(jnp.int32, shape, 1)


def as_row(column):
    return jnp.sum(jnp.where(diagonal(), column, 0.0), axis=0, keepdims=True)


def as_column(row):
    return jnp.sum(jnp.where(diagonal(), row, 0.0), axis=1, keepdims=True)


def attend_kernel(
    q_own, q_other, kv_own, kv_other, keep_ref, send_ref, scores, query, tops, norms, accs
):
    _, yl, c, t = coordinates()
    size = 2 * P_DEV
    for b in range(2):
        rows = slice(b * P_DEV, (b + 1) * P_DEV)
        query[b, :P_DEV] = q_own[rows]
        query[b, P_DEV:] = q_other[rows]
    tops[...] = jnp.full(tops.shape, NEG, jnp.float32)
    norms[...] = jnp.zeros(norms.shape, jnp.float32)
    accs[...] = jnp.zeros(accs.shape, jnp.float32)
    row = lax.broadcasted_iota(jnp.int32, (size, size), 0)
    col = lax.broadcasted_iota(jnp.int32, (size, size), 1)
    row_at = 256 * jnp.where(row < P_DEV, yl, 1 - yl) + P_DEV * c + row % P_DEV
    col_at = 256 * yl + P_DEV * jnp.where(col < P_DEV, c, 1 - c) + col % P_DEV
    hide = jnp.where(col_at <= row_at, 0.0, NEG)

    def unit(u):
        v = u - N_TP
        near = v <= t
        if u < N_TP:
            return 1, 0, u, False
        tt = jnp.where(near, v, v - 1)
        return jnp.where(near, 0, 1), jnp.where(near, 0, 1), tt, tt == t

    def part(ref, k_block, tt, lanes):
        if isinstance(k_block, int):
            return ref[tt, k_block * P_DEV : (k_block + 1) * P_DEV, lanes]
        return ref[tt, pl.ds(pl.multiple_of(k_block * P_DEV, P_DEV), P_DEV), lanes]

    def first(u):
        q_block, k_block, tt, crossed = unit(u)
        keys = jnp.concatenate(
            [part(ref, k_block, tt, slice(0, HD)) for ref in (kv_own, kv_other)], axis=0
        )
        s = nt_dot(query[q_block], keys) * SCALE
        if u >= N_TP:
            s = s + hide * jnp.where(crossed, 1.0, 0.0)
        scores[u] = s
        tops[q_block] = jnp.maximum(tops[q_block], jnp.maximum(s[:, :HD], s[:, HD:]))

    units = 2 * N_TP + 1
    for u in range(units):
        first(u)
    for b in range(2):
        tops[b] = jnp.broadcast_to(jnp.max(tops[b], axis=-1, keepdims=True), (size, HD))

    def second(u):
        q_block, k_block, tt, _ = unit(u)
        values = jnp.concatenate(
            [part(ref, k_block, tt, slice(HD, 2 * HD)) for ref in (kv_own, kv_other)], axis=0
        )
        top = tops[q_block]
        e = jnp.exp(scores[u] - jnp.concatenate([top, top], axis=1))
        norms[q_block] = norms[q_block] + (e[:, :HD] + e[:, HD:])
        accs[q_block] = accs[q_block] + jnp.dot(
            e.astype(jnp.bfloat16), values, preferred_element_type=jnp.float32
        )

    for u in range(units):
        second(u)
    for half, out in ((0, keep_ref), (1, send_ref)):
        rows = slice(half * P_DEV, (half + 1) * P_DEV)
        stats = [as_row(tops[b, rows, :1]) for b in range(2)]
        stats += [as_row(jnp.sum(norms[b, rows], axis=-1, keepdims=True)) for b in range(2)]
        for b in range(2):
            out[b * P_DEV : (b + 1) * P_DEV, :] = accs[b, rows]
        out[2 * P_DEV :, :] = jnp.concatenate(stats + [jnp.zeros((4, HD), jnp.float32)], axis=0)


def join_kernel(kept_ref, got_ref, same_ref, other_ref):
    z, _, _, _ = coordinates()
    odd = z % 2
    for b in range(2):
        rows = slice(b * P_DEV, (b + 1) * P_DEV)
        at = 2 * P_DEV + b
        top_a, top_b = (as_column(ref[at : at + 1, :]) for ref in (kept_ref, got_ref))
        sum_a, sum_b = (as_column(ref[at + 2 : at + 3, :]) for ref in (kept_ref, got_ref))
        top = jnp.maximum(top_a, top_b)
        a, g = jnp.exp(top_a - top), jnp.exp(top_b - top)
        mixed = (kept_ref[rows] * a + got_ref[rows] * g) / (sum_a * a + sum_b * g)
        mixed = mixed.astype(jnp.bfloat16)

        @pl.when(odd == b)
        def _():
            same_ref[...] = mixed

        @pl.when(odd != b)
        def _():
            other_ref[...] = mixed


def call(body, outs, scratch, flops, *args):
    vmem = pl.BlockSpec(memory_space=pltpu.VMEM)
    return pl.pallas_call(
        body,
        out_shape=[jax.ShapeDtypeStruct(shape, dtype) for shape, dtype in outs],
        in_specs=[vmem] * len(args),
        out_specs=[vmem] * len(outs),
        scratch_shapes=[pltpu.VMEM(shape, dtype) for shape, dtype in scratch],
        compiler_params=pltpu.CompilerParams(vmem_limit_bytes=VMEM),
        cost_estimate=pl.CostEstimate(flops=flops, bytes_accessed=4 << 20, transcendentals=1 << 20),
    )(*args)


BF, F32 = jnp.bfloat16, jnp.float32


def run_start(*args):
    outs = [((N_TP, VALUES, 6 * HD), BF)] + [((3 * W_ROWS + 16, HD), BF)] * 2
    return call(start_kernel, outs, [], 1 << 28, *args)


def run_encode(*args):
    outs = [((2 * P_DEV, HD), BF), ((N_TP, 2 * P_DEV, 2 * HD), BF)]
    scratch = [((N_TP, 256, 256), BF), ((N_TP, 256, 3 * HD), BF)]
    return call(encode_kernel, outs, scratch, 1 << 30, *args)


def run_latent(*args):
    return call(latent_kernel, [((P_DEV, 256), BF)], [], 1 << 26, *args)[0]


def run_attend(*args):
    block = (2, 2 * P_DEV, HD)
    scratch = [((2 * N_TP + 1, 2 * P_DEV, 2 * P_DEV), F32), (block, BF)] + [(block, F32)] * 3
    return call(attend_kernel, [((PART, HD), F32)] * 2, scratch, 1 << 30, *args)


def run_join(*args):
    return call(join_kernel, [((P_DEV, HD), BF)] * 2, [], 1 << 20, *args)


def on_device(
    byte_ids,
    patch_lens,
    byte_table,
    wq_cross,
    wk_cross,
    wv_cross,
    norm_gain,
    wq_latent,
    wk_latent,
    wv_latent,
):
    z = lax.axis_index("z")
    far, odd = z >= 8, z % 2 == 1
    swap = [(0, 1), (1, 0)]
    same, other = turns()

    tables, to_same, to_other = run_start(
        byte_ids.reshape(4, HD),
        patch_lens.reshape(1, HD),
        byte_table,
        wq_cross,
        wk_cross,
        wv_cross,
        wq_latent,
        wk_latent,
        wv_latent,
    )
    got_same = lax.ppermute(to_same, TURN, same)
    got_other = lax.ppermute(to_other, TURN, other)
    tab_own = lax.all_to_all(tables, TP, 0, 0)
    tab_other = lax.ppermute(tab_own, "c", swap)
    near = jnp.where(odd, got_other, got_same)
    away = jnp.where(odd, got_same, got_other)
    cut = 3 * W_ROWS
    message = jnp.concatenate([near[:cut], away[:cut], near[cut:], away[cut:]], axis=0)
    msg_own = to_all(message, PLANE, 16)
    msg_other = lax.ppermute(msg_own, "c", swap)

    q, kv = run_encode(tab_own, tab_other, msg_own, msg_other, norm_gain.reshape(1, 2048))
    q_other = lax.ppermute(q, "yl", swap)
    kv_own = lax.all_to_all(kv, TP, 0, 0)
    kv_other = lax.ppermute(kv_own, "c", swap)
    kept, sent = run_attend(q, q_other, kv_own, kv_other)
    head_same, head_other = run_join(kept, lax.ppermute(sent, "yl", swap))
    head_same = lax.ppermute(head_same, TURN, back(same))
    head_other = lax.ppermute(head_other, TURN, back(other))
    patch_latent = run_latent(tab_own, tab_other, msg_own, msg_other)
    latent_mixed = jnp.concatenate(
        [jnp.where(far, head_other, head_same), jnp.where(far, head_same, head_other)], axis=1
    )
    return (patch_latent, latent_mixed)


def solution(mesh):
    fine = Mesh(mesh.devices.reshape(16, 2, 2, 4, 2), ("z", "yl", "c", "x", "yh"))
    return jax.shard_map(
        on_device,
        mesh=fine,
        in_specs=(
            P(CTX),
            P(CTX),
            P(),
            P(None, TP),
            P(None, TP),
            P(None, TP),
            P(),
            P(CTX, TP),
            P(CTX, TP),
            P(CTX, TP),
        ),
        out_specs=(P(CTX, TP), P(CTX, TP)),
        check_vma=False,
    )
```

time: 166 us -> 152 us (0.916)
  the two profiles are of different devices: /device:TPU:102 before, /device:TPU:20 now
where the time goes in v3:
time: 152 us; the launch traced here: 151 us
  starting transfers between devices  61 us (40%)
  waiting for transfers between devices  39.5 us (26%)
  Pallas kernels  24.6 us (16%)
  blocking collectives  20 us (13%)
  local copies, waits for them, and re-layouts  4.38 us (3%)
    pallas_call x5, Pallas kernels, call(): pl.pallas_call(body, out_shape=[jax.ShapeDtypeStruct(shape, dtype) for sh...  24.6 us
    all_to_all x1, blocking collectives, on_device(): kv_own = lax.all_to_all(kv, TP, 0, 0)  20 us
    ppermute x1, starting transfers between devices, on_device(): head_other = lax.ppermute(head_other, TURN, back(other))  13.2 us
    ppermute x1, starting transfers between devices, on_device(): got_other = lax.ppermute(to_other, TURN, other)  11.9 us
    ppermute x1, waiting for transfers between devices, on_device(): head_same = lax.ppermute(head_same, TURN, back(same))  11.4 us
    ppermute x1, waiting for transfers between devices, on_device(): got_same = lax.ppermute(to_same, TURN, same)  9.67 us
    all_to_all x1, starting transfers between devices, on_device(): tab_own = lax.all_to_all(tables, TP, 0, 0)  9.3 us
    all_to_all x1, waiting for transfers between devices, to_all(): lax.all_to_all(jnp.broadcast_to(value[None], (count, *value.shape)), axes...  8.45 us
  transfers between devices with their start and end apart: 11, of which 6 were waited for; matrix products, arithmetic and copies ran while one was open for 0% of the time, Pallas kernels for 3%

profile of v3, /device:TPU:20, one launch (start us, length us, event | category | flops | bytes accessed | tf_op | source)
XLA Modules:
  0.0 151.1 jit_solution(1007466734992069742)
XLA Ops:
  0.6 3.2 %shard_map.113 = (bf16[8,128,768]{2,1,0:T(8,128)(2,1)}, bf16[112,128]{1,0:T(8,128)(2,1)}, bf16[112,128]{1,0:T(8,128)(2,1)}) custom-call(s32[4,128]{1,0:T(4,128)} %bitcast.4, s32[1,128]{1,0:T(1,128)} %bitcast.5, bf16[256,1024]{1,0:T(8,128)(2,1)} %table_ref.1, bf16[1024,256]{1,0:T(8,128)(2,1)} %wq.1, bf16[1024,256]{1,0:T(8,128)(2,1)} %wk.1, ...), custom_call_target="tpu_custom_call" | custom-call | flops 268435456 | bytes 4194304 | tf_op jit(solution)/shard_map/pallas_call | solution.py:296
  3.8 9.3 %all-to-all-start = ((bf16[8,128,768]{2,1,0:T(8,128)(2,1)}), bf16[8,128,768]{2,1,0:T(8,128)(2,1)S(1)}, u32[]{:S(2)}, u32[]{:S(2)}) async-start(bf16[8,128,768]{2,1,0:T(8,128)(2,1)} %get-tuple-element.11), calls=%async_computation | async-start | bytes 3145728 | tf_op jit(solution)/shard_map/all_to_all | solution.py:365
  13.1 11.9 %collective-permute-start.1 = (bf16[112,128]{1,0:T(8,128)(2,1)S(1)}, bf16[112,128]{1,0:T(8,128)(2,1)S(1)}, u32[]{:S(2)}, u32[]{:S(2)}) collective-permute-start(bf16[112,128]{1,0:T(8,128)(2,1)S(1)} %copy-done.9), channel_id=1, source_target_pairs={{0,32},{1,96},{2,160},{3,224},{4,288},{5,352},{6,416},{7,480},{32,... | collective-permute-start | bytes 86024 | tf_op jit(solution)/shard_map/ppermute | solution.py:364
  25.0 5.7 %collective-permute-start.2 = (bf16[112,128]{1,0:T(8,128)(2,1)S(1)}, bf16[112,128]{1,0:T(8,128)(2,1)S(1)}, u32[]{:S(2)}, u32[]{:S(2)}) collective-permute-start(bf16[112,128]{1,0:T(8,128)(2,1)S(1)} %copy-done.8), channel_id=1, source_target_pairs={{0,0},{1,64},{2,128},{3,192},{4,256},{5,320},{6,384},{7,448},{32,1... | collective-permute-start | bytes 86024 | tf_op jit(solution)/shard_map/ppermute | solution.py:363
  30.7 9.7 %collective-permute-done.2 = bf16[112,128]{1,0:T(8,128)(2,1)S(1)} collective-permute-done((bf16[112,128]{1,0:T(8,128)(2,1)S(1)}, bf16[112,128]{1,0:T(8,128)(2,1)S(1)}, u32[]{:S(2)}, u32[]{:S(2)}) %collective-permute-start.2) | collective-permute-done | bytes 28704 | tf_op jit(solution)/shard_map/ppermute | solution.py:363
  40.5 1.1 broadcast_in_dim.2
  41.6 7.2 %all-to-all-start.1 = ((bf16[16,224,128]{2,1,0:T(8,128)(2,1)}), bf16[16,224,128]{2,1,0:T(8,128)(2,1)S(1)}, u32[]{:S(2)}, u32[]{:S(2)}) async-start(bf16[16,224,128]{2,1,0:T(8,128)(2,1)} %broadcast_in_dim.2), calls=%async_computation.1 | async-start | bytes 1835008 | tf_op jit(solution)/shard_map/all_to_all | solution.py:46
  48.8 1.9 %collective-permute-start = (bf16[8,128,768]{2,1,0:T(8,128)(2,1)S(1)}, bf16[8,128,768]{2,1,0:T(8,128)(2,1)}, u32[]{:S(2)}, u32[]{:S(2)}) collective-permute-start(bf16[8,128,768]{2,1,0:T(8,128)(2,1)S(1)} %all-to-all-done.tab_own), channel_id=1, source_target_pairs={{0,8},{8,0},{1,9},{9,1},{2,10},{10,2},{3,11},{11,3},{4,12},{12,4},... | collective-permute-start | bytes 4718600 | tf_op jit(solution)/shard_map/ppermute | solution.py:366
  50.8 8.5 %all-to-all-done.1.own_ref = bf16[16,224,128]{2,1,0:T(8,128)(2,1)S(1)} async-done(((bf16[16,224,128]{2,1,0:T(8,128)(2,1)}), bf16[16,224,128]{2,1,0:T(8,128)(2,1)S(1)}, u32[]{:S(2)}, u32[]{:S(2)}) %all-to-all-start.1) | async-done | bytes 917536 | tf_op jit(solution)/shard_map/all_to_all | solution.py:46
  59.2 1.9 %collective-permute-start.3 = (bf16[16,224,128]{2,1,0:T(8,128)(2,1)S(1)}, bf16[16,224,128]{2,1,0:T(8,128)(2,1)S(1)}, u32[]{:S(2)}, u32[]{:S(2)}) collective-permute-start(bf16[16,224,128]{2,1,0:T(8,128)(2,1)S(1)} %all-to-all-done.1.own_ref), channel_id=1, source_target_pairs={{0,8},{8,0},{1,9},{9,1},{2,10},{10,2},{3,11},{11,3},{4,12},{12,4},... | collective-permute-start | bytes 2752520 | tf_op jit(solution)/shard_map/ppermute | solution.py:372
  61.1 2.4 %collective-permute-done.3.other_ref = bf16[16,224,128]{2,1,0:T(8,128)(2,1)S(1)} collective-permute-done((bf16[16,224,128]{2,1,0:T(8,128)(2,1)S(1)}, bf16[16,224,128]{2,1,0:T(8,128)(2,1)S(1)}, u32[]{:S(2)}, u32[]{:S(2)}) %collective-permute-start.3) | collective-permute-done | bytes 917536 | tf_op jit(solution)/shard_map/ppermute | solution.py:372
  64.5 9.7 %shard_map.115 = (bf16[256,128]{1,0:T(8,128)(2,1)}, bf16[8,256,256]{2,1,0:T(8,128)(2,1)}) custom-call(bf16[8,128,768]{2,1,0:T(8,128)(2,1)} %copy-done, bf16[8,128,768]{2,1,0:T(8,128)(2,1)} %collective-permute-done.tab_other, bf16[16,224,128]{2,1,0:T(8,128)(2,1)} %copy-done.1, bf16[16,224,128]{2,1,0:T(8,128)(2,1)} %copy-done.2, f32[1,2048]{1,0:T(1,128)} %bitcast.3), custom_call_target="tpu_custom_call" | custom-call | flops 1073741824 | bytes 4194304 | tf_op jit(solution)/shard_map/pallas_call | solution.py:296
  74.2 20.0 %all_to_all.15.kv_own = bf16[8,256,256]{2,1,0:T(8,128)(2,1)S(1)} all-to-all(bf16[8,256,256]{2,1,0:T(8,128)(2,1)} %get-tuple-element.15), channel_id=1, replica_groups=mesh['z'=16,'yl'=2,'c'=2,'x'=4,'yh'=2] {'x','yh'}, dimensions={0} | all-to-all | bytes 2097152 | tf_op jit(solution)/shard_map/all_to_all | solution.py:376
  94.2 1.9 %collective-permute-start.5 = (bf16[8,256,256]{2,1,0:T(8,128)(2,1)S(1)}, bf16[8,256,256]{2,1,0:T(8,128)(2,1)S(1)}, u32[]{:S(2)}, u32[]{:S(2)}) collective-permute-start(bf16[8,256,256]{2,1,0:T(8,128)(2,1)S(1)} %all_to_all.15.kv_own), channel_id=1, source_target_pairs={{0,8},{8,0},{1,9},{9,1},{2,10},{10,2},{3,11},{11,3},{4,12},{12,4},... | collective-permute-start | bytes 3145736 | tf_op jit(solution)/shard_map/ppermute | solution.py:377
  96.1 3.1 %collective-permute-start.4 = (bf16[256,128]{1,0:T(8,128)(2,1)S(1)}, bf16[256,128]{1,0:T(8,128)(2,1)S(1)}, u32[]{:S(2)}, u32[]{:S(2)}) collective-permute-start(bf16[256,128]{1,0:T(8,128)(2,1)S(1)} %copy-done.6), channel_id=1, source_target_pairs={{0,16},{16,0},{1,17},{17,1},{2,18},{18,2},{3,19},{19,3},{4,20},{20... | collective-permute-start | bytes 196616 | tf_op jit(solution)/shard_map/ppermute | solution.py:375
  99.2 3.3 %collective-permute-done.4.q_other = bf16[256,128]{1,0:T(8,128)(2,1)S(1)} collective-permute-done((bf16[256,128]{1,0:T(8,128)(2,1)S(1)}, bf16[256,128]{1,0:T(8,128)(2,1)S(1)}, u32[]{:S(2)}, u32[]{:S(2)}) %collective-permute-start.4) | collective-permute-done | bytes 65568 | tf_op jit(solution)/shard_map/ppermute | solution.py:375
  104.2 5.5 %shard_map.116 = (f32[264,128]{1,0:T(8,128)}, f32[264,128]{1,0:T(8,128)}) custom-call(bf16[256,128]{1,0:T(8,128)(2,1)} %get-tuple-element.14.q_own, bf16[256,128]{1,0:T(8,128)(2,1)} %copy-done.7, bf16[8,256,256]{2,1,0:T(8,128)(2,1)} %copy-done.3, bf16[8,256,256]{2,1,0:T(8,128)(2,1)} %copy-done.4), custom_call_target="tpu_custom_call" | custom-call | flops 1073741824 | bytes 4194304 | tf_op jit(solution)/shard_map/pallas_call | solution.py:296
  109.7 3.0 %collective-permute-start.6 = (f32[264,128]{1,0:T(8,128)}, f32[264,128]{1,0:T(8,128)S(1)}, u32[]{:S(2)}, u32[]{:S(2)}) collective-permute-start(f32[264,128]{1,0:T(8,128)} %get-tuple-element.17), channel_id=1, source_target_pairs={{0,16},{16,0},{1,17},{17,1},{2,18},{18,2},{3,19},{19,3},{4,20},{20... | collective-permute-start | bytes 405512 | tf_op jit(solution)/shard_map/ppermute | solution.py:379
  112.7 4.2 %collective-permute-done.6.got_ref = f32[264,128]{1,0:T(8,128)S(1)} collective-permute-done((f32[264,128]{1,0:T(8,128)}, f32[264,128]{1,0:T(8,128)S(1)}, u32[]{:S(2)}, u32[]{:S(2)}) %collective-permute-start.6) | collective-permute-done | bytes 135200 | tf_op jit(solution)/shard_map/ppermute | solution.py:379
  117.6 1.9 %shard_map.117 = (bf16[128,128]{1,0:T(8,128)(2,1)}, bf16[128,128]{1,0:T(8,128)(2,1)}) custom-call(f32[264,128]{1,0:T(8,128)} %get-tuple-element.16.kept_ref, f32[264,128]{1,0:T(8,128)} %copy-done.5), custom_call_target="tpu_custom_call" | custom-call | flops 1048576 | bytes 4194304 | tf_op jit(solution)/shard_map/pallas_call | solution.py:296
  119.5 13.2 %collective-permute-start.7 = (bf16[128,128]{1,0:T(8,128)(2,1)}, bf16[128,128]{1,0:T(8,128)(2,1)S(1)}, u32[]{:S(2)}, u32[]{:S(2)}) collective-permute-start(bf16[128,128]{1,0:T(8,128)(2,1)} %get-tuple-element.18), channel_id=1, source_target_pairs={{32,0},{96,1},{160,2},{224,3},{288,4},{352,5},{416,6},{480,7},{33,... | collective-permute-start | bytes 98312 | tf_op jit(solution)/shard_map/ppermute | solution.py:381
  132.7 1.9 %collective-permute-start.8 = (bf16[128,128]{1,0:T(8,128)(2,1)}, bf16[128,128]{1,0:T(8,128)(2,1)S(1)}, u32[]{:S(2)}, u32[]{:S(2)}) collective-permute-start(bf16[128,128]{1,0:T(8,128)(2,1)} %get-tuple-element.19), channel_id=1, source_target_pairs={{0,0},{64,1},{128,2},{192,3},{256,4},{320,5},{384,6},{448,7},{1,32... | collective-permute-start | bytes 98312 | tf_op jit(solution)/shard_map/ppermute | solution.py:380
  134.6 4.4 %shard_map.114 = bf16[128,256]{1,0:T(8,128)(2,1)} custom-call(bf16[8,128,768]{2,1,0:T(8,128)(2,1)} %copy-done, bf16[8,128,768]{2,1,0:T(8,128)(2,1)} %collective-permute-done.tab_other, bf16[16,224,128]{2,1,0:T(8,128)(2,1)} %copy-done.1, bf16[16,224,128]{2,1,0:T(8,128)(2,1)} %copy-done.2), custom_call_target="tpu_custom_call" | custom-call | flops 67108864 | bytes 4194304 | tf_op jit(solution)/shard_map/pallas_call | solution.py:296
  139.0 11.4 %collective-permute-done.8 = bf16[128,128]{1,0:T(8,128)(2,1)S(1)} collective-permute-done((bf16[128,128]{1,0:T(8,128)(2,1)}, bf16[128,128]{1,0:T(8,128)(2,1)S(1)}, u32[]{:S(2)}, u32[]{:S(2)}) %collective-permute-start.8) | collective-permute-done | bytes 32800 | tf_op jit(solution)/shard_map/ppermute | solution.py:380
  (33 shorter events, 3.9 us)
Async XLA Ops:
  3.8 9.3 %copy-start.9 = (bf16[112,128]{1,0:T(8,128)(2,1)S(1)}, bf16[112,128]{1,0:T(8,128)(2,1)}, u32[]{:S(2)}) copy-start(bf16[112,128]{1,0:T(8,128)(2,1)} %get-tuple-element.12) | copy-start | bytes 86020
  3.8 21.2 %copy-start.8 = (bf16[112,128]{1,0:T(8,128)(2,1)S(1)}, bf16[112,128]{1,0:T(8,128)(2,1)}, u32[]{:S(2)}) copy-start(bf16[112,128]{1,0:T(8,128)(2,1)} %get-tuple-element.13) | copy-start | bytes 86020
  3.8 36.6 %all-to-all-start = ((bf16[8,128,768]{2,1,0:T(8,128)(2,1)}), bf16[8,128,768]{2,1,0:T(8,128)(2,1)S(1)}, u32[]{:S(2)}, u32[]{:S(2)}) async-start(bf16[8,128,768]{2,1,0:T(8,128)(2,1)} %get-tuple-element.11), calls=%async_computation | async-start | bytes 3145728 | tf_op jit(solution)/shard_map/all_to_all | solution.py:365
  13.1 17.6 %collective-permute-start.1 = (bf16[112,128]{1,0:T(8,128)(2,1)S(1)}, bf16[112,128]{1,0:T(8,128)(2,1)S(1)}, u32[]{:S(2)}, u32[]{:S(2)}) collective-permute-start(bf16[112,128]{1,0:T(8,128)(2,1)S(1)} %copy-done.9), channel_id=1, source_target_pairs={{0,32},{1,96},{2,160},{3,224},{4,288},{5,352},{6,416},{7,480},{32,... | collective-permute-start | bytes 86024 | tf_op jit(solution)/shard_map/ppermute | solution.py:364
  25.0 15.4 %collective-permute-start.2 = (bf16[112,128]{1,0:T(8,128)(2,1)S(1)}, bf16[112,128]{1,0:T(8,128)(2,1)S(1)}, u32[]{:S(2)}, u32[]{:S(2)}) collective-permute-start(bf16[112,128]{1,0:T(8,128)(2,1)S(1)} %copy-done.8), channel_id=1, source_target_pairs={{0,0},{1,64},{2,128},{3,192},{4,256},{5,320},{6,384},{7,448},{32,1... | collective-permute-start | bytes 86024 | tf_op jit(solution)/shard_map/ppermute | solution.py:363
  40.5 23.1 %copy-start = (bf16[8,128,768]{2,1,0:T(8,128)(2,1)}, bf16[8,128,768]{2,1,0:T(8,128)(2,1)S(1)}, u32[]{:S(2)}) copy-start(bf16[8,128,768]{2,1,0:T(8,128)(2,1)S(1)} %all-to-all-done.tab_own) | copy-start | bytes 4718596
  41.6 17.6 %all-to-all-start.1 = ((bf16[16,224,128]{2,1,0:T(8,128)(2,1)}), bf16[16,224,128]{2,1,0:T(8,128)(2,1)S(1)}, u32[]{:S(2)}, u32[]{:S(2)}) async-start(bf16[16,224,128]{2,1,0:T(8,128)(2,1)} %broadcast_in_dim.2), calls=%async_computation.1 | async-start | bytes 1835008 | tf_op jit(solution)/shard_map/all_to_all | solution.py:46
  48.8 14.7 %collective-permute-start = (bf16[8,128,768]{2,1,0:T(8,128)(2,1)S(1)}, bf16[8,128,768]{2,1,0:T(8,128)(2,1)}, u32[]{:S(2)}, u32[]{:S(2)}) collective-permute-start(bf16[8,128,768]{2,1,0:T(8,128)(2,1)S(1)} %all-to-all-done.tab_own), channel_id=1, source_target_pairs={{0,8},{8,0},{1,9},{9,1},{2,10},{10,2},{3,11},{11,3},{4,12},{12,4},... | collective-permute-start | bytes 4718600 | tf_op jit(solution)/shard_map/ppermute | solution.py:366
  59.2 4.4 %copy-start.1 = (bf16[16,224,128]{2,1,0:T(8,128)(2,1)}, bf16[16,224,128]{2,1,0:T(8,128)(2,1)S(1)}, u32[]{:S(2)}) copy-start(bf16[16,224,128]{2,1,0:T(8,128)(2,1)S(1)} %all-to-all-done.1.own_ref) | copy-start | bytes 2752516
  59.2 4.4 %collective-permute-start.3 = (bf16[16,224,128]{2,1,0:T(8,128)(2,1)S(1)}, bf16[16,224,128]{2,1,0:T(8,128)(2,1)S(1)}, u32[]{:S(2)}, u32[]{:S(2)}) collective-permute-start(bf16[16,224,128]{2,1,0:T(8,128)(2,1)S(1)} %all-to-all-done.1.own_ref), channel_id=1, source_target_pairs={{0,8},{8,0},{1,9},{9,1},{2,10},{10,2},{3,11},{11,3},{4,12},{12,4},... | collective-permute-start | bytes 2752520 | tf_op jit(solution)/shard_map/ppermute | solution.py:372
  63.6 0.9 copy-start.2
  74.2 22.0 %copy-start.6 = (bf16[256,128]{1,0:T(8,128)(2,1)S(1)}, bf16[256,128]{1,0:T(8,128)(2,1)}, u32[]{:S(2)}) copy-start(bf16[256,128]{1,0:T(8,128)(2,1)} %get-tuple-element.14.q_own) | copy-start | bytes 196612
  94.2 8.3 %copy-start.3 = (bf16[8,256,256]{2,1,0:T(8,128)(2,1)}, bf16[8,256,256]{2,1,0:T(8,128)(2,1)S(1)}, u32[]{:S(2)}) copy-start(bf16[8,256,256]{2,1,0:T(8,128)(2,1)S(1)} %all_to_all.15.kv_own) | copy-start | bytes 3145732
  94.2 8.3 %collective-permute-start.5 = (bf16[8,256,256]{2,1,0:T(8,128)(2,1)S(1)}, bf16[8,256,256]{2,1,0:T(8,128)(2,1)S(1)}, u32[]{:S(2)}, u32[]{:S(2)}) collective-permute-start(bf16[8,256,256]{2,1,0:T(8,128)(2,1)S(1)} %all_to_all.15.kv_own), channel_id=1, source_target_pairs={{0,8},{8,0},{1,9},{9,1},{2,10},{10,2},{3,11},{11,3},{4,12},{12,4},... | collective-permute-start | bytes 3145736 | tf_op jit(solution)/shard_map/ppermute | solution.py:377
  96.1 6.4 %collective-permute-start.4 = (bf16[256,128]{1,0:T(8,128)(2,1)S(1)}, bf16[256,128]{1,0:T(8,128)(2,1)S(1)}, u32[]{:S(2)}, u32[]{:S(2)}) collective-permute-start(bf16[256,128]{1,0:T(8,128)(2,1)S(1)} %copy-done.6), channel_id=1, source_target_pairs={{0,16},{16,0},{1,17},{17,1},{2,18},{18,2},{3,19},{19,3},{4,20},{20... | collective-permute-start | bytes 196616 | tf_op jit(solution)/shard_map/ppermute | solution.py:375
  102.5 0.6 copy-start.7
  103.2 1.0 copy-start.4
  109.7 7.3 %collective-permute-start.6 = (f32[264,128]{1,0:T(8,128)}, f32[264,128]{1,0:T(8,128)S(1)}, u32[]{:S(2)}, u32[]{:S(2)}) collective-permute-start(f32[264,128]{1,0:T(8,128)} %get-tuple-element.17), channel_id=1, source_target_pairs={{0,16},{16,0},{1,17},{17,1},{2,18},{18,2},{3,19},{19,3},{4,20},{20... | collective-permute-start | bytes 405512 | tf_op jit(solution)/shard_map/ppermute | solution.py:379
  117.0 0.6 copy-start.5
  119.5 19.5 %collective-permute-start.7 = (bf16[128,128]{1,0:T(8,128)(2,1)}, bf16[128,128]{1,0:T(8,128)(2,1)S(1)}, u32[]{:S(2)}, u32[]{:S(2)}) collective-permute-start(bf16[128,128]{1,0:T(8,128)(2,1)} %get-tuple-element.18), channel_id=1, source_target_pairs={{32,0},{96,1},{160,2},{224,3},{288,4},{352,5},{416,6},{480,7},{33,... | collective-permute-start | bytes 98312 | tf_op jit(solution)/shard_map/ppermute | solution.py:381
  132.7 17.7 %collective-permute-start.8 = (bf16[128,128]{1,0:T(8,128)(2,1)}, bf16[128,128]{1,0:T(8,128)(2,1)S(1)}, u32[]{:S(2)}, u32[]{:S(2)}) collective-permute-start(bf16[128,128]{1,0:T(8,128)(2,1)} %get-tuple-element.19), channel_id=1, source_target_pairs={{0,0},{64,1},{128,2},{192,3},{256,4},{320,5},{384,6},{448,7},{1,32... | collective-permute-start | bytes 98312 | tf_op jit(solution)/shard_map/ppermute | solution.py:380

commit v4 on v3

--- a/solution.py
+++ b/solution.py
@@ -19,22 +19,31 @@
 VALUES = 128
 ROWS = 2 * 3 * W_ROWS
 MSG = ROWS + 2 * 16
-PART = 2 * P_DEV + 8
-VMEM = 56 * 1024 * 1024
+PART = P_DEV + 8
+VMEM = 20 * 1024 * 1024
 
 CTX = ("z", "yl", "c")
 TP = ("x", "yh")
 PLANE = ("x", "yh", "yl")
-TURN = ("z", "x", "yh")
+TURN = ("z", "yl", "x", "yh")
+
+
+def turned(index, yl):
+    return index + yl * (N_TP - 1 - 2 * index)
+
+
+def flat(z, yl, t):
+    return (z * 2 + yl) * N_TP + t
 
 
 def turns():
     same, other = [], []
     for z in range(16):
-        for t in range(N_TP):
-            far, low = z // 8, min(z, 15 - z)
-            same.append((z * N_TP + t, (2 * t + far) * N_TP + low))
-            other.append((z * N_TP + t, (2 * t + 1 - far) * N_TP + low))
+        for yl in range(2):
+            for t in range(N_TP):
+                tt = turned(z // 2, yl)
+                same.append((flat(z, yl, t), flat(2 * t + z % 2, yl, tt)))
+                other.append((flat(z, yl, t), flat(2 * t + 1 - z % 2, yl, tt)))
     return same, other
 
 
@@ -56,7 +65,7 @@
         for b in range(2):
             tiles = ref[:, ROWS + 16 * b : ROWS + 16 * (b + 1), :].astype(jnp.float32)
             unit, row = (lax.broadcasted_iota(jnp.int32, tiles.shape, i) for i in range(2))
-            z = unit // 2 if b == 0 else 15 - unit // 2
+            z = 2 * turned(unit // 2, unit % 2) + b
             place = 4 * z + 2 * (unit % 2) + core
             total = total + jnp.sum(jnp.where((row == 4) & (place < d), tiles, 0.0))
     return total
@@ -66,9 +75,9 @@
     follow = jnp.where(d < N_CTX - 1, d + 1, d - 1)
 
     def tile(ref, place):
-        z = place // 4
-        unit = 2 * jnp.minimum(z, 15 - z) + (place // 2) % 2
-        first = pl.multiple_of(ROWS + 16 * (z // 8), 16)
+        z, yl = place // 4, (place // 2) % 2
+        unit = 2 * turned(z // 2, yl) + yl
+        first = pl.multiple_of(ROWS + 16 * (z % 2), 16)
         return ref[unit, pl.ds(first, 16), :].astype(jnp.float32)
 
     here, beyond = tile(own_ref, d), tile(other_ref, follow)
@@ -131,8 +140,8 @@
     ints = jnp.concatenate(
         [ids_ref[...], lens_ref[...], jnp.zeros((11, HD), jnp.int32)], axis=0
     ).astype(jnp.float32)
-    far = z // 8
-    for out, a in ((same_ref, far), (other_ref, 1 - far)):
+    odd = z % 2
+    for out, a in ((same_ref, odd), (other_ref, 1 - odd)):
         for i, ref in enumerate((lq, lk, lv)):
             out[i * W_ROWS : (i + 1) * W_ROWS, :] = ref[:, pl.ds(pl.multiple_of(a * HD, HD), HD)]
         out[3 * W_ROWS :, :] = ints.astype(jnp.bfloat16)
@@ -142,8 +151,9 @@
     tab_own, tab_other, own_ref, other_ref, gain_ref, q_ref, kv_ref, latent, weight
 ):
     _, yl, c, t = coordinates()
+    first_z = 2 * turned(t, yl)
     parts = [
-        byte_counts(4 * z + 2 * yl + c, c, own_ref, other_ref) for z in (t, 2 * N_TP - 1 - t)
+        byte_counts(4 * z + 2 * yl + c, c, own_ref, other_ref) for z in (first_z, first_z + 1)
     ]
     counts = jnp.concatenate([part[0] for part in parts], axis=0)
     lens = jnp.concatenate([part[1] for part in parts], axis=0)
@@ -154,12 +164,11 @@
         wide = out.astype(jnp.float32)
         for ref, core in ((own_ref, c), (other_ref, 1 - c)):
             for b in range(2):
-                z = tt if b == 0 else 15 - tt
                 for side in range(2):
-                    first = pl.multiple_of(W_ROWS * (4 * (z % 2) + 2 * side + core), W_ROWS)
+                    first = pl.multiple_of(W_ROWS * (4 * b + 2 * side + core), W_ROWS)
                     for n in range(3):
                         start = (3 * b + n) * W_ROWS
-                        weight[z // 2, pl.ds(first, W_ROWS), n * HD : (n + 1) * HD] = ref[
+                        weight[turned(tt, side), pl.ds(first, W_ROWS), n * HD : (n + 1) * HD] = ref[
                             2 * tt + side, start : start + W_ROWS, :
                         ]
         return squares + jnp.sum(wide * wide, axis=-1, keepdims=True)
@@ -199,99 +208,98 @@
 
 
 def attend_kernel(
-    q_own, q_other, kv_own, kv_other, keep_ref, send_ref, scores, query, tops, norms, accs
+    q_own,
+    q_other,
+    kv_own,
+    kv_other,
+    keep_ref,
+    to_yl_ref,
+    to_z_ref,
+    to_both_ref,
+    scores,
+    query,
+    tops,
+    norms,
+    accs,
 ):
-    _, yl, c, t = coordinates()
+    z, yl, c, t = coordinates()
     size = 2 * P_DEV
-    for b in range(2):
-        rows = slice(b * P_DEV, (b + 1) * P_DEV)
-        query[b, :P_DEV] = q_own[rows]
-        query[b, P_DEV:] = q_other[rows]
+    query[yl] = q_own[...]
+    query[1 - yl] = q_other[...]
     tops[...] = jnp.full(tops.shape, NEG, jnp.float32)
     norms[...] = jnp.zeros(norms.shape, jnp.float32)
     accs[...] = jnp.zeros(accs.shape, jnp.float32)
     row = lax.broadcasted_iota(jnp.int32, (size, size), 0)
     col = lax.broadcasted_iota(jnp.int32, (size, size), 1)
-    row_at = 256 * jnp.where(row < P_DEV, yl, 1 - yl) + P_DEV * c + row % P_DEV
-    col_at = 256 * yl + P_DEV * jnp.where(col < P_DEV, c, 1 - c) + col % P_DEV
-    hide = jnp.where(col_at <= row_at, 0.0, NEG)
+    behind = 512 * (row // P_DEV - col // P_DEV) + row % P_DEV - col % P_DEV
+
+    def hide(q_yl, core):
+        return jnp.where(behind + 256 * (q_yl - yl) + P_DEV * (c - core) >= 0, 0.0, NEG)
+
+    units = N_TP + 1
 
     def unit(u):
-        v = u - N_TP
-        near = v <= t
-        if u < N_TP:
-            return 1, 0, u, False
-        tt = jnp.where(near, v, v - 1)
-        return jnp.where(near, 0, 1), jnp.where(near, 0, 1), tt, tt == t
-
-    def part(ref, k_block, tt, lanes):
-        if isinstance(k_block, int):
-            return ref[tt, k_block * P_DEV : (k_block + 1) * P_DEV, lanes]
-        return ref[tt, pl.ds(pl.multiple_of(k_block * P_DEV, P_DEV), P_DEV), lanes]
-
-    def first(u):
-        q_block, k_block, tt, crossed = unit(u)
-        keys = jnp.concatenate(
-            [part(ref, k_block, tt, slice(0, HD)) for ref in (kv_own, kv_other)], axis=0
-        )
-        s = nt_dot(query[q_block], keys) * SCALE
-        if u >= N_TP:
-            s = s + hide * jnp.where(crossed, 1.0, 0.0)
-        scores[u] = s
-        tops[q_block] = jnp.maximum(tops[q_block], jnp.maximum(s[:, :HD], s[:, HD:]))
-
-    units = 2 * N_TP + 1
+        if u == N_TP:
+            return 1, turned(N_TP - 1 - t, yl)
+        first = u <= t
+        return jnp.where(first, 0, 1), turned(jnp.where(first, u, u - t - 1), yl)
+
+    sides = ((kv_own, c), (kv_other, 1 - c))
     for u in range(units):
-        first(u)
+        q_yl, tt = unit(u)
+        best = tops[q_yl]
+        for i, (ref, core) in enumerate(sides):
+            s = nt_dot(query[q_yl], ref[tt, :, :HD]) * SCALE
+            if u == N_TP:
+                s = s + hide(1, core)
+            else:
+                s = s + hide(0, core) * jnp.where(u == t, 1.0, 0.0)
+            scores[u, i] = s
+            best = jnp.maximum(best, jnp.maximum(s[:, :HD], s[:, HD:]))
+        tops[q_yl] = best
     for b in range(2):
         tops[b] = jnp.broadcast_to(jnp.max(tops[b], axis=-1, keepdims=True), (size, HD))
-
-    def second(u):
-        q_block, k_block, tt, _ = unit(u)
-        values = jnp.concatenate(
-            [part(ref, k_block, tt, slice(HD, 2 * HD)) for ref in (kv_own, kv_other)], axis=0
-        )
-        top = tops[q_block]
-        e = jnp.exp(scores[u] - jnp.concatenate([top, top], axis=1))
-        norms[q_block] = norms[q_block] + (e[:, :HD] + e[:, HD:])
-        accs[q_block] = accs[q_block] + jnp.dot(
-            e.astype(jnp.bfloat16), values, preferred_element_type=jnp.float32
-        )
-
     for u in range(units):
-        second(u)
-    for half, out in ((0, keep_ref), (1, send_ref)):
-        rows = slice(half * P_DEV, (half + 1) * P_DEV)
-        stats = [as_row(tops[b, rows, :1]) for b in range(2)]
-        stats += [as_row(jnp.sum(norms[b, rows], axis=-1, keepdims=True)) for b in range(2)]
-        for b in range(2):
-            out[b * P_DEV : (b + 1) * P_DEV, :] = accs[b, rows]
-        out[2 * P_DEV :, :] = jnp.concatenate(stats + [jnp.zeros((4, HD), jnp.float32)], axis=0)
-
-
-def join_kernel(kept_ref, got_ref, same_ref, other_ref):
+        q_yl, tt = unit(u)
+        top = tops[q_yl]
+        top = jnp.concatenate([top, top], axis=1)
+        norm, acc = norms[q_yl], accs[q_yl]
+        for i, (ref, _) in enumerate(sides):
+            e = jnp.exp(scores[u, i] - top)
+            norm = norm + (e[:, :HD] + e[:, HD:])
+            acc = acc + jnp.dot(
+                e.astype(jnp.bfloat16), ref[tt, :, HD:], preferred_element_type=jnp.float32
+            )
+        norms[q_yl] = norm
+        accs[q_yl] = acc
+    odd = z % 2
+    for out, q_yl, b in (
+        (keep_ref, yl, odd),
+        (to_yl_ref, 1 - yl, odd),
+        (to_z_ref, yl, 1 - odd),
+        (to_both_ref, 1 - yl, 1 - odd),
+    ):
+        rows = pl.ds(pl.multiple_of(b * P_DEV, P_DEV), P_DEV)
+        out[:P_DEV, :] = accs[q_yl, rows, :]
+        total = jnp.sum(norms[q_yl, rows, :], axis=-1, keepdims=True)
+        stats = [as_row(tops[q_yl, rows, :][:, :1]), as_row(total), jnp.zeros((6, HD), jnp.float32)]
+        out[P_DEV:, :] = jnp.concatenate(stats, axis=0)
+
+
+def join_kernel(kept, got_yl, got_z, got_both, out_ref):
     z, _, _, _ = coordinates()
     odd = z % 2
-    for b in range(2):
-        rows = slice(b * P_DEV, (b + 1) * P_DEV)
-        at = 2 * P_DEV + b
-        top_a, top_b = (as_column(ref[at : at + 1, :]) for ref in (kept_ref, got_ref))
-        sum_a, sum_b = (as_column(ref[at + 2 : at + 3, :]) for ref in (kept_ref, got_ref))
-        top = jnp.maximum(top_a, top_b)
-        a, g = jnp.exp(top_a - top), jnp.exp(top_b - top)
-        mixed = (kept_ref[rows] * a + got_ref[rows] * g) / (sum_a * a + sum_b * g)
-        mixed = mixed.astype(jnp.bfloat16)
-
-        @pl.when(odd == b)
-        def _():
-            same_ref[...] = mixed
-
-        @pl.when(odd != b)
-        def _():
-            other_ref[...] = mixed
-
-
-def call(body, outs, scratch, flops, *args):
+    for a, pair in ((odd, (kept, got_yl)), (1 - odd, (got_z, got_both))):
+        tops = [as_column(ref[P_DEV : P_DEV + 1, :]) for ref in pair]
+        sums = [as_column(ref[P_DEV + 1 : P_DEV + 2, :]) for ref in pair]
+        top = jnp.maximum(*tops)
+        scale = [jnp.exp(part - top) for part in tops]
+        mixed = pair[0][:P_DEV, :] * scale[0] + pair[1][:P_DEV, :] * scale[1]
+        mixed = mixed / (sums[0] * scale[0] + sums[1] * scale[1])
+        out_ref[:, pl.ds(pl.multiple_of(a * HD, HD), HD)] = mixed.astype(jnp.bfloat16)
+
+
+def call(body, outs, scratch, flops, *args, limit=VMEM):
     vmem = pl.BlockSpec(memory_space=pltpu.VMEM)
     return pl.pallas_call(
         body,
@@ -299,7 +307,7 @@
         in_specs=[vmem] * len(args),
         out_specs=[vmem] * len(outs),
         scratch_shapes=[pltpu.VMEM(shape, dtype) for shape, dtype in scratch],
-        compiler_params=pltpu.CompilerParams(vmem_limit_bytes=VMEM),
+        compiler_params=pltpu.CompilerParams(vmem_limit_bytes=limit),
         cost_estimate=pl.CostEstimate(flops=flops, bytes_accessed=4 << 20, transcendentals=1 << 20),
     )(*args)
 
@@ -309,7 +317,7 @@
 
 def run_start(*args):
     outs = [((N_TP, VALUES, 6 * HD), BF)] + [((3 * W_ROWS + 16, HD), BF)] * 2
-    return call(start_kernel, outs, [], 1 << 28, *args)
+    return call(start_kernel, outs, [], 1 << 28, *args, limit=56 << 20)
 
 
 def run_encode(*args):
@@ -323,13 +331,14 @@
 
 
 def run_attend(*args):
-    block = (2, 2 * P_DEV, HD)
-    scratch = [((2 * N_TP + 1, 2 * P_DEV, 2 * P_DEV), F32), (block, BF)] + [(block, F32)] * 3
-    return call(attend_kernel, [((PART, HD), F32)] * 2, scratch, 1 << 30, *args)
+    size = 2 * P_DEV
+    block = (2, size, HD)
+    scratch = [((N_TP + 1, 2, size, size), F32), (block, BF)] + [(block, F32)] * 3
+    return call(attend_kernel, [((PART, HD), F32)] * 4, scratch, 1 << 30, *args)
 
 
 def run_join(*args):
-    return call(join_kernel, [((P_DEV, HD), BF)] * 2, [], 1 << 20, *args)
+    return call(join_kernel, [((P_DEV, 2 * HD), BF)], [], 1 << 20, *args)[0]
 
 
 def on_device(
@@ -345,7 +354,7 @@
     wv_latent,
 ):
     z = lax.axis_index("z")
-    far, odd = z >= 8, z % 2 == 1
+    odd = z % 2 == 1
     swap = [(0, 1), (1, 0)]
     same, other = turns()
 
@@ -374,15 +383,15 @@
     q, kv = run_encode(tab_own, tab_other, msg_own, msg_other, norm_gain.reshape(1, 2048))
     q_other = lax.ppermute(q, "yl", swap)
     kv_own = lax.all_to_all(kv, TP, 0, 0)
+    kv_own, q_other = lax.optimization_barrier((kv_own, q_other))
     kv_other = lax.ppermute(kv_own, "c", swap)
-    kept, sent = run_attend(q, q_other, kv_own, kv_other)
-    head_same, head_other = run_join(kept, lax.ppermute(sent, "yl", swap))
-    head_same = lax.ppermute(head_same, TURN, back(same))
-    head_other = lax.ppermute(head_other, TURN, back(other))
+    kept, to_yl, to_z, to_both = run_attend(q, q_other, kv_own, kv_other)
+    got_both = lax.ppermute(to_both, ("z", "yl"), [(i, i ^ 3) for i in range(32)])
+    got_z = lax.ppermute(to_z, "z", [(i, i ^ 1) for i in range(16)])
+    got_yl = lax.ppermute(to_yl, "yl", swap)
+    mixed = run_join(kept, got_yl, got_z, got_both)
+    latent_mixed = lax.ppermute(mixed, TURN, back(same))
     patch_latent = run_latent(tab_own, tab_other, msg_own, msg_other)
-    latent_mixed = jnp.concatenate(
-        [jnp.where(far, head_other, head_same), jnp.where(far, head_same, head_other)], axis=1
-    )
     return (patch_latent, latent_mixed)
 
 

time: 152 us -> 140 us (0.921)
  the two profiles are of different devices: /device:TPU:20 before, /device:TPU:10 now
where the time goes in v4:
time: 140 us
  starting transfers between devices  72.7 us (52%)
  waiting for transfers between devices  45.1 us (32%)
  Pallas kernels  18.4 us (13%)
  local copies, waits for them, and re-layouts  2.69 us (2%)
    pallas_call x5, Pallas kernels, call(): pl.pallas_call(body, out_shape=[jax.ShapeDtypeStruct(shape, dtype) for sh...  18.4 us
    ppermute x1, starting transfers between devices, on_device(): got_other = lax.ppermute(to_other, TURN, other)  14.3 us
    ppermute x1, waiting for transfers between devices, on_device(): q_other = lax.ppermute(q, 'yl', swap)  11.4 us
    all_to_all x1, starting transfers between devices, to_all(): lax.all_to_all(jnp.broadcast_to(value[None], (count, *value.shape)), axes...  11.4 us
    all_to_all x1, waiting for transfers between devices, to_all(): lax.all_to_all(jnp.broadcast_to(value[None], (count, *value.shape)), axes...  8.97 us
    ppermute x1, starting transfers between devices, on_device(): got_same = lax.ppermute(to_same, TURN, same)  8.53 us
    ppermute x1, waiting for transfers between devices, on_device(): latent_mixed = lax.ppermute(mixed, TURN, back(same))  8.13 us
    ppermute x1, starting transfers between devices, on_device(): latent_mixed = lax.ppermute(mixed, TURN, back(same))  6.9 us
  transfers between devices with their start and end apart: 13, of which 9 were waited for; matrix products, arithmetic and copies ran while one was open for 0% of the time, Pallas kernels for 2%

profile of v4, /device:TPU:10, one launch (start us, length us, event | category | flops | bytes accessed | tf_op | source)
XLA Modules:
  0.0 139.8 jit_solution(15185635641216087971)
XLA Ops:
  0.6 3.2 %shard_map.113 = (bf16[8,128,768]{2,1,0:T(8,128)(2,1)}, bf16[112,128]{1,0:T(8,128)(2,1)}, bf16[112,128]{1,0:T(8,128)(2,1)}) custom-call(s32[4,128]{1,0:T(4,128)} %bitcast.4, s32[1,128]{1,0:T(1,128)} %bitcast.5, bf16[256,1024]{1,0:T(8,128)(2,1)} %table_ref.1, bf16[1024,256]{1,0:T(8,128)(2,1)} %wq.1, bf16[1024,256]{1,0:T(8,128)(2,1)} %wk.1, ...), custom_call_target="tpu_custom_call" | custom-call | flops 268435456 | bytes 4194304 | tf_op jit(solution)/shard_map/pallas_call | solution.py:304
  3.8 6.7 %all-to-all-start = ((bf16[8,128,768]{2,1,0:T(8,128)(2,1)}), bf16[8,128,768]{2,1,0:T(8,128)(2,1)S(1)}, u32[]{:S(2)}, u32[]{:S(2)}) async-start(bf16[8,128,768]{2,1,0:T(8,128)(2,1)} %get-tuple-element.13), calls=%async_computation | async-start | bytes 3145728 | tf_op jit(solution)/shard_map/all_to_all | solution.py:374
  10.5 14.3 %collective-permute-start.1 = (bf16[112,128]{1,0:T(8,128)(2,1)S(1)}, bf16[112,128]{1,0:T(8,128)(2,1)S(1)}, u32[]{:S(2)}, u32[]{:S(2)}) collective-permute-start(bf16[112,128]{1,0:T(8,128)(2,1)S(1)} %copy-done.3), channel_id=1, source_target_pairs={{0,32},{1,96},{2,160},{3,224},{4,288},{5,352},{6,416},{7,480},{16,... | collective-permute-start | bytes 86024 | tf_op jit(solution)/shard_map/ppermute | solution.py:373
  24.9 8.5 %collective-permute-start.2 = (bf16[112,128]{1,0:T(8,128)(2,1)S(1)}, bf16[112,128]{1,0:T(8,128)(2,1)S(1)}, u32[]{:S(2)}, u32[]{:S(2)}) collective-permute-start(bf16[112,128]{1,0:T(8,128)(2,1)S(1)} %copy-done.2), channel_id=1, source_target_pairs={{0,0},{1,64},{2,128},{3,192},{4,256},{5,320},{6,384},{7,448},{16,2... | collective-permute-start | bytes 86024 | tf_op jit(solution)/shard_map/ppermute | solution.py:372
  33.4 5.0 %collective-permute-done.2 = bf16[112,128]{1,0:T(8,128)(2,1)S(1)} collective-permute-done((bf16[112,128]{1,0:T(8,128)(2,1)S(1)}, bf16[112,128]{1,0:T(8,128)(2,1)S(1)}, u32[]{:S(2)}, u32[]{:S(2)}) %collective-permute-start.2) | collective-permute-done | bytes 28704 | tf_op jit(solution)/shard_map/ppermute | solution.py:372
  39.6 11.4 %all-to-all-start.1 = ((bf16[16,224,128]{2,1,0:T(8,128)(2,1)}), bf16[16,224,128]{2,1,0:T(8,128)(2,1)S(1)}, u32[]{:S(2)}, u32[]{:S(2)}) async-start(bf16[16,224,128]{2,1,0:T(8,128)(2,1)} %broadcast_in_dim.2), calls=%async_computation.1 | async-start | bytes 1835008 | tf_op jit(solution)/shard_map/all_to_all | solution.py:55
  51.0 1.9 %collective-permute-start = (bf16[8,128,768]{2,1,0:T(8,128)(2,1)S(1)}, bf16[8,128,768]{2,1,0:T(8,128)(2,1)}, u32[]{:S(2)}, u32[]{:S(2)}) collective-permute-start(bf16[8,128,768]{2,1,0:T(8,128)(2,1)S(1)} %all-to-all-done.tab_own), channel_id=1, source_target_pairs={{0,8},{8,0},{1,9},{9,1},{2,10},{10,2},{3,11},{11,3},{4,12},{12,4},... | collective-permute-start | bytes 4718600 | tf_op jit(solution)/shard_map/ppermute | solution.py:375
  52.9 9.0 %all-to-all-done.1.own_ref = bf16[16,224,128]{2,1,0:T(8,128)(2,1)S(1)} async-done(((bf16[16,224,128]{2,1,0:T(8,128)(2,1)}), bf16[16,224,128]{2,1,0:T(8,128)(2,1)S(1)}, u32[]{:S(2)}, u32[]{:S(2)}) %all-to-all-start.1) | async-done | bytes 917536 | tf_op jit(solution)/shard_map/all_to_all | solution.py:55
  61.9 1.9 %collective-permute-start.3 = (bf16[16,224,128]{2,1,0:T(8,128)(2,1)S(1)}, bf16[16,224,128]{2,1,0:T(8,128)(2,1)S(1)}, u32[]{:S(2)}, u32[]{:S(2)}) collective-permute-start(bf16[16,224,128]{2,1,0:T(8,128)(2,1)S(1)} %all-to-all-done.1.own_ref), channel_id=1, source_target_pairs={{0,8},{8,0},{1,9},{9,1},{2,10},{10,2},{3,11},{11,3},{4,12},{12,4},... | collective-permute-start | bytes 2752520 | tf_op jit(solution)/shard_map/ppermute | solution.py:381
  63.8 2.4 %collective-permute-done.3.other_ref = bf16[16,224,128]{2,1,0:T(8,128)(2,1)S(1)} collective-permute-done((bf16[16,224,128]{2,1,0:T(8,128)(2,1)S(1)}, bf16[16,224,128]{2,1,0:T(8,128)(2,1)S(1)}, u32[]{:S(2)}, u32[]{:S(2)}) %collective-permute-start.3) | collective-permute-done | bytes 917536 | tf_op jit(solution)/shard_map/ppermute | solution.py:381
  66.3 7.8 %shard_map.115 = (bf16[256,128]{1,0:T(8,128)(2,1)S(1)}, bf16[8,256,256]{2,1,0:T(8,128)(2,1)S(1)}) custom-call(bf16[8,128,768]{2,1,0:T(8,128)(2,1)S(1)} %all-to-all-done.tab_own, bf16[8,128,768]{2,1,0:T(8,128)(2,1)} %collective-permute-done.tab_other, bf16[16,224,128]{2,1,0:T(8,128)(2,1)S(1)} %all-to-all-done.1.own_ref, ...), custom_call_target="tpu_custom_call" | custom-call | flops 1073741824 | bytes 4194304 | tf_op jit(solution)/shard_map/pallas_call | solution.py:304
  75.0 6.4 %all-to-all-start.2 = ((bf16[8,256,256]{2,1,0:T(8,128)(2,1)}), bf16[8,256,256]{2,1,0:T(8,128)(2,1)}, u32[]{:S(2)}, u32[]{:S(2)}) async-start(bf16[8,256,256]{2,1,0:T(8,128)(2,1)} %copy-done), calls=%async_computation.2 | async-start | bytes 2097152 | tf_op jit(solution)/shard_map/all_to_all | solution.py:385
  81.4 3.4 %collective-permute-start.4 = (bf16[256,128]{1,0:T(8,128)(2,1)S(1)}, bf16[256,128]{1,0:T(8,128)(2,1)S(1)}, u32[]{:S(2)}, u32[]{:S(2)}) collective-permute-start(bf16[256,128]{1,0:T(8,128)(2,1)S(1)} %get-tuple-element.16.q_own), channel_id=1, source_target_pairs={{0,16},{16,0},{1,17},{17,1},{2,18},{18,2},{3,19},{19,3},{4,20},{20... | collective-permute-start | bytes 196616 | tf_op jit(solution)/shard_map/ppermute | solution.py:384
  84.8 11.4 %collective-permute-done.4.q_other = bf16[256,128]{1,0:T(8,128)(2,1)S(1)} collective-permute-done((bf16[256,128]{1,0:T(8,128)(2,1)S(1)}, bf16[256,128]{1,0:T(8,128)(2,1)S(1)}, u32[]{:S(2)}, u32[]{:S(2)}) %collective-permute-start.4) | collective-permute-done | bytes 65568 | tf_op jit(solution)/shard_map/ppermute | solution.py:384
  97.3 1.9 %collective-permute-start.5 = (bf16[8,256,256]{2,1,0:T(8,128)(2,1)}, bf16[8,256,256]{2,1,0:T(8,128)(2,1)S(1)}, u32[]{:S(2)}, u32[]{:S(2)}) collective-permute-start(bf16[8,256,256]{2,1,0:T(8,128)(2,1)} %all-to-all-done.2.kv_own), channel_id=1, source_target_pairs={{0,8},{8,0},{1,9},{9,1},{2,10},{10,2},{3,11},{11,3},{4,12},{12,4},... | collective-permute-start | bytes 3145736 | tf_op jit(solution)/shard_map/ppermute | solution.py:387
  99.3 2.8 %collective-permute-done.5.kv_other = bf16[8,256,256]{2,1,0:T(8,128)(2,1)S(1)} collective-permute-done((bf16[8,256,256]{2,1,0:T(8,128)(2,1)}, bf16[8,256,256]{2,1,0:T(8,128)(2,1)S(1)}, u32[]{:S(2)}, u32[]{:S(2)}) %collective-permute-start.5) | collective-permute-done | bytes 1048608 | tf_op jit(solution)/shard_map/ppermute | solution.py:387
  102.1 3.9 %shard_map.116 = (f32[136,128]{1,0:T(8,128)S(1)}, f32[136,128]{1,0:T(8,128)S(1)}, f32[136,128]{1,0:T(8,128)S(1)}, f32[136,128]{1,0:T(8,128)S(1)}) custom-call(bf16[256,128]{1,0:T(8,128)(2,1)S(1)} %get-tuple-element.16.q_own, bf16[256,128]{1,0:T(8,128)(2,1)S(1)} %collective-permute-done.4.q_other, bf16[8,256,256]{2,1,0:T(8,128)(2,1)} %all-to-all-done.2.kv_own, ...), custom_call_target="tpu_custom_call" | custom-call | flops 1073741824 | bytes 4194304 | tf_op jit(solution)/shard_map/pallas_call | solution.py:304
  106.0 3.4 %collective-permute-start.6 = (f32[136,128]{1,0:T(8,128)S(1)}, f32[136,128]{1,0:T(8,128)S(1)}, u32[]{:S(2)}, u32[]{:S(2)}) collective-permute-start(f32[136,128]{1,0:T(8,128)S(1)} %get-tuple-element.21), channel_id=1, source_target_pairs={{0,16},{16,0},{1,17},{17,1},{2,18},{18,2},{3,19},{19,3},{4,20},{20... | collective-permute-start | bytes 208904 | tf_op jit(solution)/shard_map/ppermute | solution.py:391
  109.4 4.0 %collective-permute-start.7 = (f32[136,128]{1,0:T(8,128)S(1)}, f32[136,128]{1,0:T(8,128)S(1)}, u32[]{:S(2)}, u32[]{:S(2)}) collective-permute-start(f32[136,128]{1,0:T(8,128)S(1)} %get-tuple-element.22), channel_id=1, source_target_pairs={{0,32},{32,0},{64,96},{96,64},{128,160},{160,128},{192,224},{224,1... | collective-permute-start | bytes 208904 | tf_op jit(solution)/shard_map/ppermute | solution.py:390
  113.4 1.9 %collective-permute-start.8 = (f32[136,128]{1,0:T(8,128)S(1)}, f32[136,128]{1,0:T(8,128)S(1)}, u32[]{:S(2)}, u32[]{:S(2)}) collective-permute-start(f32[136,128]{1,0:T(8,128)S(1)} %get-tuple-element.23), channel_id=1, source_target_pairs={{0,48},{16,32},{32,16},{48,0},{64,112},{80,96},{96,80},{112,64},{1... | collective-permute-start | bytes 208904 | tf_op jit(solution)/shard_map/ppermute | solution.py:389
  115.6 4.8 %collective-permute-done.8.got_both = f32[136,128]{1,0:T(8,128)S(1)} collective-permute-done((f32[136,128]{1,0:T(8,128)S(1)}, f32[136,128]{1,0:T(8,128)S(1)}, u32[]{:S(2)}, u32[]{:S(2)}) %collective-permute-start.8) | collective-permute-done | bytes 69664 | tf_op jit(solution)/shard_map/ppermute | solution.py:389
  120.7 6.9 %collective-permute-start.9 = (bf16[128,256]{1,0:T(8,128)(2,1)S(1)}, bf16[128,256]{1,0:T(8,128)(2,1)S(1)}, u32[]{:S(2)}, u32[]{:S(2)}) collective-permute-start(bf16[128,256]{1,0:T(8,128)(2,1)S(1)} %shard_map.117), channel_id=1, source_target_pairs={{0,0},{64,1},{128,2},{192,3},{256,4},{320,5},{384,6},{448,7},{23,1... | collective-permute-start | bytes 196616 | tf_op jit(solution)/shard_map/ppermute | solution.py:393
  127.6 3.4 %shard_map.114 = bf16[128,256]{1,0:T(8,128)(2,1)} custom-call(bf16[8,128,768]{2,1,0:T(8,128)(2,1)S(1)} %all-to-all-done.tab_own, bf16[8,128,768]{2,1,0:T(8,128)(2,1)} %collective-permute-done.tab_other, bf16[16,224,128]{2,1,0:T(8,128)(2,1)S(1)} %all-to-all-done.1.own_ref, bf16[16,224,128]{2,1,0:T(8,128)(2,1)S(1)} %collective-permute-done.3.other_ref), custom_call_target="tpu_custom_call" | custom-call | flops 67108864 | bytes 4194304 | tf_op jit(solution)/shard_map/pallas_call | solution.py:304
  131.0 8.1 %collective-permute-done.9 = bf16[128,256]{1,0:T(8,128)(2,1)S(1)} collective-permute-done((bf16[128,256]{1,0:T(8,128)(2,1)S(1)}, bf16[128,256]{1,0:T(8,128)(2,1)S(1)}, u32[]{:S(2)}, u32[]{:S(2)}) %collective-permute-start.9) | collective-permute-done | bytes 65568 | tf_op jit(solution)/shard_map/ppermute | solution.py:393
  (23 shorter events, 4.4 us)
Async XLA Ops:
  3.8 6.7 %copy-start.3 = (bf16[112,128]{1,0:T(8,128)(2,1)S(1)}, bf16[112,128]{1,0:T(8,128)(2,1)}, u32[]{:S(2)}) copy-start(bf16[112,128]{1,0:T(8,128)(2,1)} %get-tuple-element.14) | copy-start | bytes 86020
  3.8 21.1 %copy-start.2 = (bf16[112,128]{1,0:T(8,128)(2,1)S(1)}, bf16[112,128]{1,0:T(8,128)(2,1)}, u32[]{:S(2)}) copy-start(bf16[112,128]{1,0:T(8,128)(2,1)} %get-tuple-element.15) | copy-start | bytes 86020
  3.8 34.7 %all-to-all-start = ((bf16[8,128,768]{2,1,0:T(8,128)(2,1)}), bf16[8,128,768]{2,1,0:T(8,128)(2,1)S(1)}, u32[]{:S(2)}, u32[]{:S(2)}) async-start(bf16[8,128,768]{2,1,0:T(8,128)(2,1)} %get-tuple-element.13), calls=%async_computation | async-start | bytes 3145728 | tf_op jit(solution)/shard_map/all_to_all | solution.py:374
  10.5 22.9 %collective-permute-start.1 = (bf16[112,128]{1,0:T(8,128)(2,1)S(1)}, bf16[112,128]{1,0:T(8,128)(2,1)S(1)}, u32[]{:S(2)}, u32[]{:S(2)}) collective-permute-start(bf16[112,128]{1,0:T(8,128)(2,1)S(1)} %copy-done.3), channel_id=1, source_target_pairs={{0,32},{1,96},{2,160},{3,224},{4,288},{5,352},{6,416},{7,480},{16,... | collective-permute-start | bytes 86024 | tf_op jit(solution)/shard_map/ppermute | solution.py:373
  24.9 13.6 %collective-permute-start.2 = (bf16[112,128]{1,0:T(8,128)(2,1)S(1)}, bf16[112,128]{1,0:T(8,128)(2,1)S(1)}, u32[]{:S(2)}, u32[]{:S(2)}) collective-permute-start(bf16[112,128]{1,0:T(8,128)(2,1)S(1)} %copy-done.2), channel_id=1, source_target_pairs={{0,0},{1,64},{2,128},{3,192},{4,256},{5,320},{6,384},{7,448},{16,2... | collective-permute-start | bytes 86024 | tf_op jit(solution)/shard_map/ppermute | solution.py:372
  33.4 32.8 %copy-start.1 = (f32[2048]{0:T(1024)S(1)}, f32[2048]{0:T(1024)}, u32[]{:S(2)}) copy-start(f32[2048]{0:T(1024)} %param.16) | copy-start | bytes 24580
  39.6 22.3 %all-to-all-start.1 = ((bf16[16,224,128]{2,1,0:T(8,128)(2,1)}), bf16[16,224,128]{2,1,0:T(8,128)(2,1)S(1)}, u32[]{:S(2)}, u32[]{:S(2)}) async-start(bf16[16,224,128]{2,1,0:T(8,128)(2,1)} %broadcast_in_dim.2), calls=%async_computation.1 | async-start | bytes 1835008 | tf_op jit(solution)/shard_map/all_to_all | solution.py:55
  51.0 15.2 %collective-permute-start = (bf16[8,128,768]{2,1,0:T(8,128)(2,1)S(1)}, bf16[8,128,768]{2,1,0:T(8,128)(2,1)}, u32[]{:S(2)}, u32[]{:S(2)}) collective-permute-start(bf16[8,128,768]{2,1,0:T(8,128)(2,1)S(1)} %all-to-all-done.tab_own), channel_id=1, source_target_pairs={{0,8},{8,0},{1,9},{9,1},{2,10},{10,2},{3,11},{11,3},{4,12},{12,4},... | collective-permute-start | bytes 4718600 | tf_op jit(solution)/shard_map/ppermute | solution.py:375
  61.9 4.4 %collective-permute-start.3 = (bf16[16,224,128]{2,1,0:T(8,128)(2,1)S(1)}, bf16[16,224,128]{2,1,0:T(8,128)(2,1)S(1)}, u32[]{:S(2)}, u32[]{:S(2)}) collective-permute-start(bf16[16,224,128]{2,1,0:T(8,128)(2,1)S(1)} %all-to-all-done.1.own_ref), channel_id=1, source_target_pairs={{0,8},{8,0},{1,9},{9,1},{2,10},{10,2},{3,11},{11,3},{4,12},{12,4},... | collective-permute-start | bytes 2752520 | tf_op jit(solution)/shard_map/ppermute | solution.py:381
  74.0 1.0 copy-start
  75.0 22.3 %all-to-all-start.2 = ((bf16[8,256,256]{2,1,0:T(8,128)(2,1)}), bf16[8,256,256]{2,1,0:T(8,128)(2,1)}, u32[]{:S(2)}, u32[]{:S(2)}) async-start(bf16[8,256,256]{2,1,0:T(8,128)(2,1)} %copy-done), calls=%async_computation.2 | async-start | bytes 2097152 | tf_op jit(solution)/shard_map/all_to_all | solution.py:385
  81.4 14.8 %collective-permute-start.4 = (bf16[256,128]{1,0:T(8,128)(2,1)S(1)}, bf16[256,128]{1,0:T(8,128)(2,1)S(1)}, u32[]{:S(2)}, u32[]{:S(2)}) collective-permute-start(bf16[256,128]{1,0:T(8,128)(2,1)S(1)} %get-tuple-element.16.q_own), channel_id=1, source_target_pairs={{0,16},{16,0},{1,17},{17,1},{2,18},{18,2},{3,19},{19,3},{4,20},{20... | collective-permute-start | bytes 196616 | tf_op jit(solution)/shard_map/ppermute | solution.py:384
  97.3 4.8 %collective-permute-start.5 = (bf16[8,256,256]{2,1,0:T(8,128)(2,1)}, bf16[8,256,256]{2,1,0:T(8,128)(2,1)S(1)}, u32[]{:S(2)}, u32[]{:S(2)}) collective-permute-start(bf16[8,256,256]{2,1,0:T(8,128)(2,1)} %all-to-all-done.2.kv_own), channel_id=1, source_target_pairs={{0,8},{8,0},{1,9},{9,1},{2,10},{10,2},{3,11},{11,3},{4,12},{12,4},... | collective-permute-start | bytes 3145736 | tf_op jit(solution)/shard_map/ppermute | solution.py:387
  106.0 9.3 %collective-permute-start.6 = (f32[136,128]{1,0:T(8,128)S(1)}, f32[136,128]{1,0:T(8,128)S(1)}, u32[]{:S(2)}, u32[]{:S(2)}) collective-permute-start(f32[136,128]{1,0:T(8,128)S(1)} %get-tuple-element.21), channel_id=1, source_target_pairs={{0,16},{16,0},{1,17},{17,1},{2,18},{18,2},{3,19},{19,3},{4,20},{20... | collective-permute-start | bytes 208904 | tf_op jit(solution)/shard_map/ppermute | solution.py:391
  109.4 6.2 %collective-permute-start.7 = (f32[136,128]{1,0:T(8,128)S(1)}, f32[136,128]{1,0:T(8,128)S(1)}, u32[]{:S(2)}, u32[]{:S(2)}) collective-permute-start(f32[136,128]{1,0:T(8,128)S(1)} %get-tuple-element.22), channel_id=1, source_target_pairs={{0,32},{32,0},{64,96},{96,64},{128,160},{160,128},{192,224},{224,1... | collective-permute-start | bytes 208904 | tf_op jit(solution)/shard_map/ppermute | solution.py:390
  113.4 7.1 %collective-permute-start.8 = (f32[136,128]{1,0:T(8,128)S(1)}, f32[136,128]{1,0:T(8,128)S(1)}, u32[]{:S(2)}, u32[]{:S(2)}) collective-permute-start(f32[136,128]{1,0:T(8,128)S(1)} %get-tuple-element.23), channel_id=1, source_target_pairs={{0,48},{16,32},{32,16},{48,0},{64,112},{80,96},{96,80},{112,64},{1... | collective-permute-start | bytes 208904 | tf_op jit(solution)/shard_map/ppermute | solution.py:389
  120.7 18.5 %collective-permute-start.9 = (bf16[128,256]{1,0:T(8,128)(2,1)S(1)}, bf16[128,256]{1,0:T(8,128)(2,1)S(1)}, u32[]{:S(2)}, u32[]{:S(2)}) collective-permute-start(bf16[128,256]{1,0:T(8,128)(2,1)S(1)} %shard_map.117), channel_id=1, source_target_pairs={{0,0},{64,1},{128,2},{192,3},{256,4},{320,5},{384,6},{448,7},{23,1... | collective-permute-start | bytes 196616 | tf_op jit(solution)/shard_map/ppermute | solution.py:393

commit v5 on v4

--- a/solution.py
+++ b/solution.py
@@ -17,15 +17,17 @@
 P_DEV = 128
 W_ROWS = 32
 VALUES = 128
-ROWS = 2 * 3 * W_ROWS
-MSG = ROWS + 2 * 16
+ROWS = 3 * W_ROWS
+MSG = ROWS + 16
 PART = P_DEV + 8
 VMEM = 20 * 1024 * 1024
 
-CTX = ("z", "yl", "c")
+Z = ("zh", "zl")
+CTX = (*Z, "yl", "c")
+PAIR = ("zl", "yl")
 TP = ("x", "yh")
-PLANE = ("x", "yh", "yl")
-TURN = ("z", "yl", "x", "yh")
+PLANES = ("zl", "x", "yh", "yl")
+TURN = (*Z, "yl", "x", "yh")
 
 
 def turned(index, yl):
@@ -37,22 +39,12 @@
 
 
 def turns():
-    same, other = [], []
-    for z in range(16):
-        for yl in range(2):
-            for t in range(N_TP):
-                tt = turned(z // 2, yl)
-                same.append((flat(z, yl, t), flat(2 * t + z % 2, yl, tt)))
-                other.append((flat(z, yl, t), flat(2 * t + 1 - z % 2, yl, tt)))
-    return same, other
-
-
-def back(pairs):
-    return [(target, source) for source, target in pairs]
-
-
-def to_all(value, axes, count):
-    return lax.all_to_all(jnp.broadcast_to(value[None], (count, *value.shape)), axes, 0, 0)
+    return [
+        (flat(z, yl, t), flat(2 * t + z % 2, yl, turned(z // 2, yl)))
+        for z in range(16)
+        for yl in range(2)
+        for t in range(N_TP)
+    ]
 
 
 def nt_dot(a, b):
@@ -62,12 +54,11 @@
 def lens_before(d, c, own_ref, other_ref):
     total = jnp.zeros((), jnp.float32)
     for ref, core in ((own_ref, c), (other_ref, 1 - c)):
-        for b in range(2):
-            tiles = ref[:, ROWS + 16 * b : ROWS + 16 * (b + 1), :].astype(jnp.float32)
-            unit, row = (lax.broadcasted_iota(jnp.int32, tiles.shape, i) for i in range(2))
-            z = 2 * turned(unit // 2, unit % 2) + b
-            place = 4 * z + 2 * (unit % 2) + core
-            total = total + jnp.sum(jnp.where((row == 4) & (place < d), tiles, 0.0))
+        tiles = ref[:, ROWS:, :].astype(jnp.float32)
+        slot, row = (lax.broadcasted_iota(jnp.int32, tiles.shape, i) for i in range(2))
+        unit, b = slot % 16, slot // 16
+        place = 8 * turned(unit // 2, unit % 2) + 4 * b + 2 * (unit % 2) + core
+        total = total + jnp.sum(jnp.where((row == 4) & (place < d), tiles, 0.0))
     return total
 
 
@@ -77,8 +68,7 @@
     def tile(ref, place):
         z, yl = place // 4, (place // 2) % 2
         unit = 2 * turned(z // 2, yl) + yl
-        first = pl.multiple_of(ROWS + 16 * (z % 2), 16)
-        return ref[unit, pl.ds(first, 16), :].astype(jnp.float32)
+        return ref[16 * (z % 2) + unit, ROWS:, :].astype(jnp.float32)
 
     here, beyond = tile(own_ref, d), tile(other_ref, follow)
     begin = lens_before(d, c, own_ref, other_ref) - (d * BYTES_DEV).astype(jnp.float32)
@@ -88,7 +78,7 @@
     lens = jnp.sum(jnp.where(col == row, lens_row, 0.0), axis=1, keepdims=True)
     start = begin + jnp.sum(jnp.where(col < row, lens_row, 0.0), axis=1, keepdims=True)
     end = start + lens
-    value = (lax.broadcasted_iota(jnp.int32, (256, P_DEV), 0) + 128 * c) % 256
+    value = lax.broadcasted_iota(jnp.int32, (256, P_DEV), 0) ^ (VALUES * c)
     value = value.astype(jnp.float32)
     slot = col.astype(jnp.float32)
     counts = jnp.zeros((P_DEV, 256), jnp.float32)
@@ -120,19 +110,20 @@
 
 
 def coordinates():
-    z, yl, c = (lax.axis_index(name) for name in CTX)
-    return z, yl, c, 2 * lax.axis_index("x") + lax.axis_index("yh")
-
-
-def table_of(tt, own_ref, other_ref):
-    return jnp.concatenate([own_ref[tt], other_ref[tt]], axis=0)
+    zh, zl, yl, c = (lax.axis_index(name) for name in CTX)
+    return 2 * zh + zl, yl, c, 2 * lax.axis_index("x") + lax.axis_index("yh")
+
+
+def table_of(tt, refs):
+    return jnp.concatenate([ref[tt] for ref in refs], axis=0)
 
 
 def start_kernel(
-    ids_ref, lens_ref, table_ref, wq, wk, wv, lq, lk, lv, tables_ref, same_ref, other_ref
+    ids_ref, lens_ref, table_ref, wq, wk, wv, lq, lk, lv, tables_ref, message_ref
 ):
-    z, _, c, _ = coordinates()
-    rows = table_ref[pl.ds(pl.multiple_of(VALUES * c, VALUES), VALUES), :]
+    _, _, c, _ = coordinates()
+    first = pl.multiple_of(VALUES * c, VALUES)
+    rows = table_ref[pl.ds(first, VALUES), :]
     for i, ref in enumerate((wq, wk, wv)):
         part = jnp.dot(rows, ref[...], preferred_element_type=jnp.float32).astype(jnp.bfloat16)
         for tt in range(N_TP):
@@ -140,26 +131,26 @@
     ints = jnp.concatenate(
         [ids_ref[...], lens_ref[...], jnp.zeros((11, HD), jnp.int32)], axis=0
     ).astype(jnp.float32)
-    odd = z % 2
-    for out, a in ((same_ref, odd), (other_ref, 1 - odd)):
+    for a in range(2):
         for i, ref in enumerate((lq, lk, lv)):
-            out[i * W_ROWS : (i + 1) * W_ROWS, :] = ref[:, pl.ds(pl.multiple_of(a * HD, HD), HD)]
-        out[3 * W_ROWS :, :] = ints.astype(jnp.bfloat16)
-
-
-def encode_kernel(
-    tab_own, tab_other, own_ref, other_ref, gain_ref, q_ref, kv_ref, latent, weight
-):
+            message_ref[a, i * W_ROWS : (i + 1) * W_ROWS, :] = ref[:, a * HD : (a + 1) * HD]
+        message_ref[a, ROWS:, :] = ints.astype(jnp.bfloat16)
+
+
+def encode_kernel(*refs):
+    tables = refs[:2]
+    own_ref, other_ref, gain_ref, q_ref, kv_ref, latent, weight = refs[2:]
     _, yl, c, t = coordinates()
     first_z = 2 * turned(t, yl)
     parts = [
-        byte_counts(4 * z + 2 * yl + c, c, own_ref, other_ref) for z in (first_z, first_z + 1)
+        byte_counts(4 * z + 2 * yl + c, c, own_ref, other_ref)
+        for z in (first_z, first_z + 1)
     ]
     counts = jnp.concatenate([part[0] for part in parts], axis=0)
     lens = jnp.concatenate([part[1] for part in parts], axis=0)
 
     def heads(tt, squares):
-        out = two_heads(counts, lens, table_of(tt, tab_own, tab_other))
+        out = two_heads(counts, lens, table_of(tt, tables))
         latent[tt] = out
         wide = out.astype(jnp.float32)
         for ref, core in ((own_ref, c), (other_ref, 1 - c)):
@@ -167,9 +158,8 @@
                 for side in range(2):
                     first = pl.multiple_of(W_ROWS * (4 * b + 2 * side + core), W_ROWS)
                     for n in range(3):
-                        start = (3 * b + n) * W_ROWS
                         weight[turned(tt, side), pl.ds(first, W_ROWS), n * HD : (n + 1) * HD] = ref[
-                            2 * tt + side, start : start + W_ROWS, :
+                            16 * b + 2 * tt + side, n * W_ROWS : (n + 1) * W_ROWS, :
                         ]
         return squares + jnp.sum(wide * wide, axis=-1, keepdims=True)
 
@@ -188,10 +178,11 @@
         kv_ref[tt] = total[:, HD:]
 
 
-def latent_kernel(tab_own, tab_other, own_ref, other_ref, out_ref):
+def latent_kernel(*refs):
+    own_ref, other_ref, out_ref = refs[2:]
     z, yl, c, t = coordinates()
     counts, lens = byte_counts(4 * z + 2 * yl + c, c, own_ref, other_ref)
-    out_ref[...] = two_heads(counts, lens, table_of(t, tab_own, tab_other))
+    out_ref[...] = two_heads(counts, lens, table_of(t, refs[:2]))
 
 
 def diagonal():
@@ -212,17 +203,14 @@
     q_other,
     kv_own,
     kv_other,
-    keep_ref,
-    to_yl_ref,
-    to_z_ref,
-    to_both_ref,
+    out_ref,
     scores,
     query,
     tops,
     norms,
     accs,
 ):
-    z, yl, c, t = coordinates()
+    _, yl, c, t = coordinates()
     size = 2 * P_DEV
     query[yl] = q_own[...]
     query[1 - yl] = q_other[...]
@@ -272,31 +260,26 @@
             )
         norms[q_yl] = norm
         accs[q_yl] = acc
-    odd = z % 2
-    for out, q_yl, b in (
-        (keep_ref, yl, odd),
-        (to_yl_ref, 1 - yl, odd),
-        (to_z_ref, yl, 1 - odd),
-        (to_both_ref, 1 - yl, 1 - odd),
-    ):
-        rows = pl.ds(pl.multiple_of(b * P_DEV, P_DEV), P_DEV)
-        out[:P_DEV, :] = accs[q_yl, rows, :]
-        total = jnp.sum(norms[q_yl, rows, :], axis=-1, keepdims=True)
-        stats = [as_row(tops[q_yl, rows, :][:, :1]), as_row(total), jnp.zeros((6, HD), jnp.float32)]
-        out[P_DEV:, :] = jnp.concatenate(stats, axis=0)
-
-
-def join_kernel(kept, got_yl, got_z, got_both, out_ref):
-    z, _, _, _ = coordinates()
-    odd = z % 2
-    for a, pair in ((odd, (kept, got_yl)), (1 - odd, (got_z, got_both))):
-        tops = [as_column(ref[P_DEV : P_DEV + 1, :]) for ref in pair]
-        sums = [as_column(ref[P_DEV + 1 : P_DEV + 2, :]) for ref in pair]
+    for b in range(2):
+        rows = slice(b * P_DEV, (b + 1) * P_DEV)
+        for q_yl in range(2):
+            slot = 2 * b + q_yl
+            out_ref[slot, :P_DEV, :] = accs[q_yl, rows, :]
+            total = jnp.sum(norms[q_yl, rows, :], axis=-1, keepdims=True)
+            stats = [as_row(tops[q_yl, rows, :1]), as_row(total), jnp.zeros((6, HD), jnp.float32)]
+            out_ref[slot, P_DEV:, :] = jnp.concatenate(stats, axis=0)
+
+
+def join_kernel(part_ref, out_ref):
+    for a in range(2):
+        slots = (2 * a, 2 * a + 1)
+        tops = [as_column(part_ref[i, P_DEV : P_DEV + 1, :]) for i in slots]
+        sums = [as_column(part_ref[i, P_DEV + 1 : P_DEV + 2, :]) for i in slots]
         top = jnp.maximum(*tops)
         scale = [jnp.exp(part - top) for part in tops]
-        mixed = pair[0][:P_DEV, :] * scale[0] + pair[1][:P_DEV, :] * scale[1]
+        mixed = part_ref[slots[0], :P_DEV, :] * scale[0] + part_ref[slots[1], :P_DEV, :] * scale[1]
         mixed = mixed / (sums[0] * scale[0] + sums[1] * scale[1])
-        out_ref[:, pl.ds(pl.multiple_of(a * HD, HD), HD)] = mixed.astype(jnp.bfloat16)
+        out_ref[:, a * HD : (a + 1) * HD] = mixed.astype(jnp.bfloat16)
 
 
 def call(body, outs, scratch, flops, *args, limit=VMEM):
@@ -316,7 +299,7 @@
 
 
 def run_start(*args):
-    outs = [((N_TP, VALUES, 6 * HD), BF)] + [((3 * W_ROWS + 16, HD), BF)] * 2
+    outs = [((N_TP, VALUES, 6 * HD), BF), ((2, MSG, HD), BF)]
     return call(start_kernel, outs, [], 1 << 28, *args, limit=56 << 20)
 
 
@@ -334,7 +317,7 @@
     size = 2 * P_DEV
     block = (2, size, HD)
     scratch = [((N_TP + 1, 2, size, size), F32), (block, BF)] + [(block, F32)] * 3
-    return call(attend_kernel, [((PART, HD), F32)] * 4, scratch, 1 << 30, *args)
+    return call(attend_kernel, [((4, PART, HD), F32)], scratch, 1 << 30, *args)[0]
 
 
 def run_join(*args):
@@ -353,12 +336,10 @@
     wk_latent,
     wv_latent,
 ):
-    z = lax.axis_index("z")
-    odd = z % 2 == 1
     swap = [(0, 1), (1, 0)]
-    same, other = turns()
-
-    tables, to_same, to_other = run_start(
+    turn = turns()
+
+    tables, message = run_start(
         byte_ids.reshape(4, HD),
         patch_lens.reshape(1, HD),
         byte_table,
@@ -369,34 +350,27 @@
         wk_latent,
         wv_latent,
     )
-    got_same = lax.ppermute(to_same, TURN, same)
-    got_other = lax.ppermute(to_other, TURN, other)
+    message = lax.ppermute(message, TURN, turn)
     tab_own = lax.all_to_all(tables, TP, 0, 0)
-    tab_other = lax.ppermute(tab_own, "c", swap)
-    near = jnp.where(odd, got_other, got_same)
-    away = jnp.where(odd, got_same, got_other)
-    cut = 3 * W_ROWS
-    message = jnp.concatenate([near[:cut], away[:cut], near[cut:], away[cut:]], axis=0)
-    msg_own = to_all(message, PLANE, 16)
+    byte_tables = (tab_own, lax.ppermute(tab_own, "c", swap))
+    message = jnp.broadcast_to(message[:, None], (2, 16, MSG, HD)).reshape(32, MSG, HD)
+    msg_own = lax.all_to_all(message, PLANES, 0, 0, tiled=True)
     msg_other = lax.ppermute(msg_own, "c", swap)
 
-    q, kv = run_encode(tab_own, tab_other, msg_own, msg_other, norm_gain.reshape(1, 2048))
+    q, kv = run_encode(*byte_tables, msg_own, msg_other, norm_gain.reshape(1, 2048))
     q_other = lax.ppermute(q, "yl", swap)
     kv_own = lax.all_to_all(kv, TP, 0, 0)
     kv_own, q_other = lax.optimization_barrier((kv_own, q_other))
     kv_other = lax.ppermute(kv_own, "c", swap)
-    kept, to_yl, to_z, to_both = run_attend(q, q_other, kv_own, kv_other)
-    got_both = lax.ppermute(to_both, ("z", "yl"), [(i, i ^ 3) for i in range(32)])
-    got_z = lax.ppermute(to_z, "z", [(i, i ^ 1) for i in range(16)])
-    got_yl = lax.ppermute(to_yl, "yl", swap)
-    mixed = run_join(kept, got_yl, got_z, got_both)
-    latent_mixed = lax.ppermute(mixed, TURN, back(same))
-    patch_latent = run_latent(tab_own, tab_other, msg_own, msg_other)
+    parts = run_attend(q, q_other, kv_own, kv_other)
+    mixed = run_join(lax.all_to_all(parts, PAIR, 0, 0))
+    latent_mixed = lax.ppermute(mixed, TURN, [(target, source) for source, target in turn])
+    patch_latent = run_latent(*byte_tables, msg_own, msg_other)
     return (patch_latent, latent_mixed)
 
 
 def solution(mesh):
-    fine = Mesh(mesh.devices.reshape(16, 2, 2, 4, 2), ("z", "yl", "c", "x", "yh"))
+    fine = Mesh(mesh.devices.reshape(8, 2, 2, 2, 4, 2), (*CTX, *TP))
     return jax.shard_map(
         on_device,
         mesh=fine,

time: 140 us -> 132 us (0.943)
  the two profiles are of different devices: /device:TPU:10 before, /device:TPU:4 now
where the time goes in v5:
time: 132 us; the launch traced here: 131 us
  starting transfers between devices  64.2 us (49%)
  waiting for transfers between devices  36.2 us (27%)
  Pallas kernels  18.4 us (14%)
  blocking collectives  9.26 us (7%)
  local copies, waits for them, and re-layouts  2.65 us (2%)
    ppermute x1, starting transfers between devices, on_device(): lax.ppermute(mixed, TURN, [(target, source) for source, target in turn])  19.5 us
    pallas_call x5, Pallas kernels, call(): pl.pallas_call(body, out_shape=[jax.ShapeDtypeStruct(shape, dtype) for sh...  18.4 us
    ppermute x1, starting transfers between devices, on_device(): message = lax.ppermute(message, TURN, turn)  13.2 us
    ppermute x1, waiting for transfers between devices, on_device(): q_other = lax.ppermute(q, 'yl', swap)  11.6 us
    all_to_all x1, waiting for transfers between devices, on_device(): msg_own = lax.all_to_all(message, PLANES, 0, 0, tiled=True)  11.1 us
    all_to_all x1, starting transfers between devices, on_device(): tab_own = lax.all_to_all(tables, TP, 0, 0)  9.51 us
    all_to_all x1, blocking collectives, on_device(): mixed = run_join(lax.all_to_all(parts, PAIR, 0, 0))  9.26 us
    all_to_all x1, starting transfers between devices, on_device(): msg_own = lax.all_to_all(message, PLANES, 0, 0, tiled=True)  7.46 us
  transfers between devices with their start and end apart: 9, of which 7 were waited for; matrix products, arithmetic and copies ran while one was open for 0% of the time, Pallas kernels for 3%

profile of v5, /device:TPU:4, one launch (start us, length us, event | category | flops | bytes accessed | tf_op | source)
XLA Modules:
  0.0 131.4 jit_solution(5047204638220662840)
XLA Ops:
  0.6 3.2 %shard_map.113 = (bf16[8,128,768]{2,1,0:T(8,128)(2,1)}, bf16[2,112,128]{2,1,0:T(8,128)(2,1)}) custom-call(s32[4,128]{1,0:T(4,128)} %bitcast.5, s32[1,128]{1,0:T(1,128)} %bitcast.6, bf16[256,1024]{1,0:T(8,128)(2,1)} %table_ref.1, bf16[1024,256]{1,0:T(8,128)(2,1)} %wq.1, bf16[1024,256]{1,0:T(8,128)(2,1)} %wk.1, bf16[1024,256]{1,0:T(8,128)(2,1)} %wv.1, ...), custom_call_target="tpu_custom_call" | custom-call | flops 268435456 | bytes 4194304 | tf_op jit(solution)/shard_map/pallas_call | solution.py:287
  3.8 9.5 %all-to-all-start = ((bf16[8,128,768]{2,1,0:T(8,128)(2,1)}), bf16[8,128,768]{2,1,0:T(8,128)(2,1)S(1)}, u32[]{:S(2)}, u32[]{:S(2)}) async-start(bf16[8,128,768]{2,1,0:T(8,128)(2,1)} %get-tuple-element.8), calls=%async_computation | async-start | bytes 3145728 | tf_op jit(solution)/shard_map/all_to_all | solution.py:354
  13.3 13.2 %collective-permute-start.1 = (bf16[2,112,128]{2,1,0:T(8,128)(2,1)S(1)}, bf16[2,112,128]{2,1,0:T(8,128)(2,1)S(1)}, u32[]{:S(2)}, u32[]{:S(2)}) collective-permute-start(bf16[2,112,128]{2,1,0:T(8,128)(2,1)S(1)} %copy-done.2), channel_id=1, source_target_pairs={{0,0},{1,64},{2,128},{3,192},{4,256},{5,320},{6,384},{7,448},{16,2... | collective-permute-start | bytes 172040 | tf_op jit(solution)/shard_map/ppermute | solution.py:353
  26.6 4.2 %collective-permute-done.1 = bf16[2,112,128]{2,1,0:T(8,128)(2,1)S(1)} collective-permute-done((bf16[2,112,128]{2,1,0:T(8,128)(2,1)S(1)}, bf16[2,112,128]{2,1,0:T(8,128)(2,1)S(1)}, u32[]{:S(2)}, u32[]{:S(2)}) %collective-permute-start.1) | collective-permute-done | bytes 57376 | tf_op jit(solution)/shard_map/ppermute | solution.py:353
  30.7 3.0 %all-to-all-done.refs_0_ = bf16[8,128,768]{2,1,0:T(8,128)(2,1)S(1)} async-done(((bf16[8,128,768]{2,1,0:T(8,128)(2,1)}), bf16[8,128,768]{2,1,0:T(8,128)(2,1)S(1)}, u32[]{:S(2)}, u32[]{:S(2)}) %all-to-all-start) | async-done | bytes 1572896 | tf_op jit(solution)/shard_map/all_to_all | solution.py:354
  33.8 1.1 broadcast_in_dim.2
  34.8 7.5 %all-to-all-start.1 = ((bf16[32,112,128]{2,1,0:T(8,128)(2,1)}), bf16[32,112,128]{2,1,0:T(8,128)(2,1)S(1)}, u32[]{:S(2)}, u32[]{:S(2)}) async-start(bf16[32,112,128]{2,1,0:T(8,128)(2,1)} %bitcast.2), calls=%async_computation.1 | async-start | bytes 1835008 | tf_op jit(solution)/shard_map/all_to_all | solution.py:357
  42.3 1.9 %collective-permute-start = (bf16[8,128,768]{2,1,0:T(8,128)(2,1)S(1)}, bf16[8,128,768]{2,1,0:T(8,128)(2,1)}, u32[]{:S(2)}, u32[]{:S(2)}) collective-permute-start(bf16[8,128,768]{2,1,0:T(8,128)(2,1)S(1)} %all-to-all-done.refs_0_), channel_id=1, source_target_pairs={{0,8},{8,0},{1,9},{9,1},{2,10},{10,2},{3,11},{11,3},{4,12},{12,4},... | collective-permute-start | bytes 4718600 | tf_op jit(solution)/shard_map/ppermute | solution.py:355
  44.2 11.1 %all-to-all-done.1.refs_2_ = bf16[32,112,128]{2,1,0:T(8,128)(2,1)S(1)} async-done(((bf16[32,112,128]{2,1,0:T(8,128)(2,1)}), bf16[32,112,128]{2,1,0:T(8,128)(2,1)S(1)}, u32[]{:S(2)}, u32[]{:S(2)}) %all-to-all-start.1) | async-done | bytes 917536 | tf_op jit(solution)/shard_map/all_to_all | solution.py:357
  55.4 1.9 %collective-permute-start.2 = (bf16[32,112,128]{2,1,0:T(8,128)(2,1)S(1)}, bf16[32,112,128]{2,1,0:T(8,128)(2,1)S(1)}, u32[]{:S(2)}, u32[]{:S(2)}) collective-permute-start(bf16[32,112,128]{2,1,0:T(8,128)(2,1)S(1)} %all-to-all-done.1.refs_2_), channel_id=1, source_target_pairs={{0,8},{8,0},{1,9},{9,1},{2,10},{10,2},{3,11},{11,3},{4,12},{12,4},... | collective-permute-start | bytes 2752520 | tf_op jit(solution)/shard_map/ppermute | solution.py:358
  57.3 2.4 %collective-permute-done.2.refs_3_ = bf16[32,112,128]{2,1,0:T(8,128)(2,1)S(1)} collective-permute-done((bf16[32,112,128]{2,1,0:T(8,128)(2,1)S(1)}, bf16[32,112,128]{2,1,0:T(8,128)(2,1)S(1)}, u32[]{:S(2)}, u32[]{:S(2)}) %collective-permute-start.2) | collective-permute-done | bytes 917536 | tf_op jit(solution)/shard_map/ppermute | solution.py:358
  59.7 7.7 %shard_map.115 = (bf16[256,128]{1,0:T(8,128)(2,1)S(1)}, bf16[8,256,256]{2,1,0:T(8,128)(2,1)S(1)}) custom-call(bf16[8,128,768]{2,1,0:T(8,128)(2,1)S(1)} %all-to-all-done.refs_0_, bf16[8,128,768]{2,1,0:T(8,128)(2,1)} %collective-permute-done.refs_1_, bf16[32,112,128]{2,1,0:T(8,128)(2,1)S(1)} %all-to-all-done.1.refs_2_, ...), custom_call_target="tpu_custom_call" | custom-call | flops 1073741824 | bytes 4194304 | tf_op jit(solution)/shard_map/pallas_call | solution.py:287
  67.4 1.0 copy-done
  68.4 5.6 %all-to-all-start.2 = ((bf16[8,256,256]{2,1,0:T(8,128)(2,1)}), bf16[8,256,256]{2,1,0:T(8,128)(2,1)}, u32[]{:S(2)}, u32[]{:S(2)}) async-start(bf16[8,256,256]{2,1,0:T(8,128)(2,1)} %copy-done), calls=%async_computation.2 | async-start | bytes 2097152 | tf_op jit(solution)/shard_map/all_to_all | solution.py:362
  74.0 3.1 %collective-permute-start.3 = (bf16[256,128]{1,0:T(8,128)(2,1)S(1)}, bf16[256,128]{1,0:T(8,128)(2,1)S(1)}, u32[]{:S(2)}, u32[]{:S(2)}) collective-permute-start(bf16[256,128]{1,0:T(8,128)(2,1)S(1)} %get-tuple-element.10.q_own), channel_id=1, source_target_pairs={{0,16},{16,0},{1,17},{17,1},{2,18},{18,2},{3,19},{19,3},{4,20},{20... | collective-permute-start | bytes 196616 | tf_op jit(solution)/shard_map/ppermute | solution.py:361
  77.1 11.6 %collective-permute-done.3.q_other = bf16[256,128]{1,0:T(8,128)(2,1)S(1)} collective-permute-done((bf16[256,128]{1,0:T(8,128)(2,1)S(1)}, bf16[256,128]{1,0:T(8,128)(2,1)S(1)}, u32[]{:S(2)}, u32[]{:S(2)}) %collective-permute-start.3) | collective-permute-done | bytes 65568 | tf_op jit(solution)/shard_map/ppermute | solution.py:361
  88.7 0.9 all-to-all-done.2.kv_own
  89.6 1.9 %collective-permute-start.4 = (bf16[8,256,256]{2,1,0:T(8,128)(2,1)}, bf16[8,256,256]{2,1,0:T(8,128)(2,1)S(1)}, u32[]{:S(2)}, u32[]{:S(2)}) collective-permute-start(bf16[8,256,256]{2,1,0:T(8,128)(2,1)} %all-to-all-done.2.kv_own), channel_id=1, source_target_pairs={{0,8},{8,0},{1,9},{9,1},{2,10},{10,2},{3,11},{11,3},{4,12},{12,4},... | collective-permute-start | bytes 3145736 | tf_op jit(solution)/shard_map/ppermute | solution.py:364
  91.6 2.8 %collective-permute-done.4.kv_other = bf16[8,256,256]{2,1,0:T(8,128)(2,1)S(1)} collective-permute-done((bf16[8,256,256]{2,1,0:T(8,128)(2,1)}, bf16[8,256,256]{2,1,0:T(8,128)(2,1)S(1)}, u32[]{:S(2)}, u32[]{:S(2)}) %collective-permute-start.4) | collective-permute-done | bytes 1048608 | tf_op jit(solution)/shard_map/ppermute | solution.py:364
  94.4 3.9 %shard_map.116 = f32[4,136,128]{2,1,0:T(8,128)S(1)} custom-call(bf16[256,128]{1,0:T(8,128)(2,1)S(1)} %get-tuple-element.10.q_own, bf16[256,128]{1,0:T(8,128)(2,1)S(1)} %collective-permute-done.3.q_other, bf16[8,256,256]{2,1,0:T(8,128)(2,1)} %all-to-all-done.2.kv_own, bf16[8,256,256]{2,1,0:T(8,128)(2,1)S(1)} %collective-permute-done.4.kv_other), custom_call_target="tpu_custom_call" | custom-call | flops 1073741824 | bytes 4194304 | tf_op jit(solution)/shard_map/pallas_call | solution.py:287
  98.3 9.3 %all_to_all.20.part_ref = f32[4,136,128]{2,1,0:T(8,128)S(1)} all-to-all(f32[4,136,128]{2,1,0:T(8,128)S(1)} %shard_map.116), channel_id=1, replica_groups=mesh['zh'=8,'zl'=2,'yl'=2,'c'=2,'x'=4,'yh'=2] {'zl','yl'}, dimensions={0} | all-to-all | bytes 557056 | tf_op jit(solution)/shard_map/all_to_all | solution.py:366
  107.8 19.5 %collective-permute-start.5 = (bf16[128,256]{1,0:T(8,128)(2,1)S(1)}, bf16[128,256]{1,0:T(8,128)(2,1)S(1)}, u32[]{:S(2)}, u32[]{:S(2)}) collective-permute-start(bf16[128,256]{1,0:T(8,128)(2,1)S(1)} %shard_map.117), channel_id=1, source_target_pairs={{0,0},{64,1},{128,2},{192,3},{256,4},{320,5},{384,6},{448,7},{23,1... | collective-permute-start | bytes 196616 | tf_op jit(solution)/shard_map/ppermute | solution.py:367
  127.3 3.4 %shard_map.114 = bf16[128,256]{1,0:T(8,128)(2,1)} custom-call(bf16[8,128,768]{2,1,0:T(8,128)(2,1)S(1)} %all-to-all-done.refs_0_, bf16[8,128,768]{2,1,0:T(8,128)(2,1)} %collective-permute-done.refs_1_, bf16[32,112,128]{2,1,0:T(8,128)(2,1)S(1)} %all-to-all-done.1.refs_2_, bf16[32,112,128]{2,1,0:T(8,128)(2,1)S(1)} %collective-permute-done.2.refs_3_), custom_call_target="tpu_custom_call" | custom-call | flops 67108864 | bytes 4194304 | tf_op jit(solution)/shard_map/pallas_call | solution.py:287
  130.8 0.6 copy.13
  (8 shorter events, 0.2 us)
Async XLA Ops:
  3.8 9.5 %copy-start.2 = (bf16[2,112,128]{2,1,0:T(8,128)(2,1)S(1)}, bf16[2,112,128]{2,1,0:T(8,128)(2,1)}, u32[]{:S(2)}) copy-start(bf16[2,112,128]{2,1,0:T(8,128)(2,1)} %get-tuple-element.9) | copy-start | bytes 172036
  3.8 30.0 %all-to-all-start = ((bf16[8,128,768]{2,1,0:T(8,128)(2,1)}), bf16[8,128,768]{2,1,0:T(8,128)(2,1)S(1)}, u32[]{:S(2)}, u32[]{:S(2)}) async-start(bf16[8,128,768]{2,1,0:T(8,128)(2,1)} %get-tuple-element.8), calls=%async_computation | async-start | bytes 3145728 | tf_op jit(solution)/shard_map/all_to_all | solution.py:354
  13.3 46.4 %copy-start.1 = (f32[2048]{0:T(1024)S(1)}, f32[2048]{0:T(1024)}, u32[]{:S(2)}) copy-start(f32[2048]{0:T(1024)} %param.16) | copy-start | bytes 24580
  13.3 17.4 %collective-permute-start.1 = (bf16[2,112,128]{2,1,0:T(8,128)(2,1)S(1)}, bf16[2,112,128]{2,1,0:T(8,128)(2,1)S(1)}, u32[]{:S(2)}, u32[]{:S(2)}) collective-permute-start(bf16[2,112,128]{2,1,0:T(8,128)(2,1)S(1)} %copy-done.2), channel_id=1, source_target_pairs={{0,0},{1,64},{2,128},{3,192},{4,256},{5,320},{6,384},{7,448},{16,2... | collective-permute-start | bytes 172040 | tf_op jit(solution)/shard_map/ppermute | solution.py:353
  34.8 20.5 %all-to-all-start.1 = ((bf16[32,112,128]{2,1,0:T(8,128)(2,1)}), bf16[32,112,128]{2,1,0:T(8,128)(2,1)S(1)}, u32[]{:S(2)}, u32[]{:S(2)}) async-start(bf16[32,112,128]{2,1,0:T(8,128)(2,1)} %bitcast.2), calls=%async_computation.1 | async-start | bytes 1835008 | tf_op jit(solution)/shard_map/all_to_all | solution.py:357
  42.3 15.0 %collective-permute-start = (bf16[8,128,768]{2,1,0:T(8,128)(2,1)S(1)}, bf16[8,128,768]{2,1,0:T(8,128)(2,1)}, u32[]{:S(2)}, u32[]{:S(2)}) collective-permute-start(bf16[8,128,768]{2,1,0:T(8,128)(2,1)S(1)} %all-to-all-done.refs_0_), channel_id=1, source_target_pairs={{0,8},{8,0},{1,9},{9,1},{2,10},{10,2},{3,11},{11,3},{4,12},{12,4},... | collective-permute-start | bytes 4718600 | tf_op jit(solution)/shard_map/ppermute | solution.py:355
  55.4 4.4 %collective-permute-start.2 = (bf16[32,112,128]{2,1,0:T(8,128)(2,1)S(1)}, bf16[32,112,128]{2,1,0:T(8,128)(2,1)S(1)}, u32[]{:S(2)}, u32[]{:S(2)}) collective-permute-start(bf16[32,112,128]{2,1,0:T(8,128)(2,1)S(1)} %all-to-all-done.1.refs_2_), channel_id=1, source_target_pairs={{0,8},{8,0},{1,9},{9,1},{2,10},{10,2},{3,11},{11,3},{4,12},{12,4},... | collective-permute-start | bytes 2752520 | tf_op jit(solution)/shard_map/ppermute | solution.py:358
  67.4 1.0 copy-start
  68.4 21.2 %all-to-all-start.2 = ((bf16[8,256,256]{2,1,0:T(8,128)(2,1)}), bf16[8,256,256]{2,1,0:T(8,128)(2,1)}, u32[]{:S(2)}, u32[]{:S(2)}) async-start(bf16[8,256,256]{2,1,0:T(8,128)(2,1)} %copy-done), calls=%async_computation.2 | async-start | bytes 2097152 | tf_op jit(solution)/shard_map/all_to_all | solution.py:362
  74.0 14.7 %collective-permute-start.3 = (bf16[256,128]{1,0:T(8,128)(2,1)S(1)}, bf16[256,128]{1,0:T(8,128)(2,1)S(1)}, u32[]{:S(2)}, u32[]{:S(2)}) collective-permute-start(bf16[256,128]{1,0:T(8,128)(2,1)S(1)} %get-tuple-element.10.q_own), channel_id=1, source_target_pairs={{0,16},{16,0},{1,17},{17,1},{2,18},{18,2},{3,19},{19,3},{4,20},{20... | collective-permute-start | bytes 196616 | tf_op jit(solution)/shard_map/ppermute | solution.py:361
  89.6 4.8 %collective-permute-start.4 = (bf16[8,256,256]{2,1,0:T(8,128)(2,1)}, bf16[8,256,256]{2,1,0:T(8,128)(2,1)S(1)}, u32[]{:S(2)}, u32[]{:S(2)}) collective-permute-start(bf16[8,256,256]{2,1,0:T(8,128)(2,1)} %all-to-all-done.2.kv_own), channel_id=1, source_target_pairs={{0,8},{8,0},{1,9},{9,1},{2,10},{10,2},{3,11},{11,3},{4,12},{12,4},... | collective-permute-start | bytes 3145736 | tf_op jit(solution)/shard_map/ppermute | solution.py:364
  107.8 23.0 %collective-permute-start.5 = (bf16[128,256]{1,0:T(8,128)(2,1)S(1)}, bf16[128,256]{1,0:T(8,128)(2,1)S(1)}, u32[]{:S(2)}, u32[]{:S(2)}) collective-permute-start(bf16[128,256]{1,0:T(8,128)(2,1)S(1)} %shard_map.117), channel_id=1, source_target_pairs={{0,0},{64,1},{128,2},{192,3},{256,4},{320,5},{384,6},{448,7},{23,1... | collective-permute-start | bytes 196616 | tf_op jit(solution)/shard_map/ppermute | solution.py:367

commit v6 on v5

--- a/solution.py
+++ b/solution.py
@@ -9,7 +9,7 @@
 from jax.sharding import PartitionSpec as P
 
 HD = 128
-SCALE = 1.0 / math.sqrt(HD)
+SCALE = math.log2(math.e) / math.sqrt(HD)
 NEG = -1e30
 N_CTX = 64
 N_TP = 8
@@ -40,7 +40,7 @@
 
 def turns():
     return [
-        (flat(z, yl, t), flat(2 * t + z % 2, yl, turned(z // 2, yl)))
+        (flat(z, yl, t), flat(2 * (t ^ 2) + z % 2, yl, turned(z // 2, yl)))
         for z in range(16)
         for yl in range(2)
         for t in range(N_TP)
@@ -101,10 +101,10 @@
     for a in range(2):
         keys, values = (table[:, (i + a) * HD : (i + a + 1) * HD] for i in (2, 4))
         scores = nt_dot(query[:, a * HD : (a + 1) * HD], keys) * SCALE + hide
-        expo = jnp.exp(scores - jnp.max(scores, axis=-1, keepdims=True))
+        expo = jnp.exp2(scores - jnp.max(scores, axis=-1, keepdims=True))
         norm = jnp.sum(expo * counts, axis=-1, keepdims=True)
-        weights = (expo * (1.0 / norm)).astype(jnp.bfloat16).astype(jnp.float32) * counts
-        out = jnp.dot(weights.astype(jnp.bfloat16), values, preferred_element_type=jnp.float32)
+        weights = (expo * (1.0 / norm)).astype(jnp.bfloat16) * times
+        out = jnp.dot(weights, values, preferred_element_type=jnp.float32)
         outs.append(out.astype(jnp.bfloat16))
     return jnp.concatenate(outs, axis=1)
 
@@ -163,7 +163,7 @@
                         ]
         return squares + jnp.sum(wide * wide, axis=-1, keepdims=True)
 
-    squares = lax.fori_loop(0, N_TP, heads, jnp.zeros((2 * P_DEV, 1), jnp.float32), unroll=4)
+    squares = lax.fori_loop(0, N_TP, heads, jnp.zeros((2 * P_DEV, 1), jnp.float32), unroll=8)
     inverse = lax.rsqrt(squares / 2048.0 + 1e-05)
     total = jnp.zeros((2 * P_DEV, 3 * HD), jnp.float32)
     for tt in range(N_TP):
@@ -253,7 +253,7 @@
         top = jnp.concatenate([top, top], axis=1)
         norm, acc = norms[q_yl], accs[q_yl]
         for i, (ref, _) in enumerate(sides):
-            e = jnp.exp(scores[u, i] - top)
+            e = jnp.exp2(scores[u, i] - top)
             norm = norm + (e[:, :HD] + e[:, HD:])
             acc = acc + jnp.dot(
                 e.astype(jnp.bfloat16), ref[tt, :, HD:], preferred_element_type=jnp.float32
@@ -276,7 +276,7 @@
         tops = [as_column(part_ref[i, P_DEV : P_DEV + 1, :]) for i in slots]
         sums = [as_column(part_ref[i, P_DEV + 1 : P_DEV + 2, :]) for i in slots]
         top = jnp.maximum(*tops)
-        scale = [jnp.exp(part - top) for part in tops]
+        scale = [jnp.exp2(part - top) for part in tops]
         mixed = part_ref[slots[0], :P_DEV, :] * scale[0] + part_ref[slots[1], :P_DEV, :] * scale[1]
         mixed = mixed / (sums[0] * scale[0] + sums[1] * scale[1])
         out_ref[:, a * HD : (a + 1) * HD] = mixed.astype(jnp.bfloat16)
@@ -360,12 +360,12 @@
     q, kv = run_encode(*byte_tables, msg_own, msg_other, norm_gain.reshape(1, 2048))
     q_other = lax.ppermute(q, "yl", swap)
     kv_own = lax.all_to_all(kv, TP, 0, 0)
-    kv_own, q_other = lax.optimization_barrier((kv_own, q_other))
+    patch_latent = run_latent(*byte_tables, msg_own, msg_other)
+    kv_own, q_other, patch_latent = lax.optimization_barrier((kv_own, q_other, patch_latent))
     kv_other = lax.ppermute(kv_own, "c", swap)
     parts = run_attend(q, q_other, kv_own, kv_other)
     mixed = run_join(lax.all_to_all(parts, PAIR, 0, 0))
     latent_mixed = lax.ppermute(mixed, TURN, [(target, source) for source, target in turn])
-    patch_latent = run_latent(*byte_tables, msg_own, msg_other)
     return (patch_latent, latent_mixed)
 
 

time: 132 us -> 132 us (level)
  the two profiles are of different devices: /device:TPU:4 before, /device:TPU:70 now
where the time goes in v6:
time: 132 us; the launch traced here: 131 us
  starting transfers between devices  62.5 us (47%)
  waiting for transfers between devices  38 us (29%)
  Pallas kernels  18 us (14%)
  blocking collectives  9.25 us (7%)
  local copies, waits for them, and re-layouts  2.65 us (2%)
    pallas_call x5, Pallas kernels, call(): pl.pallas_call(body, out_shape=[jax.ShapeDtypeStruct(shape, dtype) for sh...  18 us
    ppermute x1, starting transfers between devices, on_device(): message = lax.ppermute(message, TURN, turn)  15.5 us
    ppermute x1, starting transfers between devices, on_device(): lax.ppermute(mixed, TURN, [(target, source) for source, target in turn])  13 us
    all_to_all x1, starting transfers between devices, on_device(): msg_own = lax.all_to_all(message, PLANES, 0, 0, tiled=True)  12.4 us
    all_to_all x1, waiting for transfers between devices, on_device(): msg_own = lax.all_to_all(message, PLANES, 0, 0, tiled=True)  10.9 us
    all_to_all x1, blocking collectives, on_device(): mixed = run_join(lax.all_to_all(parts, PAIR, 0, 0))  9.25 us
    ppermute x1, waiting for transfers between devices, on_device(): q_other = lax.ppermute(q, 'yl', swap)  7.98 us
    all_to_all x1, starting transfers between devices, on_device(): tab_own = lax.all_to_all(tables, TP, 0, 0)  7.53 us
  transfers between devices with their start and end apart: 9, of which 8 were waited for; matrix products, arithmetic and copies ran while one was open for 0% of the time, Pallas kernels for 3%

profile of v6, /device:TPU:70, one launch (start us, length us, event | category | flops | bytes accessed | tf_op | source)
XLA Modules:
  0.0 131.1 jit_solution(333197824121326894)
XLA Ops:
  0.6 3.2 %shard_map.113 = (bf16[8,128,768]{2,1,0:T(8,128)(2,1)}, bf16[2,112,128]{2,1,0:T(8,128)(2,1)}) custom-call(s32[4,128]{1,0:T(4,128)} %bitcast.5, s32[1,128]{1,0:T(1,128)} %bitcast.6, bf16[256,1024]{1,0:T(8,128)(2,1)} %table_ref.1, bf16[1024,256]{1,0:T(8,128)(2,1)} %wq.1, bf16[1024,256]{1,0:T(8,128)(2,1)} %wk.1, bf16[1024,256]{1,0:T(8,128)(2,1)} %wv.1, ...), custom_call_target="tpu_custom_call" | custom-call | flops 268435456 | bytes 4194304 | tf_op jit(solution)/shard_map/pallas_call | solution.py:287
  3.8 7.5 %all-to-all-start = ((bf16[8,128,768]{2,1,0:T(8,128)(2,1)}), bf16[8,128,768]{2,1,0:T(8,128)(2,1)S(1)}, u32[]{:S(2)}, u32[]{:S(2)}) async-start(bf16[8,128,768]{2,1,0:T(8,128)(2,1)} %get-tuple-element.9), calls=%async_computation | async-start | bytes 3145728 | tf_op jit(solution)/shard_map/all_to_all | solution.py:354
  11.3 15.5 %collective-permute-start.1 = (bf16[2,112,128]{2,1,0:T(8,128)(2,1)S(1)}, bf16[2,112,128]{2,1,0:T(8,128)(2,1)S(1)}, u32[]{:S(2)}, u32[]{:S(2)}) collective-permute-start(bf16[2,112,128]{2,1,0:T(8,128)(2,1)S(1)} %copy-done.2), channel_id=1, source_target_pairs={{0,128},{1,192},{2,0},{3,64},{4,384},{5,448},{6,256},{7,320},{16,1... | collective-permute-start | bytes 172040 | tf_op jit(solution)/shard_map/ppermute | solution.py:353
  26.9 3.9 %collective-permute-done.1 = bf16[2,112,128]{2,1,0:T(8,128)(2,1)S(1)} collective-permute-done((bf16[2,112,128]{2,1,0:T(8,128)(2,1)S(1)}, bf16[2,112,128]{2,1,0:T(8,128)(2,1)S(1)}, u32[]{:S(2)}, u32[]{:S(2)}) %collective-permute-start.1) | collective-permute-done | bytes 57376 | tf_op jit(solution)/shard_map/ppermute | solution.py:353
  30.8 1.9 %all-to-all-done.refs_0_ = bf16[8,128,768]{2,1,0:T(8,128)(2,1)S(1)} async-done(((bf16[8,128,768]{2,1,0:T(8,128)(2,1)}), bf16[8,128,768]{2,1,0:T(8,128)(2,1)S(1)}, u32[]{:S(2)}, u32[]{:S(2)}) %all-to-all-start) | async-done | bytes 1572896 | tf_op jit(solution)/shard_map/all_to_all | solution.py:354
  32.7 1.1 broadcast_in_dim.2
  33.8 12.4 %all-to-all-start.1 = ((bf16[32,112,128]{2,1,0:T(8,128)(2,1)}), bf16[32,112,128]{2,1,0:T(8,128)(2,1)S(1)}, u32[]{:S(2)}, u32[]{:S(2)}) async-start(bf16[32,112,128]{2,1,0:T(8,128)(2,1)} %bitcast.2), calls=%async_computation.1 | async-start | bytes 1835008 | tf_op jit(solution)/shard_map/all_to_all | solution.py:357
  46.2 1.9 %collective-permute-start = (bf16[8,128,768]{2,1,0:T(8,128)(2,1)S(1)}, bf16[8,128,768]{2,1,0:T(8,128)(2,1)}, u32[]{:S(2)}, u32[]{:S(2)}) collective-permute-start(bf16[8,128,768]{2,1,0:T(8,128)(2,1)S(1)} %all-to-all-done.refs_0_), channel_id=1, source_target_pairs={{0,8},{8,0},{1,9},{9,1},{2,10},{10,2},{3,11},{11,3},{4,12},{12,4},... | collective-permute-start | bytes 4718600 | tf_op jit(solution)/shard_map/ppermute | solution.py:355
  48.1 10.9 %all-to-all-done.1.refs_2_ = bf16[32,112,128]{2,1,0:T(8,128)(2,1)S(1)} async-done(((bf16[32,112,128]{2,1,0:T(8,128)(2,1)}), bf16[32,112,128]{2,1,0:T(8,128)(2,1)S(1)}, u32[]{:S(2)}, u32[]{:S(2)}) %all-to-all-start.1) | async-done | bytes 917536 | tf_op jit(solution)/shard_map/all_to_all | solution.py:357
  59.0 1.9 %collective-permute-start.2 = (bf16[32,112,128]{2,1,0:T(8,128)(2,1)S(1)}, bf16[32,112,128]{2,1,0:T(8,128)(2,1)S(1)}, u32[]{:S(2)}, u32[]{:S(2)}) collective-permute-start(bf16[32,112,128]{2,1,0:T(8,128)(2,1)S(1)} %all-to-all-done.1.refs_2_), channel_id=1, source_target_pairs={{0,8},{8,0},{1,9},{9,1},{2,10},{10,2},{3,11},{11,3},{4,12},{12,4},... | collective-permute-start | bytes 2752520 | tf_op jit(solution)/shard_map/ppermute | solution.py:358
  60.9 2.4 %collective-permute-done.2.refs_3_ = bf16[32,112,128]{2,1,0:T(8,128)(2,1)S(1)} collective-permute-done((bf16[32,112,128]{2,1,0:T(8,128)(2,1)S(1)}, bf16[32,112,128]{2,1,0:T(8,128)(2,1)S(1)}, u32[]{:S(2)}, u32[]{:S(2)}) %collective-permute-start.2) | collective-permute-done | bytes 917536 | tf_op jit(solution)/shard_map/ppermute | solution.py:358
  63.3 7.3 %shard_map.114 = (bf16[256,128]{1,0:T(8,128)(2,1)S(1)}, bf16[8,256,256]{2,1,0:T(8,128)(2,1)S(1)}) custom-call(bf16[8,128,768]{2,1,0:T(8,128)(2,1)S(1)} %all-to-all-done.refs_0_, bf16[8,128,768]{2,1,0:T(8,128)(2,1)} %collective-permute-done.refs_1_, bf16[32,112,128]{2,1,0:T(8,128)(2,1)S(1)} %all-to-all-done.1.refs_2_, ...), custom_call_target="tpu_custom_call" | custom-call | flops 1073741824 | bytes 4194304 | tf_op jit(solution)/shard_map/pallas_call | solution.py:287
  70.7 1.0 copy-done
  71.6 5.3 %all-to-all-start.2 = ((bf16[8,256,256]{2,1,0:T(8,128)(2,1)}), bf16[8,256,256]{2,1,0:T(8,128)(2,1)}, u32[]{:S(2)}, u32[]{:S(2)}) async-start(bf16[8,256,256]{2,1,0:T(8,128)(2,1)} %copy-done), calls=%async_computation.2 | async-start | bytes 2097152 | tf_op jit(solution)/shard_map/all_to_all | solution.py:362
  77.0 3.1 %collective-permute-start.3 = (bf16[256,128]{1,0:T(8,128)(2,1)S(1)}, bf16[256,128]{1,0:T(8,128)(2,1)S(1)}, u32[]{:S(2)}, u32[]{:S(2)}) collective-permute-start(bf16[256,128]{1,0:T(8,128)(2,1)S(1)} %get-tuple-element.12.q_own), channel_id=1, source_target_pairs={{0,16},{16,0},{1,17},{17,1},{2,18},{18,2},{3,19},{19,3},{4,20},{20... | collective-permute-start | bytes 196616 | tf_op jit(solution)/shard_map/ppermute | solution.py:361
  80.0 3.4 %shard_map.115 = bf16[128,256]{1,0:T(8,128)(2,1)} custom-call(bf16[8,128,768]{2,1,0:T(8,128)(2,1)S(1)} %all-to-all-done.refs_0_, bf16[8,128,768]{2,1,0:T(8,128)(2,1)} %collective-permute-done.refs_1_, bf16[32,112,128]{2,1,0:T(8,128)(2,1)S(1)} %all-to-all-done.1.refs_2_, bf16[32,112,128]{2,1,0:T(8,128)(2,1)S(1)} %collective-permute-done.2.refs_3_), custom_call_target="tpu_custom_call" | custom-call | flops 67108864 | bytes 4194304 | tf_op jit(solution)/shard_map/pallas_call | solution.py:287
  83.4 8.0 %collective-permute-done.3.q_other = bf16[256,128]{1,0:T(8,128)(2,1)S(1)} collective-permute-done((bf16[256,128]{1,0:T(8,128)(2,1)S(1)}, bf16[256,128]{1,0:T(8,128)(2,1)S(1)}, u32[]{:S(2)}, u32[]{:S(2)}) %collective-permute-start.3) | collective-permute-done | bytes 65568 | tf_op jit(solution)/shard_map/ppermute | solution.py:361
  91.4 1.5 %all-to-all-done.2.kv_own = bf16[8,256,256]{2,1,0:T(8,128)(2,1)} async-done(((bf16[8,256,256]{2,1,0:T(8,128)(2,1)}), bf16[8,256,256]{2,1,0:T(8,128)(2,1)}, u32[]{:S(2)}, u32[]{:S(2)}) %all-to-all-start.2) | async-done | bytes 1048608 | tf_op jit(solution)/shard_map/all_to_all | solution.py:362
  92.9 1.9 %collective-permute-start.4 = (bf16[8,256,256]{2,1,0:T(8,128)(2,1)}, bf16[8,256,256]{2,1,0:T(8,128)(2,1)S(1)}, u32[]{:S(2)}, u32[]{:S(2)}) collective-permute-start(bf16[8,256,256]{2,1,0:T(8,128)(2,1)} %all-to-all-done.2.kv_own), channel_id=1, source_target_pairs={{0,8},{8,0},{1,9},{9,1},{2,10},{10,2},{3,11},{11,3},{4,12},{12,4},... | collective-permute-start | bytes 3145736 | tf_op jit(solution)/shard_map/ppermute | solution.py:365
  94.8 2.8 %collective-permute-done.4.kv_other = bf16[8,256,256]{2,1,0:T(8,128)(2,1)S(1)} collective-permute-done((bf16[8,256,256]{2,1,0:T(8,128)(2,1)}, bf16[8,256,256]{2,1,0:T(8,128)(2,1)S(1)}, u32[]{:S(2)}, u32[]{:S(2)}) %collective-permute-start.4) | collective-permute-done | bytes 1048608 | tf_op jit(solution)/shard_map/ppermute | solution.py:365
  97.6 3.9 %shard_map.116 = f32[4,136,128]{2,1,0:T(8,128)S(1)} custom-call(bf16[256,128]{1,0:T(8,128)(2,1)S(1)} %get-tuple-element.12.q_own, bf16[256,128]{1,0:T(8,128)(2,1)S(1)} %collective-permute-done.3.q_other, bf16[8,256,256]{2,1,0:T(8,128)(2,1)} %all-to-all-done.2.kv_own, bf16[8,256,256]{2,1,0:T(8,128)(2,1)S(1)} %collective-permute-done.4.kv_other), custom_call_target="tpu_custom_call" | custom-call | flops 1073741824 | bytes 4194304 | tf_op jit(solution)/shard_map/pallas_call | solution.py:287
  101.5 9.3 %all_to_all.20.part_ref = f32[4,136,128]{2,1,0:T(8,128)S(1)} all-to-all(f32[4,136,128]{2,1,0:T(8,128)S(1)} %shard_map.116), channel_id=1, replica_groups=mesh['zh'=8,'zl'=2,'yl'=2,'c'=2,'x'=4,'yh'=2] {'zl','yl'}, dimensions={0} | all-to-all | bytes 557056 | tf_op jit(solution)/shard_map/all_to_all | solution.py:367
  111.0 13.0 %collective-permute-start.5 = (bf16[128,256]{1,0:T(8,128)(2,1)S(1)}, bf16[128,256]{1,0:T(8,128)(2,1)S(1)}, u32[]{:S(2)}, u32[]{:S(2)}) collective-permute-start(bf16[128,256]{1,0:T(8,128)(2,1)S(1)} %shard_map.117), channel_id=1, source_target_pairs={{128,0},{192,1},{0,2},{64,3},{384,4},{448,5},{256,6},{320,7},{151,... | collective-permute-start | bytes 196616 | tf_op jit(solution)/shard_map/ppermute | solution.py:368
  124.0 6.5 %collective-permute-done.5 = bf16[128,256]{1,0:T(8,128)(2,1)S(1)} collective-permute-done((bf16[128,256]{1,0:T(8,128)(2,1)S(1)}, bf16[128,256]{1,0:T(8,128)(2,1)S(1)}, u32[]{:S(2)}, u32[]{:S(2)}) %collective-permute-start.5) | collective-permute-done | bytes 65568 | tf_op jit(solution)/shard_map/ppermute | solution.py:368
  (8 shorter events, 0.9 us)
Async XLA Ops:
  3.8 7.5 %copy-start.2 = (bf16[2,112,128]{2,1,0:T(8,128)(2,1)S(1)}, bf16[2,112,128]{2,1,0:T(8,128)(2,1)}, u32[]{:S(2)}) copy-start(bf16[2,112,128]{2,1,0:T(8,128)(2,1)} %get-tuple-element.10) | copy-start | bytes 172036
  3.8 28.9 %all-to-all-start = ((bf16[8,128,768]{2,1,0:T(8,128)(2,1)}), bf16[8,128,768]{2,1,0:T(8,128)(2,1)S(1)}, u32[]{:S(2)}, u32[]{:S(2)}) async-start(bf16[8,128,768]{2,1,0:T(8,128)(2,1)} %get-tuple-element.9), calls=%async_computation | async-start | bytes 3145728 | tf_op jit(solution)/shard_map/all_to_all | solution.py:354
  11.3 52.0 %copy-start.1 = (f32[2048]{0:T(1024)S(1)}, f32[2048]{0:T(1024)}, u32[]{:S(2)}) copy-start(f32[2048]{0:T(1024)} %param.16) | copy-start | bytes 24580
  11.3 19.4 %collective-permute-start.1 = (bf16[2,112,128]{2,1,0:T(8,128)(2,1)S(1)}, bf16[2,112,128]{2,1,0:T(8,128)(2,1)S(1)}, u32[]{:S(2)}, u32[]{:S(2)}) collective-permute-start(bf16[2,112,128]{2,1,0:T(8,128)(2,1)S(1)} %copy-done.2), channel_id=1, source_target_pairs={{0,128},{1,192},{2,0},{3,64},{4,384},{5,448},{6,256},{7,320},{16,1... | collective-permute-start | bytes 172040 | tf_op jit(solution)/shard_map/ppermute | solution.py:353
  33.8 25.2 %all-to-all-start.1 = ((bf16[32,112,128]{2,1,0:T(8,128)(2,1)}), bf16[32,112,128]{2,1,0:T(8,128)(2,1)S(1)}, u32[]{:S(2)}, u32[]{:S(2)}) async-start(bf16[32,112,128]{2,1,0:T(8,128)(2,1)} %bitcast.2), calls=%async_computation.1 | async-start | bytes 1835008 | tf_op jit(solution)/shard_map/all_to_all | solution.py:357
  46.2 14.7 %collective-permute-start = (bf16[8,128,768]{2,1,0:T(8,128)(2,1)S(1)}, bf16[8,128,768]{2,1,0:T(8,128)(2,1)}, u32[]{:S(2)}, u32[]{:S(2)}) collective-permute-start(bf16[8,128,768]{2,1,0:T(8,128)(2,1)S(1)} %all-to-all-done.refs_0_), channel_id=1, source_target_pairs={{0,8},{8,0},{1,9},{9,1},{2,10},{10,2},{3,11},{11,3},{4,12},{12,4},... | collective-permute-start | bytes 4718600 | tf_op jit(solution)/shard_map/ppermute | solution.py:355
  59.0 4.4 %collective-permute-start.2 = (bf16[32,112,128]{2,1,0:T(8,128)(2,1)S(1)}, bf16[32,112,128]{2,1,0:T(8,128)(2,1)S(1)}, u32[]{:S(2)}, u32[]{:S(2)}) collective-permute-start(bf16[32,112,128]{2,1,0:T(8,128)(2,1)S(1)} %all-to-all-done.1.refs_2_), channel_id=1, source_target_pairs={{0,8},{8,0},{1,9},{9,1},{2,10},{10,2},{3,11},{11,3},{4,12},{12,4},... | collective-permute-start | bytes 2752520 | tf_op jit(solution)/shard_map/ppermute | solution.py:358
  70.7 1.0 copy-start
  71.6 21.2 %all-to-all-start.2 = ((bf16[8,256,256]{2,1,0:T(8,128)(2,1)}), bf16[8,256,256]{2,1,0:T(8,128)(2,1)}, u32[]{:S(2)}, u32[]{:S(2)}) async-start(bf16[8,256,256]{2,1,0:T(8,128)(2,1)} %copy-done), calls=%async_computation.2 | async-start | bytes 2097152 | tf_op jit(solution)/shard_map/all_to_all | solution.py:362
  77.0 14.4 %collective-permute-start.3 = (bf16[256,128]{1,0:T(8,128)(2,1)S(1)}, bf16[256,128]{1,0:T(8,128)(2,1)S(1)}, u32[]{:S(2)}, u32[]{:S(2)}) collective-permute-start(bf16[256,128]{1,0:T(8,128)(2,1)S(1)} %get-tuple-element.12.q_own), channel_id=1, source_target_pairs={{0,16},{16,0},{1,17},{17,1},{2,18},{18,2},{3,19},{19,3},{4,20},{20... | collective-permute-start | bytes 196616 | tf_op jit(solution)/shard_map/ppermute | solution.py:361
  92.9 4.8 %collective-permute-start.4 = (bf16[8,256,256]{2,1,0:T(8,128)(2,1)}, bf16[8,256,256]{2,1,0:T(8,128)(2,1)S(1)}, u32[]{:S(2)}, u32[]{:S(2)}) collective-permute-start(bf16[8,256,256]{2,1,0:T(8,128)(2,1)} %all-to-all-done.2.kv_own), channel_id=1, source_target_pairs={{0,8},{8,0},{1,9},{9,1},{2,10},{10,2},{3,11},{11,3},{4,12},{12,4},... | collective-permute-start | bytes 3145736 | tf_op jit(solution)/shard_map/ppermute | solution.py:365
  111.0 19.5 %collective-permute-start.5 = (bf16[128,256]{1,0:T(8,128)(2,1)S(1)}, bf16[128,256]{1,0:T(8,128)(2,1)S(1)}, u32[]{:S(2)}, u32[]{:S(2)}) collective-permute-start(bf16[128,256]{1,0:T(8,128)(2,1)S(1)} %shard_map.117), channel_id=1, source_target_pairs={{128,0},{192,1},{0,2},{64,3},{384,4},{448,5},{256,6},{320,7},{151,... | collective-permute-start | bytes 196616 | tf_op jit(solution)/shard_map/ppermute | solution.py:368

commit v7 on v6

--- a/solution.py
+++ b/solution.py
@@ -19,7 +19,7 @@
 VALUES = 128
 ROWS = 3 * W_ROWS
 MSG = ROWS + 16
-PART = P_DEV + 8
+PART = P_DEV + 16
 VMEM = 20 * 1024 * 1024
 
 Z = ("zh", "zl")
@@ -264,21 +264,27 @@
         rows = slice(b * P_DEV, (b + 1) * P_DEV)
         for q_yl in range(2):
             slot = 2 * b + q_yl
-            out_ref[slot, :P_DEV, :] = accs[q_yl, rows, :]
             total = jnp.sum(norms[q_yl, rows, :], axis=-1, keepdims=True)
-            stats = [as_row(tops[q_yl, rows, :1]), as_row(total), jnp.zeros((6, HD), jnp.float32)]
-            out_ref[slot, P_DEV:, :] = jnp.concatenate(stats, axis=0)
+            out_ref[slot, :P_DEV, :] = (accs[q_yl, rows, :] / total).astype(jnp.bfloat16)
+            rest = as_row(tops[q_yl, rows, :1] + jnp.log2(total))
+            pieces = []
+            for _ in range(3):
+                pieces.append(rest.astype(jnp.bfloat16).astype(jnp.float32))
+                rest = rest - pieces[-1]
+            pieces.append(jnp.zeros((13, HD), jnp.float32))
+            out_ref[slot, P_DEV:, :] = jnp.concatenate(pieces, axis=0).astype(jnp.bfloat16)
 
 
 def join_kernel(part_ref, out_ref):
     for a in range(2):
-        slots = (2 * a, 2 * a + 1)
-        tops = [as_column(part_ref[i, P_DEV : P_DEV + 1, :]) for i in slots]
-        sums = [as_column(part_ref[i, P_DEV + 1 : P_DEV + 2, :]) for i in slots]
-        top = jnp.maximum(*tops)
-        scale = [jnp.exp2(part - top) for part in tops]
-        mixed = part_ref[slots[0], :P_DEV, :] * scale[0] + part_ref[slots[1], :P_DEV, :] * scale[1]
-        mixed = mixed / (sums[0] * scale[0] + sums[1] * scale[1])
+        parts, logs = [], []
+        for i in (2 * a, 2 * a + 1):
+            parts.append(part_ref[i, :P_DEV, :].astype(jnp.float32))
+            tail = part_ref[i, P_DEV:, :].astype(jnp.float32)
+            logs.append(as_column(tail[0:1, :] + tail[1:2, :] + tail[2:3, :]))
+        top = jnp.maximum(*logs)
+        scale = [jnp.exp2(log - top) for log in logs]
+        mixed = (parts[0] * scale[0] + parts[1] * scale[1]) / (scale[0] + scale[1])
         out_ref[:, a * HD : (a + 1) * HD] = mixed.astype(jnp.bfloat16)
 
 
@@ -317,7 +323,7 @@
     size = 2 * P_DEV
     block = (2, size, HD)
     scratch = [((N_TP + 1, 2, size, size), F32), (block, BF)] + [(block, F32)] * 3
-    return call(attend_kernel, [((4, PART, HD), F32)], scratch, 1 << 30, *args)[0]
+    return call(attend_kernel, [((4, PART, HD), BF)], scratch, 1 << 30, *args)[0]
 
 
 def run_join(*args):

time: 132 us -> 130 us (0.985)
  the two profiles are of different devices: /device:TPU:70 before, /device:TPU:8 now
where the time goes in v7:
time: 130 us
  starting transfers between devices  54.2 us (42%)
  waiting for transfers between devices  46.4 us (36%)
  Pallas kernels  18 us (14%)
  blocking collectives  7.63 us (6%)
  local copies, waits for them, and re-layouts  2.65 us (2%)
    pallas_call x5, Pallas kernels, call(): pl.pallas_call(body, out_shape=[jax.ShapeDtypeStruct(shape, dtype) for sh...  18 us
    ppermute x1, starting transfers between devices, on_device(): message = lax.ppermute(message, TURN, turn)  14.3 us
    all_to_all x1, waiting for transfers between devices, on_device(): msg_own = lax.all_to_all(message, PLANES, 0, 0, tiled=True)  11.2 us
    all_to_all x1, starting transfers between devices, on_device(): msg_own = lax.all_to_all(message, PLANES, 0, 0, tiled=True)  10.6 us
    ppermute x1, starting transfers between devices, on_device(): lax.ppermute(mixed, TURN, [(target, source) for source, target in turn])  10.4 us
    ppermute x1, waiting for transfers between devices, on_device(): lax.ppermute(mixed, TURN, [(target, source) for source, target in turn])  9.52 us
    all_to_all x1, blocking collectives, on_device(): mixed = run_join(lax.all_to_all(parts, PAIR, 0, 0))  7.63 us
    ppermute x1, waiting for transfers between devices, on_device(): message = lax.ppermute(message, TURN, turn)  6.74 us
  transfers between devices with their start and end apart: 9, of which 8 were waited for; matrix products, arithmetic and copies ran while one was open for 0% of the time, Pallas kernels for 3%

profile of v7, /device:TPU:8, one launch (start us, length us, event | category | flops | bytes accessed | tf_op | source)
XLA Modules:
  0.0 129.6 jit_solution(6096063165605693)
XLA Ops:
  0.6 3.2 %shard_map.113 = (bf16[8,128,768]{2,1,0:T(8,128)(2,1)}, bf16[2,112,128]{2,1,0:T(8,128)(2,1)}) custom-call(s32[4,128]{1,0:T(4,128)} %bitcast.5, s32[1,128]{1,0:T(1,128)} %bitcast.6, bf16[256,1024]{1,0:T(8,128)(2,1)} %table_ref.1, bf16[1024,256]{1,0:T(8,128)(2,1)} %wq.1, bf16[1024,256]{1,0:T(8,128)(2,1)} %wk.1, bf16[1024,256]{1,0:T(8,128)(2,1)} %wv.1, ...), custom_call_target="tpu_custom_call" | custom-call | flops 268435456 | bytes 4194304 | tf_op jit(solution)/shard_map/pallas_call | solution.py:293
  3.8 6.2 %all-to-all-start = ((bf16[8,128,768]{2,1,0:T(8,128)(2,1)}), bf16[8,128,768]{2,1,0:T(8,128)(2,1)S(1)}, u32[]{:S(2)}, u32[]{:S(2)}) async-start(bf16[8,128,768]{2,1,0:T(8,128)(2,1)} %get-tuple-element.9), calls=%async_computation | async-start | bytes 3145728 | tf_op jit(solution)/shard_map/all_to_all | solution.py:360
  10.0 14.3 %collective-permute-start.1 = (bf16[2,112,128]{2,1,0:T(8,128)(2,1)S(1)}, bf16[2,112,128]{2,1,0:T(8,128)(2,1)S(1)}, u32[]{:S(2)}, u32[]{:S(2)}) collective-permute-start(bf16[2,112,128]{2,1,0:T(8,128)(2,1)S(1)} %copy-done.2), channel_id=1, source_target_pairs={{0,128},{1,192},{2,0},{3,64},{4,384},{5,448},{6,256},{7,320},{16,1... | collective-permute-start | bytes 172040 | tf_op jit(solution)/shard_map/ppermute | solution.py:359
  24.3 6.7 %collective-permute-done.1 = bf16[2,112,128]{2,1,0:T(8,128)(2,1)S(1)} collective-permute-done((bf16[2,112,128]{2,1,0:T(8,128)(2,1)S(1)}, bf16[2,112,128]{2,1,0:T(8,128)(2,1)S(1)}, u32[]{:S(2)}, u32[]{:S(2)}) %collective-permute-start.1) | collective-permute-done | bytes 57376 | tf_op jit(solution)/shard_map/ppermute | solution.py:359
  31.0 2.6 %all-to-all-done.refs_0_ = bf16[8,128,768]{2,1,0:T(8,128)(2,1)S(1)} async-done(((bf16[8,128,768]{2,1,0:T(8,128)(2,1)}), bf16[8,128,768]{2,1,0:T(8,128)(2,1)S(1)}, u32[]{:S(2)}, u32[]{:S(2)}) %all-to-all-start) | async-done | bytes 1572896 | tf_op jit(solution)/shard_map/all_to_all | solution.py:360
  33.7 1.1 broadcast_in_dim.2
  34.7 10.6 %all-to-all-start.1 = ((bf16[32,112,128]{2,1,0:T(8,128)(2,1)}), bf16[32,112,128]{2,1,0:T(8,128)(2,1)S(1)}, u32[]{:S(2)}, u32[]{:S(2)}) async-start(bf16[32,112,128]{2,1,0:T(8,128)(2,1)} %bitcast.2), calls=%async_computation.1 | async-start | bytes 1835008 | tf_op jit(solution)/shard_map/all_to_all | solution.py:363
  45.3 1.9 %collective-permute-start = (bf16[8,128,768]{2,1,0:T(8,128)(2,1)S(1)}, bf16[8,128,768]{2,1,0:T(8,128)(2,1)}, u32[]{:S(2)}, u32[]{:S(2)}) collective-permute-start(bf16[8,128,768]{2,1,0:T(8,128)(2,1)S(1)} %all-to-all-done.refs_0_), channel_id=1, source_target_pairs={{0,8},{8,0},{1,9},{9,1},{2,10},{10,2},{3,11},{11,3},{4,12},{12,4},... | collective-permute-start | bytes 4718600 | tf_op jit(solution)/shard_map/ppermute | solution.py:361
  47.3 11.2 %all-to-all-done.1.refs_2_ = bf16[32,112,128]{2,1,0:T(8,128)(2,1)S(1)} async-done(((bf16[32,112,128]{2,1,0:T(8,128)(2,1)}), bf16[32,112,128]{2,1,0:T(8,128)(2,1)S(1)}, u32[]{:S(2)}, u32[]{:S(2)}) %all-to-all-start.1) | async-done | bytes 917536 | tf_op jit(solution)/shard_map/all_to_all | solution.py:363
  58.5 1.9 %collective-permute-start.2 = (bf16[32,112,128]{2,1,0:T(8,128)(2,1)S(1)}, bf16[32,112,128]{2,1,0:T(8,128)(2,1)S(1)}, u32[]{:S(2)}, u32[]{:S(2)}) collective-permute-start(bf16[32,112,128]{2,1,0:T(8,128)(2,1)S(1)} %all-to-all-done.1.refs_2_), channel_id=1, source_target_pairs={{0,8},{8,0},{1,9},{9,1},{2,10},{10,2},{3,11},{11,3},{4,12},{12,4},... | collective-permute-start | bytes 2752520 | tf_op jit(solution)/shard_map/ppermute | solution.py:364
  60.4 2.4 %collective-permute-done.2.refs_3_ = bf16[32,112,128]{2,1,0:T(8,128)(2,1)S(1)} collective-permute-done((bf16[32,112,128]{2,1,0:T(8,128)(2,1)S(1)}, bf16[32,112,128]{2,1,0:T(8,128)(2,1)S(1)}, u32[]{:S(2)}, u32[]{:S(2)}) %collective-permute-start.2) | collective-permute-done | bytes 917536 | tf_op jit(solution)/shard_map/ppermute | solution.py:364
  62.8 7.3 %shard_map.114 = (bf16[256,128]{1,0:T(8,128)(2,1)S(1)}, bf16[8,256,256]{2,1,0:T(8,128)(2,1)S(1)}) custom-call(bf16[8,128,768]{2,1,0:T(8,128)(2,1)S(1)} %all-to-all-done.refs_0_, bf16[8,128,768]{2,1,0:T(8,128)(2,1)} %collective-permute-done.refs_1_, bf16[32,112,128]{2,1,0:T(8,128)(2,1)S(1)} %all-to-all-done.1.refs_2_, ...), custom_call_target="tpu_custom_call" | custom-call | flops 1073741824 | bytes 4194304 | tf_op jit(solution)/shard_map/pallas_call | solution.py:293
  70.2 1.0 copy-done
  71.1 4.2 %all-to-all-start.2 = ((bf16[8,256,256]{2,1,0:T(8,128)(2,1)}), bf16[8,256,256]{2,1,0:T(8,128)(2,1)}, u32[]{:S(2)}, u32[]{:S(2)}) async-start(bf16[8,256,256]{2,1,0:T(8,128)(2,1)} %copy-done), calls=%async_computation.2 | async-start | bytes 2097152 | tf_op jit(solution)/shard_map/all_to_all | solution.py:368
  75.4 2.8 %collective-permute-start.3 = (bf16[256,128]{1,0:T(8,128)(2,1)S(1)}, bf16[256,128]{1,0:T(8,128)(2,1)S(1)}, u32[]{:S(2)}, u32[]{:S(2)}) collective-permute-start(bf16[256,128]{1,0:T(8,128)(2,1)S(1)} %get-tuple-element.12.q_own), channel_id=1, source_target_pairs={{0,16},{16,0},{1,17},{17,1},{2,18},{18,2},{3,19},{19,3},{4,20},{20... | collective-permute-start | bytes 196616 | tf_op jit(solution)/shard_map/ppermute | solution.py:367
  78.2 3.4 %shard_map.115 = bf16[128,256]{1,0:T(8,128)(2,1)} custom-call(bf16[8,128,768]{2,1,0:T(8,128)(2,1)S(1)} %all-to-all-done.refs_0_, bf16[8,128,768]{2,1,0:T(8,128)(2,1)} %collective-permute-done.refs_1_, bf16[32,112,128]{2,1,0:T(8,128)(2,1)S(1)} %all-to-all-done.1.refs_2_, bf16[32,112,128]{2,1,0:T(8,128)(2,1)S(1)} %collective-permute-done.2.refs_3_), custom_call_target="tpu_custom_call" | custom-call | flops 67108864 | bytes 4194304 | tf_op jit(solution)/shard_map/pallas_call | solution.py:293
  81.6 6.5 %collective-permute-done.3.q_other = bf16[256,128]{1,0:T(8,128)(2,1)S(1)} collective-permute-done((bf16[256,128]{1,0:T(8,128)(2,1)S(1)}, bf16[256,128]{1,0:T(8,128)(2,1)S(1)}, u32[]{:S(2)}, u32[]{:S(2)}) %collective-permute-start.3) | collective-permute-done | bytes 65568 | tf_op jit(solution)/shard_map/ppermute | solution.py:367
  88.1 4.5 %all-to-all-done.2.kv_own = bf16[8,256,256]{2,1,0:T(8,128)(2,1)} async-done(((bf16[8,256,256]{2,1,0:T(8,128)(2,1)}), bf16[8,256,256]{2,1,0:T(8,128)(2,1)}, u32[]{:S(2)}, u32[]{:S(2)}) %all-to-all-start.2) | async-done | bytes 1048608 | tf_op jit(solution)/shard_map/all_to_all | solution.py:368
  92.6 1.9 %collective-permute-start.4 = (bf16[8,256,256]{2,1,0:T(8,128)(2,1)}, bf16[8,256,256]{2,1,0:T(8,128)(2,1)S(1)}, u32[]{:S(2)}, u32[]{:S(2)}) collective-permute-start(bf16[8,256,256]{2,1,0:T(8,128)(2,1)} %all-to-all-done.2.kv_own), channel_id=1, source_target_pairs={{0,8},{8,0},{1,9},{9,1},{2,10},{10,2},{3,11},{11,3},{4,12},{12,4},... | collective-permute-start | bytes 3145736 | tf_op jit(solution)/shard_map/ppermute | solution.py:371
  94.5 2.8 %collective-permute-done.4.kv_other = bf16[8,256,256]{2,1,0:T(8,128)(2,1)S(1)} collective-permute-done((bf16[8,256,256]{2,1,0:T(8,128)(2,1)}, bf16[8,256,256]{2,1,0:T(8,128)(2,1)S(1)}, u32[]{:S(2)}, u32[]{:S(2)}) %collective-permute-start.4) | collective-permute-done | bytes 1048608 | tf_op jit(solution)/shard_map/ppermute | solution.py:371
  97.3 3.9 %shard_map.116 = bf16[4,144,128]{2,1,0:T(8,128)(2,1)S(1)} custom-call(bf16[256,128]{1,0:T(8,128)(2,1)S(1)} %get-tuple-element.12.q_own, bf16[256,128]{1,0:T(8,128)(2,1)S(1)} %collective-permute-done.3.q_other, bf16[8,256,256]{2,1,0:T(8,128)(2,1)} %all-to-all-done.2.kv_own, bf16[8,256,256]{2,1,0:T(8,128)(2,1)S(1)} %collective-permute-done.4.kv_other), custom_call_target="tpu_custom_call" | custom-call | flops 1073741824 | bytes 4194304 | tf_op jit(solution)/shard_map/pallas_call | solution.py:293
  101.2 7.6 %all_to_all.20.part_ref = bf16[4,144,128]{2,1,0:T(8,128)(2,1)S(1)} all-to-all(bf16[4,144,128]{2,1,0:T(8,128)(2,1)S(1)} %shard_map.116), channel_id=1, replica_groups=mesh['zh'=8,'zl'=2,'yl'=2,'c'=2,'x'=4,'yh'=2] {'zl','yl'}, dimensions={0} | all-to-all | bytes 294912 | tf_op jit(solution)/shard_map/all_to_all | solution.py:373
  109.1 10.4 %collective-permute-start.5 = (bf16[128,256]{1,0:T(8,128)(2,1)S(1)}, bf16[128,256]{1,0:T(8,128)(2,1)S(1)}, u32[]{:S(2)}, u32[]{:S(2)}) collective-permute-start(bf16[128,256]{1,0:T(8,128)(2,1)S(1)} %shard_map.117), channel_id=1, source_target_pairs={{128,0},{192,1},{0,2},{64,3},{384,4},{448,5},{256,6},{320,7},{151,... | collective-permute-start | bytes 196616 | tf_op jit(solution)/shard_map/ppermute | solution.py:374
  119.4 9.5 %collective-permute-done.5 = bf16[128,256]{1,0:T(8,128)(2,1)S(1)} collective-permute-done((bf16[128,256]{1,0:T(8,128)(2,1)S(1)}, bf16[128,256]{1,0:T(8,128)(2,1)S(1)}, u32[]{:S(2)}, u32[]{:S(2)}) %collective-permute-start.5) | collective-permute-done | bytes 65568 | tf_op jit(solution)/shard_map/ppermute | solution.py:374
  (8 shorter events, 0.8 us)
Async XLA Ops:
  3.8 6.2 %copy-start.2 = (bf16[2,112,128]{2,1,0:T(8,128)(2,1)S(1)}, bf16[2,112,128]{2,1,0:T(8,128)(2,1)}, u32[]{:S(2)}) copy-start(bf16[2,112,128]{2,1,0:T(8,128)(2,1)} %get-tuple-element.10) | copy-start | bytes 172036
  3.8 29.9 %all-to-all-start = ((bf16[8,128,768]{2,1,0:T(8,128)(2,1)}), bf16[8,128,768]{2,1,0:T(8,128)(2,1)S(1)}, u32[]{:S(2)}, u32[]{:S(2)}) async-start(bf16[8,128,768]{2,1,0:T(8,128)(2,1)} %get-tuple-element.9), calls=%async_computation | async-start | bytes 3145728 | tf_op jit(solution)/shard_map/all_to_all | solution.py:360
  10.0 52.9 %copy-start.1 = (f32[2048]{0:T(1024)S(1)}, f32[2048]{0:T(1024)}, u32[]{:S(2)}) copy-start(f32[2048]{0:T(1024)} %param.16) | copy-start | bytes 24580
  10.0 21.0 %collective-permute-start.1 = (bf16[2,112,128]{2,1,0:T(8,128)(2,1)S(1)}, bf16[2,112,128]{2,1,0:T(8,128)(2,1)S(1)}, u32[]{:S(2)}, u32[]{:S(2)}) collective-permute-start(bf16[2,112,128]{2,1,0:T(8,128)(2,1)S(1)} %copy-done.2), channel_id=1, source_target_pairs={{0,128},{1,192},{2,0},{3,64},{4,384},{5,448},{6,256},{7,320},{16,1... | collective-permute-start | bytes 172040 | tf_op jit(solution)/shard_map/ppermute | solution.py:359
  34.7 23.7 %all-to-all-start.1 = ((bf16[32,112,128]{2,1,0:T(8,128)(2,1)}), bf16[32,112,128]{2,1,0:T(8,128)(2,1)S(1)}, u32[]{:S(2)}, u32[]{:S(2)}) async-start(bf16[32,112,128]{2,1,0:T(8,128)(2,1)} %bitcast.2), calls=%async_computation.1 | async-start | bytes 1835008 | tf_op jit(solution)/shard_map/all_to_all | solution.py:363
  45.3 15.0 %collective-permute-start = (bf16[8,128,768]{2,1,0:T(8,128)(2,1)S(1)}, bf16[8,128,768]{2,1,0:T(8,128)(2,1)}, u32[]{:S(2)}, u32[]{:S(2)}) collective-permute-start(bf16[8,128,768]{2,1,0:T(8,128)(2,1)S(1)} %all-to-all-done.refs_0_), channel_id=1, source_target_pairs={{0,8},{8,0},{1,9},{9,1},{2,10},{10,2},{3,11},{11,3},{4,12},{12,4},... | collective-permute-start | bytes 4718600 | tf_op jit(solution)/shard_map/ppermute | solution.py:361
  58.5 4.4 %collective-permute-start.2 = (bf16[32,112,128]{2,1,0:T(8,128)(2,1)S(1)}, bf16[32,112,128]{2,1,0:T(8,128)(2,1)S(1)}, u32[]{:S(2)}, u32[]{:S(2)}) collective-permute-start(bf16[32,112,128]{2,1,0:T(8,128)(2,1)S(1)} %all-to-all-done.1.refs_2_), channel_id=1, source_target_pairs={{0,8},{8,0},{1,9},{9,1},{2,10},{10,2},{3,11},{11,3},{4,12},{12,4},... | collective-permute-start | bytes 2752520 | tf_op jit(solution)/shard_map/ppermute | solution.py:364
  70.2 1.0 copy-start
  71.1 21.4 %all-to-all-start.2 = ((bf16[8,256,256]{2,1,0:T(8,128)(2,1)}), bf16[8,256,256]{2,1,0:T(8,128)(2,1)}, u32[]{:S(2)}, u32[]{:S(2)}) async-start(bf16[8,256,256]{2,1,0:T(8,128)(2,1)} %copy-done), calls=%async_computation.2 | async-start | bytes 2097152 | tf_op jit(solution)/shard_map/all_to_all | solution.py:368
  75.4 12.7 %collective-permute-start.3 = (bf16[256,128]{1,0:T(8,128)(2,1)S(1)}, bf16[256,128]{1,0:T(8,128)(2,1)S(1)}, u32[]{:S(2)}, u32[]{:S(2)}) collective-permute-start(bf16[256,128]{1,0:T(8,128)(2,1)S(1)} %get-tuple-element.12.q_own), channel_id=1, source_target_pairs={{0,16},{16,0},{1,17},{17,1},{2,18},{18,2},{3,19},{19,3},{4,20},{20... | collective-permute-start | bytes 196616 | tf_op jit(solution)/shard_map/ppermute | solution.py:367
  92.6 4.8 %collective-permute-start.4 = (bf16[8,256,256]{2,1,0:T(8,128)(2,1)}, bf16[8,256,256]{2,1,0:T(8,128)(2,1)S(1)}, u32[]{:S(2)}, u32[]{:S(2)}) collective-permute-start(bf16[8,256,256]{2,1,0:T(8,128)(2,1)} %all-to-all-done.2.kv_own), channel_id=1, source_target_pairs={{0,8},{8,0},{1,9},{9,1},{2,10},{10,2},{3,11},{11,3},{4,12},{12,4},... | collective-permute-start | bytes 3145736 | tf_op jit(solution)/shard_map/ppermute | solution.py:371
  109.1 19.9 %collective-permute-start.5 = (bf16[128,256]{1,0:T(8,128)(2,1)S(1)}, bf16[128,256]{1,0:T(8,128)(2,1)S(1)}, u32[]{:S(2)}, u32[]{:S(2)}) collective-permute-start(bf16[128,256]{1,0:T(8,128)(2,1)S(1)} %shard_map.117), channel_id=1, source_target_pairs={{128,0},{192,1},{0,2},{64,3},{384,4},{448,5},{256,6},{320,7},{151,... | collective-permute-start | bytes 196616 | tf_op jit(solution)/shard_map/ppermute | solution.py:374

commit v8 on v7

--- a/solution.py
+++ b/solution.py
@@ -1,3 +1,4 @@
+import functools
 import math
 
 import jax
@@ -198,25 +199,17 @@
     return jnp.sum(jnp.where(diagonal(), row, 0.0), axis=1, keepdims=True)
 
 
-def attend_kernel(
-    q_own,
-    q_other,
-    kv_own,
-    kv_other,
-    out_ref,
-    scores,
-    query,
-    tops,
-    norms,
-    accs,
-):
+def attend_kernel(last, *refs):
+    q_own, q_other, kv_ref = refs[:3]
+    if last:
+        top_in, norm_in, acc_in, out_ref, scores, query, tops, norms, accs = refs[3:]
+    else:
+        tops, norms, accs, scores, query = refs[3:]
     _, yl, c, t = coordinates()
     size = 2 * P_DEV
     query[yl] = q_own[...]
     query[1 - yl] = q_other[...]
-    tops[...] = jnp.full(tops.shape, NEG, jnp.float32)
-    norms[...] = jnp.zeros(norms.shape, jnp.float32)
-    accs[...] = jnp.zeros(accs.shape, jnp.float32)
+    tops[...] = top_in[...] if last else jnp.full(tops.shape, NEG, jnp.float32)
     row = lax.broadcasted_iota(jnp.int32, (size, size), 0)
     col = lax.broadcasted_iota(jnp.int32, (size, size), 1)
     behind = 512 * (row // P_DEV - col // P_DEV) + row % P_DEV - col % P_DEV
@@ -232,7 +225,7 @@
         first = u <= t
         return jnp.where(first, 0, 1), turned(jnp.where(first, u, u - t - 1), yl)
 
-    sides = ((kv_own, c), (kv_other, 1 - c))
+    sides = ((kv_ref, 1 - c if last else c),)
     for u in range(units):
         q_yl, tt = unit(u)
         best = tops[q_yl]
@@ -247,6 +240,13 @@
         tops[q_yl] = best
     for b in range(2):
         tops[b] = jnp.broadcast_to(jnp.max(tops[b], axis=-1, keepdims=True), (size, HD))
+        if last:
+            scale = jnp.exp2(top_in[b] - tops[b])
+            norms[b] = norm_in[b] * scale
+            accs[b] = acc_in[b] * scale
+        else:
+            norms[b] = jnp.zeros((size, HD), jnp.float32)
+            accs[b] = jnp.zeros((size, HD), jnp.float32)
     for u in range(units):
         q_yl, tt = unit(u)
         top = tops[q_yl]
@@ -260,6 +260,8 @@
             )
         norms[q_yl] = norm
         accs[q_yl] = acc
+    if not last:
+        return
     for b in range(2):
         rows = slice(b * P_DEV, (b + 1) * P_DEV)
         for q_yl in range(2):
@@ -319,11 +321,15 @@
     return call(latent_kernel, [((P_DEV, 256), BF)], [], 1 << 26, *args)[0]
 
 
-def run_attend(*args):
+def run_attend(last, *args):
     size = 2 * P_DEV
     block = (2, size, HD)
-    scratch = [((N_TP + 1, 2, size, size), F32), (block, BF)] + [(block, F32)] * 3
-    return call(attend_kernel, [((4, PART, HD), BF)], scratch, 1 << 30, *args)[0]
+    held = [((N_TP + 1, 1, size, size), F32), (block, BF)]
+    state = [(block, F32)] * 3
+    body = functools.partial(attend_kernel, last)
+    if last:
+        return call(body, [((4, PART, HD), BF)], held + state, 1 << 29, *args)[0]
+    return call(body, state, held, 1 << 29, *args)
 
 
 def run_join(*args):
@@ -369,7 +375,8 @@
     patch_latent = run_latent(*byte_tables, msg_own, msg_other)
     kv_own, q_other, patch_latent = lax.optimization_barrier((kv_own, q_other, patch_latent))
     kv_other = lax.ppermute(kv_own, "c", swap)
-    parts = run_attend(q, q_other, kv_own, kv_other)
+    state = run_attend(False, q, q_other, kv_own)
+    parts = run_attend(True, q, q_other, kv_other, *state)
     mixed = run_join(lax.all_to_all(parts, PAIR, 0, 0))
     latent_mixed = lax.ppermute(mixed, TURN, [(target, source) for source, target in turn])
     return (patch_latent, latent_mixed)

time: 130 us -> 129 us (level)
  the two profiles are of different devices: /device:TPU:8 before, /device:TPU:70 now
where the time goes in v8:
time: 129 us
  starting transfers between devices  62.6 us (49%)
  waiting for transfers between devices  35.3 us (27%)
  Pallas kernels  19.2 us (15%)
  blocking collectives  8.24 us (6%)
  local copies, waits for them, and re-layouts  2.64 us (2%)
    pallas_call x6, Pallas kernels, call(): pl.pallas_call(body, out_shape=[jax.ShapeDtypeStruct(shape, dtype) for sh...  19.2 us
    ppermute x1, starting transfers between devices, on_device(): message = lax.ppermute(message, TURN, turn)  15.5 us
    ppermute x1, starting transfers between devices, on_device(): lax.ppermute(mixed, TURN, [(target, source) for source, target in turn])  13 us
    all_to_all x1, starting transfers between devices, on_device(): msg_own = lax.all_to_all(message, PLANES, 0, 0, tiled=True)  12.4 us
    all_to_all x1, waiting for transfers between devices, on_device(): msg_own = lax.all_to_all(message, PLANES, 0, 0, tiled=True)  10.9 us
    all_to_all x1, blocking collectives, on_device(): mixed = run_join(lax.all_to_all(parts, PAIR, 0, 0))  8.24 us
    ppermute x1, waiting for transfers between devices, on_device(): q_other = lax.ppermute(q, 'yl', swap)  7.98 us
    all_to_all x1, starting transfers between devices, on_device(): tab_own = lax.all_to_all(tables, TP, 0, 0)  7.53 us
  transfers between devices with their start and end apart: 9, of which 7 were waited for; matrix products, arithmetic and copies ran while one was open for 0% of the time, Pallas kernels for 5%

profile of v8, /device:TPU:70, one launch (start us, length us, event | category | flops | bytes accessed | tf_op | source)
XLA Modules:
  0.0 128.7 jit_solution(2466704979770324509)
XLA Ops:
  0.6 3.2 %shard_map.113 = (bf16[8,128,768]{2,1,0:T(8,128)(2,1)}, bf16[2,112,128]{2,1,0:T(8,128)(2,1)}) custom-call(s32[4,128]{1,0:T(4,128)} %bitcast.5, s32[1,128]{1,0:T(1,128)} %bitcast.6, bf16[256,1024]{1,0:T(8,128)(2,1)} %table_ref.1, bf16[1024,256]{1,0:T(8,128)(2,1)} %wq.1, bf16[1024,256]{1,0:T(8,128)(2,1)} %wk.1, bf16[1024,256]{1,0:T(8,128)(2,1)} %wv.1, ...), custom_call_target="tpu_custom_call" | custom-call | flops 268435456 | bytes 4194304 | tf_op jit(solution)/shard_map/pallas_call | solution.py:295
  3.8 7.5 %all-to-all-start = ((bf16[8,128,768]{2,1,0:T(8,128)(2,1)}), bf16[8,128,768]{2,1,0:T(8,128)(2,1)S(1)}, u32[]{:S(2)}, u32[]{:S(2)}) async-start(bf16[8,128,768]{2,1,0:T(8,128)(2,1)} %get-tuple-element.12), calls=%async_computation | async-start | bytes 3145728 | tf_op jit(solution)/shard_map/all_to_all | solution.py:366
  11.3 15.5 %collective-permute-start.1 = (bf16[2,112,128]{2,1,0:T(8,128)(2,1)S(1)}, bf16[2,112,128]{2,1,0:T(8,128)(2,1)S(1)}, u32[]{:S(2)}, u32[]{:S(2)}) collective-permute-start(bf16[2,112,128]{2,1,0:T(8,128)(2,1)S(1)} %copy-done.2), channel_id=1, source_target_pairs={{0,128},{1,192},{2,0},{3,64},{4,384},{5,448},{6,256},{7,320},{16,1... | collective-permute-start | bytes 172040 | tf_op jit(solution)/shard_map/ppermute | solution.py:365
  26.9 3.9 %collective-permute-done.1 = bf16[2,112,128]{2,1,0:T(8,128)(2,1)S(1)} collective-permute-done((bf16[2,112,128]{2,1,0:T(8,128)(2,1)S(1)}, bf16[2,112,128]{2,1,0:T(8,128)(2,1)S(1)}, u32[]{:S(2)}, u32[]{:S(2)}) %collective-permute-start.1) | collective-permute-done | bytes 57376 | tf_op jit(solution)/shard_map/ppermute | solution.py:365
  30.8 1.9 %all-to-all-done.refs_0_ = bf16[8,128,768]{2,1,0:T(8,128)(2,1)S(1)} async-done(((bf16[8,128,768]{2,1,0:T(8,128)(2,1)}), bf16[8,128,768]{2,1,0:T(8,128)(2,1)S(1)}, u32[]{:S(2)}, u32[]{:S(2)}) %all-to-all-start) | async-done | bytes 1572896 | tf_op jit(solution)/shard_map/all_to_all | solution.py:366
  32.7 1.0 broadcast_in_dim.2
  33.8 12.4 %all-to-all-start.1 = ((bf16[32,112,128]{2,1,0:T(8,128)(2,1)}), bf16[32,112,128]{2,1,0:T(8,128)(2,1)S(1)}, u32[]{:S(2)}, u32[]{:S(2)}) async-start(bf16[32,112,128]{2,1,0:T(8,128)(2,1)} %bitcast.2), calls=%async_computation.1 | async-start | bytes 1835008 | tf_op jit(solution)/shard_map/all_to_all | solution.py:369
  46.1 1.9 %collective-permute-start = (bf16[8,128,768]{2,1,0:T(8,128)(2,1)S(1)}, bf16[8,128,768]{2,1,0:T(8,128)(2,1)}, u32[]{:S(2)}, u32[]{:S(2)}) collective-permute-start(bf16[8,128,768]{2,1,0:T(8,128)(2,1)S(1)} %all-to-all-done.refs_0_), channel_id=1, source_target_pairs={{0,8},{8,0},{1,9},{9,1},{2,10},{10,2},{3,11},{11,3},{4,12},{12,4},... | collective-permute-start | bytes 4718600 | tf_op jit(solution)/shard_map/ppermute | solution.py:367
  48.1 10.9 %all-to-all-done.1.refs_2_ = bf16[32,112,128]{2,1,0:T(8,128)(2,1)S(1)} async-done(((bf16[32,112,128]{2,1,0:T(8,128)(2,1)}), bf16[32,112,128]{2,1,0:T(8,128)(2,1)S(1)}, u32[]{:S(2)}, u32[]{:S(2)}) %all-to-all-start.1) | async-done | bytes 917536 | tf_op jit(solution)/shard_map/all_to_all | solution.py:369
  59.0 1.9 %collective-permute-start.2 = (bf16[32,112,128]{2,1,0:T(8,128)(2,1)S(1)}, bf16[32,112,128]{2,1,0:T(8,128)(2,1)S(1)}, u32[]{:S(2)}, u32[]{:S(2)}) collective-permute-start(bf16[32,112,128]{2,1,0:T(8,128)(2,1)S(1)} %all-to-all-done.1.refs_2_), channel_id=1, source_target_pairs={{0,8},{8,0},{1,9},{9,1},{2,10},{10,2},{3,11},{11,3},{4,12},{12,4},... | collective-permute-start | bytes 2752520 | tf_op jit(solution)/shard_map/ppermute | solution.py:370
  60.9 2.4 %collective-permute-done.2.refs_3_ = bf16[32,112,128]{2,1,0:T(8,128)(2,1)S(1)} collective-permute-done((bf16[32,112,128]{2,1,0:T(8,128)(2,1)S(1)}, bf16[32,112,128]{2,1,0:T(8,128)(2,1)S(1)}, u32[]{:S(2)}, u32[]{:S(2)}) %collective-permute-start.2) | collective-permute-done | bytes 917536 | tf_op jit(solution)/shard_map/ppermute | solution.py:370
  63.3 7.3 %shard_map.114 = (bf16[256,128]{1,0:T(8,128)(2,1)S(1)}, bf16[8,256,256]{2,1,0:T(8,128)(2,1)S(1)}) custom-call(bf16[8,128,768]{2,1,0:T(8,128)(2,1)S(1)} %all-to-all-done.refs_0_, bf16[8,128,768]{2,1,0:T(8,128)(2,1)} %collective-permute-done.refs_1_, bf16[32,112,128]{2,1,0:T(8,128)(2,1)S(1)} %all-to-all-done.1.refs_2_, ...), custom_call_target="tpu_custom_call" | custom-call | flops 1073741824 | bytes 4194304 | tf_op jit(solution)/shard_map/pallas_call | solution.py:295
  70.7 1.0 copy-done
  71.6 5.3 %all-to-all-start.2 = ((bf16[8,256,256]{2,1,0:T(8,128)(2,1)}), bf16[8,256,256]{2,1,0:T(8,128)(2,1)}, u32[]{:S(2)}, u32[]{:S(2)}) async-start(bf16[8,256,256]{2,1,0:T(8,128)(2,1)} %copy-done), calls=%async_computation.2 | async-start | bytes 2097152 | tf_op jit(solution)/shard_map/all_to_all | solution.py:374
  76.9 3.1 %collective-permute-start.3 = (bf16[256,128]{1,0:T(8,128)(2,1)S(1)}, bf16[256,128]{1,0:T(8,128)(2,1)S(1)}, u32[]{:S(2)}, u32[]{:S(2)}) collective-permute-start(bf16[256,128]{1,0:T(8,128)(2,1)S(1)} %get-tuple-element.15.refs_0_), channel_id=1, source_target_pairs={{0,16},{16,0},{1,17},{17,1},{2,18},{18,2},{3,19},{19,3},{4,20},{20... | collective-permute-start | bytes 196616 | tf_op jit(solution)/shard_map/ppermute | solution.py:373
  80.0 3.4 %shard_map.115 = bf16[128,256]{1,0:T(8,128)(2,1)} custom-call(bf16[8,128,768]{2,1,0:T(8,128)(2,1)S(1)} %all-to-all-done.refs_0_, bf16[8,128,768]{2,1,0:T(8,128)(2,1)} %collective-permute-done.refs_1_, bf16[32,112,128]{2,1,0:T(8,128)(2,1)S(1)} %all-to-all-done.1.refs_2_, bf16[32,112,128]{2,1,0:T(8,128)(2,1)S(1)} %collective-permute-done.2.refs_3_), custom_call_target="tpu_custom_call" | custom-call | flops 67108864 | bytes 4194304 | tf_op jit(solution)/shard_map/pallas_call | solution.py:295
  83.4 8.0 %collective-permute-done.3.refs_1_ = bf16[256,128]{1,0:T(8,128)(2,1)S(1)} collective-permute-done((bf16[256,128]{1,0:T(8,128)(2,1)S(1)}, bf16[256,128]{1,0:T(8,128)(2,1)S(1)}, u32[]{:S(2)}, u32[]{:S(2)}) %collective-permute-start.3) | collective-permute-done | bytes 65568 | tf_op jit(solution)/shard_map/ppermute | solution.py:373
  91.4 1.5 %all-to-all-done.2.refs_2_ = bf16[8,256,256]{2,1,0:T(8,128)(2,1)} async-done(((bf16[8,256,256]{2,1,0:T(8,128)(2,1)}), bf16[8,256,256]{2,1,0:T(8,128)(2,1)}, u32[]{:S(2)}, u32[]{:S(2)}) %all-to-all-start.2) | async-done | bytes 1048608 | tf_op jit(solution)/shard_map/all_to_all | solution.py:374
  92.9 1.9 %collective-permute-start.4 = (bf16[8,256,256]{2,1,0:T(8,128)(2,1)}, bf16[8,256,256]{2,1,0:T(8,128)(2,1)S(1)}, u32[]{:S(2)}, u32[]{:S(2)}) collective-permute-start(bf16[8,256,256]{2,1,0:T(8,128)(2,1)} %all-to-all-done.2.refs_2_), channel_id=1, source_target_pairs={{0,8},{8,0},{1,9},{9,1},{2,10},{10,2},{3,11},{11,3},{4,12},{12,4},... | collective-permute-start | bytes 3145736 | tf_op jit(solution)/shard_map/ppermute | solution.py:377
  94.8 3.0 %shard_map.116 = (f32[2,256,128]{2,1,0:T(8,128)S(1)}, f32[2,256,128]{2,1,0:T(8,128)S(1)}, f32[2,256,128]{2,1,0:T(8,128)S(1)}) custom-call(bf16[256,128]{1,0:T(8,128)(2,1)S(1)} %get-tuple-element.15.refs_0_, bf16[256,128]{1,0:T(8,128)(2,1)S(1)} %collective-permute-done.3.refs_1_, bf16[8,256,256]{2,1,0:T(8,128)(2,1)} %all-to-all-done.2.refs_2_), custom_call_target="tpu_custom_call" | custom-call | flops 536870912 | bytes 4194304 | tf_op jit(solution)/shard_map/pallas_call | solution.py:295
  97.8 2.2 %shard_map.117 = bf16[4,144,128]{2,1,0:T(8,128)(2,1)S(1)} custom-call(bf16[256,128]{1,0:T(8,128)(2,1)S(1)} %get-tuple-element.15.refs_0_, bf16[256,128]{1,0:T(8,128)(2,1)S(1)} %collective-permute-done.3.refs_1_, bf16[8,256,256]{2,1,0:T(8,128)(2,1)S(1)} %collective-permute-done.4.refs_2_, f32[2,256,128]{2,1,0:T(8,128)S(1)} %get-tuple-element.19.refs_3_, ...), custom_call_target="tpu_custom_call" | custom-call | flops 536870912 | bytes 4194304 | tf_op jit(solution)/shard_map/pallas_call | solution.py:295
  99.9 8.2 %all_to_all.20.part_ref = bf16[4,144,128]{2,1,0:T(8,128)(2,1)S(1)} all-to-all(bf16[4,144,128]{2,1,0:T(8,128)(2,1)S(1)} %shard_map.117), channel_id=1, replica_groups=mesh['zh'=8,'zl'=2,'yl'=2,'c'=2,'x'=4,'yh'=2] {'zl','yl'}, dimensions={0} | all-to-all | bytes 294912 | tf_op jit(solution)/shard_map/all_to_all | solution.py:380
  108.4 13.0 %collective-permute-start.5 = (bf16[128,256]{1,0:T(8,128)(2,1)S(1)}, bf16[128,256]{1,0:T(8,128)(2,1)S(1)}, u32[]{:S(2)}, u32[]{:S(2)}) collective-permute-start(bf16[128,256]{1,0:T(8,128)(2,1)S(1)} %shard_map.118), channel_id=1, source_target_pairs={{128,0},{192,1},{0,2},{64,3},{384,4},{448,5},{256,6},{320,7},{151,... | collective-permute-start | bytes 196616 | tf_op jit(solution)/shard_map/ppermute | solution.py:381
  121.4 6.7 %collective-permute-done.5 = bf16[128,256]{1,0:T(8,128)(2,1)S(1)} collective-permute-done((bf16[128,256]{1,0:T(8,128)(2,1)S(1)}, bf16[128,256]{1,0:T(8,128)(2,1)S(1)}, u32[]{:S(2)}, u32[]{:S(2)}) %collective-permute-start.5) | collective-permute-done | bytes 65568 | tf_op jit(solution)/shard_map/ppermute | solution.py:381
  (9 shorter events, 0.8 us)
Async XLA Ops:
  3.8 7.5 %copy-start.2 = (bf16[2,112,128]{2,1,0:T(8,128)(2,1)S(1)}, bf16[2,112,128]{2,1,0:T(8,128)(2,1)}, u32[]{:S(2)}) copy-start(bf16[2,112,128]{2,1,0:T(8,128)(2,1)} %get-tuple-element.13) | copy-start | bytes 172036
  3.8 28.9 %all-to-all-start = ((bf16[8,128,768]{2,1,0:T(8,128)(2,1)}), bf16[8,128,768]{2,1,0:T(8,128)(2,1)S(1)}, u32[]{:S(2)}, u32[]{:S(2)}) async-start(bf16[8,128,768]{2,1,0:T(8,128)(2,1)} %get-tuple-element.12), calls=%async_computation | async-start | bytes 3145728 | tf_op jit(solution)/shard_map/all_to_all | solution.py:366
  11.3 52.0 %copy-start.1 = (f32[2048]{0:T(1024)S(1)}, f32[2048]{0:T(1024)}, u32[]{:S(2)}) copy-start(f32[2048]{0:T(1024)} %param.16) | copy-start | bytes 24580
  11.3 19.4 %collective-permute-start.1 = (bf16[2,112,128]{2,1,0:T(8,128)(2,1)S(1)}, bf16[2,112,128]{2,1,0:T(8,128)(2,1)S(1)}, u32[]{:S(2)}, u32[]{:S(2)}) collective-permute-start(bf16[2,112,128]{2,1,0:T(8,128)(2,1)S(1)} %copy-done.2), channel_id=1, source_target_pairs={{0,128},{1,192},{2,0},{3,64},{4,384},{5,448},{6,256},{7,320},{16,1... | collective-permute-start | bytes 172040 | tf_op jit(solution)/shard_map/ppermute | solution.py:365
  33.8 25.2 %all-to-all-start.1 = ((bf16[32,112,128]{2,1,0:T(8,128)(2,1)}), bf16[32,112,128]{2,1,0:T(8,128)(2,1)S(1)}, u32[]{:S(2)}, u32[]{:S(2)}) async-start(bf16[32,112,128]{2,1,0:T(8,128)(2,1)} %bitcast.2), calls=%async_computation.1 | async-start | bytes 1835008 | tf_op jit(solution)/shard_map/all_to_all | solution.py:369
  46.1 14.7 %collective-permute-start = (bf16[8,128,768]{2,1,0:T(8,128)(2,1)S(1)}, bf16[8,128,768]{2,1,0:T(8,128)(2,1)}, u32[]{:S(2)}, u32[]{:S(2)}) collective-permute-start(bf16[8,128,768]{2,1,0:T(8,128)(2,1)S(1)} %all-to-all-done.refs_0_), channel_id=1, source_target_pairs={{0,8},{8,0},{1,9},{9,1},{2,10},{10,2},{3,11},{11,3},{4,12},{12,4},... | collective-permute-start | bytes 4718600 | tf_op jit(solution)/shard_map/ppermute | solution.py:367
  59.0 4.4 %collective-permute-start.2 = (bf16[32,112,128]{2,1,0:T(8,128)(2,1)S(1)}, bf16[32,112,128]{2,1,0:T(8,128)(2,1)S(1)}, u32[]{:S(2)}, u32[]{:S(2)}) collective-permute-start(bf16[32,112,128]{2,1,0:T(8,128)(2,1)S(1)} %all-to-all-done.1.refs_2_), channel_id=1, source_target_pairs={{0,8},{8,0},{1,9},{9,1},{2,10},{10,2},{3,11},{11,3},{4,12},{12,4},... | collective-permute-start | bytes 2752520 | tf_op jit(solution)/shard_map/ppermute | solution.py:370
  70.7 1.0 copy-start
  71.6 21.2 %all-to-all-start.2 = ((bf16[8,256,256]{2,1,0:T(8,128)(2,1)}), bf16[8,256,256]{2,1,0:T(8,128)(2,1)}, u32[]{:S(2)}, u32[]{:S(2)}) async-start(bf16[8,256,256]{2,1,0:T(8,128)(2,1)} %copy-done), calls=%async_computation.2 | async-start | bytes 2097152 | tf_op jit(solution)/shard_map/all_to_all | solution.py:374
  76.9 14.5 %collective-permute-start.3 = (bf16[256,128]{1,0:T(8,128)(2,1)S(1)}, bf16[256,128]{1,0:T(8,128)(2,1)S(1)}, u32[]{:S(2)}, u32[]{:S(2)}) collective-permute-start(bf16[256,128]{1,0:T(8,128)(2,1)S(1)} %get-tuple-element.15.refs_0_), channel_id=1, source_target_pairs={{0,16},{16,0},{1,17},{17,1},{2,18},{18,2},{3,19},{19,3},{4,20},{20... | collective-permute-start | bytes 196616 | tf_op jit(solution)/shard_map/ppermute | solution.py:373
  92.9 4.9 %collective-permute-start.4 = (bf16[8,256,256]{2,1,0:T(8,128)(2,1)}, bf16[8,256,256]{2,1,0:T(8,128)(2,1)S(1)}, u32[]{:S(2)}, u32[]{:S(2)}) collective-permute-start(bf16[8,256,256]{2,1,0:T(8,128)(2,1)} %all-to-all-done.2.refs_2_), channel_id=1, source_target_pairs={{0,8},{8,0},{1,9},{9,1},{2,10},{10,2},{3,11},{11,3},{4,12},{12,4},... | collective-permute-start | bytes 3145736 | tf_op jit(solution)/shard_map/ppermute | solution.py:377
  108.4 19.7 %collective-permute-start.5 = (bf16[128,256]{1,0:T(8,128)(2,1)S(1)}, bf16[128,256]{1,0:T(8,128)(2,1)S(1)}, u32[]{:S(2)}, u32[]{:S(2)}) collective-permute-start(bf16[128,256]{1,0:T(8,128)(2,1)S(1)} %shard_map.118), channel_id=1, source_target_pairs={{128,0},{192,1},{0,2},{64,3},{384,4},{448,5},{256,6},{320,7},{151,... | collective-permute-start | bytes 196616 | tf_op jit(solution)/shard_map/ppermute | solution.py:381
